TPU v7x, 128 devices: a whole 4x4x4 slice. The times are simulated.
128 devices in a mesh: fsdp: 8 (over y, core), mat: 16 (over z, x).
Axes of the slice: x: 4, y: 4, z: 4, core: 2. Of those that a mesh axis runs over, the one named last changes fastest.
Arguments:
- momentum: float32 [8, 2048, 7168], P(None, 'mat', 'fsdp'), may hold values from -24 to 24
- gradient: bfloat16 [8, 2048, 7168], P(None, 'mat', 'fsdp')
Outputs:
- new_momentum: float32 [8, 2048, 7168], P(None, 'mat', 'fsdp')
- update: bfloat16 [8, 2048, 7168], P(None, 'mat', 'fsdp')
All inputs are finite; a program needn't handle non-finite values.
Results may differ from a plain program's by a relative error of at most 0.015.
Values may be sent and summed in bfloat16 or wider, within the bound.
No kernel may reach another device: no remote copies, remote signals or barrier semaphores. Data moves between devices by JAX's collectives and lax.ppermute only.
A program may use at most 128 MiB of HBM per device.

v0:
```python
import math

import jax
import jax.numpy as jnp
from jax import lax
from jax.sharding import PartitionSpec as P

COLS = 7168
POWER = 3


momentum_rate = 0.95
first_coef = 3.4445
second_coef = -4.775
third_coef = 2.0315
epsilon_value = 1e-06
highest = lax.Precision.HIGHEST


def regroup_in(values):
    segmented = lax.all_to_all(values, "fsdp", split_axis=0, concat_axis=2, tiled=True)
    return lax.all_to_all(segmented, "mat", split_axis=2, concat_axis=1, tiled=True)


def regroup_out(values):
    segmented = lax.all_to_all(values, "mat", split_axis=1, concat_axis=2, tiled=True)
    return lax.all_to_all(segmented, "fsdp", split_axis=2, concat_axis=0, tiled=True)


def gram_rows_full(columns_block):
    return lax.psum_scatter(
        lax.dot_general(
            columns_block,
            columns_block,
            (((1,), (1,)), ((), ())),
            preferred_element_type=jnp.float32,
        ),
        "mat",
        scatter_dimension=0,
        tiled=True,
    )


def orthogonal_step(columns_block):
    vector = jnp.ones((columns_block.shape[0],), jnp.float32)
    raw_rows = gram_rows_full(columns_block)
    for step_index in range(POWER):
        row_piece = jnp.dot(raw_rows, vector, precision=highest, preferred_element_type=jnp.float32)
        gram_image = lax.all_gather(row_piece, "mat", axis=0, tiled=True)
        length = jnp.sqrt(jnp.sum(gram_image * gram_image) + epsilon_value)
        vector = gram_image / length
    scaling = lax.rsqrt(length + epsilon_value)
    started = (columns_block.astype(jnp.float32) * scaling).astype(jnp.bfloat16)
    gram_low = (raw_rows * (scaling * scaling)).astype(jnp.bfloat16)
    squared = jnp.dot(
        gram_low,
        lax.all_gather(gram_low, "mat", axis=0, tiled=True),
        preferred_element_type=jnp.float32,
    )
    poly_low = (second_coef * gram_low.astype(jnp.float32) + third_coef * squared).astype(
        jnp.bfloat16
    )
    product = jnp.dot(
        lax.all_gather(poly_low, "mat", axis=0, tiled=True),
        started,
        preferred_element_type=jnp.float32,
    )
    iterate = first_coef * started.astype(jnp.float32) + product
    return (math.sqrt(COLS) * iterate).astype(jnp.bfloat16)


def shards(momentum, gradient):
    gradient_full = gradient.astype(jnp.float32)
    new_momentum = momentum_rate * momentum + gradient_full
    blended = (gradient_full + momentum_rate * new_momentum).astype(jnp.bfloat16)
    regrouped = regroup_in(blended)
    results = [orthogonal_step(regrouped[0])]
    update = regroup_out(jnp.stack(results))
    return (new_momentum, update)


def solution(mesh):
    in_specs = (P(None, "mat", "fsdp"), P(None, "mat", "fsdp"))
    out_specs = (P(None, "mat", "fsdp"), P(None, "mat", "fsdp"))
    return jax.shard_map(shards, mesh=mesh, in_specs=in_specs, out_specs=out_specs, check_vma=False)
```

profile of v0, /device:TPU:1, one launch (start us, length us, event | category | flops | bytes accessed | tf_op | source)
XLA Modules:
  0.0 710.8 jit_solution(1335500377268689678)
XLA Ops:
  7.2 0.0 reduce-scatter.2.cloned.1.call-start
  7.2 3.2 copy.19
  10.4 5.0 copy.18
  15.4 4.6 fusion
  20.0 29.4 %all_to_all.69 = bf16[8,128,896]{1,2,0:T(8,128)(2,1)S(1)} all-to-all(bf16[8,128,896]{1,2,0:T(8,128)(2,1)S(1)} %get-tuple-element.8), channel_id=1, replica_groups=mesh['fsdp'=8,'mat'=16] {'fsdp'}, dimensions={0} | all-to-all | bytes 3670016 | tf_op jit(solution)/shard_map/all_to_all | solution.py:21
  49.3 29.2 %copy.44 = bf16[1,128,7168]{1,0,2:T(2,128)(2,1)} copy(bf16[1,128,7168]{1,2,0:T(8,128)(2,1)S(1)} %bitcast.75) | data formatting | bytes 3670016 | tf_op jit(solution)/shard_map/all_to_all | solution.py:21
  78.5 0.6 broadcast.24
  79.1 41.0 %reduce.3 = bf16[7168,128]{1,0:T(8,128)(2,1)} reduce(bf16[7168,1,128]{2,1,0:T(2,128)(2,1)} %bitcast.69, bf16[]{:T(256)} %broadcast.24), dimensions={1}, to_apply=%bitcast.66.reduce_sub_computation | reduce | bytes 3670018
  120.0 3.9 reshape.25
  123.9 31.8 %all_to_all.70 = bf16[16,2,28672]{2,1,0:T(2,128)(2,1)} all-to-all(bf16[16,2,28672]{2,1,0:T(2,128)(2,1)S(1)} %reshape.25), channel_id=1, replica_groups=mesh['fsdp'=8,'mat'=16] {'mat'}, dimensions={0} | all-to-all | bytes 3670016 | tf_op jit(solution)/shard_map/all_to_all | solution.py:22
  155.7 10.2 %reshape.26 = bf16[7168,1,128]{2,1,0:T(2,128)(2,1)} reshape(bf16[16,2,28672]{2,1,0:T(2,128)(2,1)} %all_to_all.70) | data formatting | bytes 3670016
  165.9 2.3 copy.29
  168.2 1.2 copy.21
  169.4 8.4 %fusion.4 = f32[2048,2048]{1,0:T(8,128)} fusion(bf16[56,8,16,128]{3,2,1,0:T(8,128)(2,1)S(1)} %bitcast.79), kind=kOutput, calls=%fused_computation.9 | convolution fusion | flops 3758096384 | bytes 18612224 | tf_op jit(solution)/shard_map/dot_general | solution.py:32
  177.8 0.0 reduce-scatter.2.cloned.1.call-update
  177.8 0.0 all-gather.6.cloned.1.call-start
  177.9 107.8 %reduce-scatter.2.cloned.1.call-done = f32[128,2048]{1,0:T(8,128)} async-done(((f32[2048,2048]{1,0:T(8,128)}), f32[128,2048]{1,0:T(8,128)}) %reduce-scatter.2.cloned.1.call-update) | async-done | bytes 1048592 | tf_op jit(solution)/shard_map/reduce_scatter | solution.py:31
  285.7 0.0 copy-start
  285.7 2.2 convolution_bitcast_fusion.2
  287.9 15.8 %all-gather = f32[16,1,128]{2,1,0:T(1,128)S(1)} all-gather(f32[1,1,128]{2,1,0:T(1,128)S(1)} %convolution_bitcast_fusion.2), channel_id=1, replica_groups=mesh['fsdp'=8,'mat'=16] {'mat'}, dimensions={0}, use_global_device_ids=true | all-gather | bytes 8704 | tf_op jit(solution)/shard_map/all_gather | solution.py:49
  303.7 0.6 multiply_reduce_fusion.2
  305.0 2.1 convolution_bitcast_fusion.1
  307.2 14.3 %all-gather.1 = f32[16,1,128]{2,1,0:T(1,128)S(1)} all-gather(f32[1,1,128]{2,1,0:T(1,128)S(1)} %convolution_bitcast_fusion.1), channel_id=1, replica_groups=mesh['fsdp'=8,'mat'=16] {'mat'}, dimensions={0}, use_global_device_ids=true | all-gather | bytes 8704 | tf_op jit(solution)/shard_map/all_gather | solution.py:49
  321.5 0.6 multiply_reduce_fusion.1
  322.8 2.1 convolution_bitcast_fusion
  324.9 14.5 %all-gather.2 = f32[16,1,128]{2,1,0:T(1,128)S(1)} all-gather(f32[1,1,128]{2,1,0:T(1,128)S(1)} %convolution_bitcast_fusion), channel_id=1, replica_groups=mesh['fsdp'=8,'mat'=16] {'mat'}, dimensions={0}, use_global_device_ids=true | all-gather | bytes 8704 | tf_op jit(solution)/shard_map/all_gather | solution.py:49
  339.4 0.6 multiply_reduce_fusion
  340.8 0.0 copy-done
  340.8 0.9 multiply_convert_fusion.3
  341.7 0.0 all-gather.6.cloned.1.call-update
  341.7 0.0 all-gather.8.cloned.1.call-start
  341.7 83.7 %all-gather.6.cloned.1.call-done = bf16[2048,2048]{1,0:T(8,128)(2,1)} async-done(((bf16[128,2048]{1,0:T(8,128)(2,1)}), bf16[2048,2048]{1,0:T(8,128)(2,1)}) %all-gather.6.cloned.1.call-update) | async-done | bytes 8388624 | tf_op jit(solution)/shard_map/all_gather | solution.py:57
  425.5 5.7 fusion.3
  431.2 0.0 all-gather.8.cloned.1.call-update
  431.2 70.6 %all-gather.8.cloned.1.call-done = bf16[2048,2048]{1,0:T(8,128)(2,1)} async-done(((bf16[128,2048]{1,0:T(8,128)(2,1)}), bf16[2048,2048]{1,0:T(8,128)(2,1)}) %all-gather.8.cloned.1.call-update) | async-done | bytes 8388624 | tf_op jit(solution)/shard_map/all_gather | solution.py:64
  501.8 9.9 %fusion.1 = bf16[1,2048,448]{1,2,0:T(8,128)(2,1)} fusion(bf16[2048,2048]{1,0:T(8,128)(2,1)} %all-gather.8.cloned.1.call-done, f32[]{:T(128)S(6)} %rsqrt.3, bf16[56,8,16,128]{3,2,1,0:T(8,128)(2,1)S(1)} %bitcast.80), kind=kOutput, calls=%fused_computation.5 | convolution fusion | flops 3768188928 | bytes 12058628 | tf_op jit(solution)/shard_map/dot_general | solution.py:63
  511.7 10.7 %copy.22 = bf16[1,2048,448]{2,0,1:T(2,128)(2,1)} copy(bf16[1,2048,448]{1,2,0:T(8,128)(2,1)} %fusion.1) | data formatting | bytes 3670016 | tf_op jit(solution)/shard_map/stack | solution.py:78
  522.4 14.1 %reduce.4 = bf16[2048,448]{1,0:T(8,128)(2,1)S(1)} reduce(bf16[2048,1,448]{2,1,0:T(2,128)(2,1)} %bitcast.67, bf16[]{:T(256)} %broadcast.24), dimensions={1}, to_apply=%bitcast.53.reduce_sub_computation | reduce | bytes 3670018
  536.5 3.3 reshape.27
  539.8 38.6 %all_to_all.71 = bf16[16,2,28672]{2,1,0:T(2,128)(2,1)S(1)} all-to-all(bf16[16,2,28672]{2,1,0:T(2,128)(2,1)} %reshape.27), channel_id=1, replica_groups=mesh['fsdp'=8,'mat'=16] {'mat'}, dimensions={0} | all-to-all | bytes 3670016 | tf_op jit(solution)/shard_map/all_to_all | solution.py:26
  578.4 7.2 %reshape.28 = bf16[2048,1,448]{2,1,0:T(2,128)(2,1)} reshape(bf16[16,2,28672]{2,1,0:T(2,128)(2,1)S(1)} %all_to_all.71) | data formatting | bytes 3670016
  585.6 2.8 copy.30
  588.4 3.0 copy.28
  591.4 2.0 copy.24
  593.3 29.2 %copy.43 = bf16[1,128,7168]{1,0,2:T(2,128)(2,1)} copy(bf16[1,128,7168]{1,2,0:T(8,128)(2,1)S(1)} %bitcast.77) | data formatting | bytes 3670016 | tf_op jit(solution)/shard_map/all_to_all | solution.py:26
  622.6 39.7 %reduce.5 = bf16[7168,128]{1,0:T(8,128)(2,1)S(1)} reduce(bf16[7168,1,128]{2,1,0:T(2,128)(2,1)} %bitcast.70, bf16[]{:T(256)} %broadcast.24), dimensions={1}, to_apply=%bitcast.65.reduce_sub_computation | reduce | bytes 3670018
  662.3 3.1 reshape.29
  665.4 6.1 all-to-all-start.3
  671.5 5.0 copy.26
  676.4 18.5 %all-to-all-done.3 = bf16[8,2,57344]{2,1,0:T(2,128)(2,1)S(1)} async-done(((bf16[8,2,57344]{2,1,0:T(2,128)(2,1)}), bf16[8,2,57344]{2,1,0:T(2,128)(2,1)S(1)}, u32[]{:S(2)}, u32[]{:S(2)}) %all-to-all-start.3) | async-done | bytes 1835040 | tf_op jit(solution)/shard_map/all_to_all | solution.py:27
  695.0 4.1 reshape.30
  699.1 2.3 copy.31
  701.4 2.6 copy.27
Async XLA Ops:
  7.2 278.5 %reduce-scatter.2.cloned.1.call-start = ((), (), s32[]{:S(2)}) async-start(), calls=%async_computation.5 | async-start | bytes 17825792 | tf_op jit(solution)/shard_map/reduce_scatter | solution.py:31
  177.8 247.6 %all-gather.6.cloned.1.call-start = ((), (), s32[]{:S(2)}) async-start(), calls=%async_computation.6 | async-start | bytes 8912896 | tf_op jit(solution)/shard_map/all_gather | solution.py:57
  285.7 55.1 %copy-start = (f32[128,2048]{1,0:T(8,128)S(1)}, f32[128,2048]{1,0:T(8,128)}, u32[]{:S(2)}) copy-start(f32[128,2048]{1,0:T(8,128)} %reduce-scatter.2.cloned.1.call-done) | copy-start | bytes 3145732
  341.7 160.1 %all-gather.8.cloned.1.call-start = ((), (), s32[]{:S(2)}) async-start(), calls=%async_computation.7 | async-start | bytes 8912896 | tf_op jit(solution)/shard_map/all_gather | solution.py:64
  665.4 29.6 %all-to-all-start.3 = ((bf16[8,2,57344]{2,1,0:T(2,128)(2,1)}), bf16[8,2,57344]{2,1,0:T(2,128)(2,1)S(1)}, u32[]{:S(2)}, u32[]{:S(2)}) async-start(bf16[8,2,57344]{2,1,0:T(2,128)(2,1)} %reshape.29), calls=%async_computation.4 | async-start | bytes 3670016 | tf_op jit(solution)/shard_map/all_to_all | solution.py:27
Sparse Core Ops, SparseCore 0:
  177.9 107.7 reduce-scatter.1
  341.8 83.5 all-gather.5
  431.3 70.4 all-gather.7
where the time goes:
time: 721 us; the launch traced here: 711 us
  waiting for transfers between devices  281 us (39%)
  blocking collectives  144 us (20%)
  local copies, waits for them, and re-layouts  131 us (18%)
  other arithmetic  102 us (14%)
  matrix products  30.5 us (4%)
  between operations  16.1 us (2%)
    reduce_scatter x1, waiting for transfers between devices, gram_rows_full(): lax.psum_scatter(lax.dot_general(columns_block, columns_block, (((1,), (1...  108 us
    unnamed x3, other arithmetic  94.8 us
    all_gather x1, waiting for transfers between devices, orthogonal_step(): lax.all_gather(gram_low, 'mat', axis=0, tiled=True)  83.7 us
    all_gather x1, waiting for transfers between devices, orthogonal_step(): lax.all_gather(poly_low, 'mat', axis=0, tiled=True)  70.6 us
    unnamed x16, local copies, waits for them, and re-layouts  55.5 us
    all_gather x3, blocking collectives, orthogonal_step(): gram_image = lax.all_gather(row_piece, 'mat', axis=0, tiled=True)  44.6 us
    all_to_all x1, blocking collectives, regroup_out(): lax.all_to_all(values, 'mat', split_axis=1, concat_axis=2, tiled=True)  38.6 us
    all_to_all x3, local copies, waits for them, and re-layouts, regroup_out(): lax.all_to_all(values, 'mat', split_axis=1, concat_axis=2, tiled=True)  34.2 us
  transfers between devices with their start and end apart: 4, of which 4 were waited for; matrix products, arithmetic and copies ran while one was open for 1% of the time, Pallas kernels for 0%

commit v1 on v0

v1 whole, which is shorter than its diff:
```python
import math

import jax
import jax.numpy as jnp
from jax import lax
from jax.experimental import pallas as pl
from jax.experimental.pallas import tpu as pltpu
from jax.sharding import PartitionSpec as P

EXPERTS, ROWS, COLS = 8, 2048, 7168
CORES, RING, PAIR = 2, 4, 2
MEMBERS = 16
LANES = ROWS // MEMBERS
WIDE = COLS // 8
HALF = WIDE // 2
BLOCK = 256
FOLD = 9 * BLOCK
PIECE = 128

momentum_rate = 0.95
first_coef = 3.4445
second_coef = -4.775
third_coef = 2.0315
epsilon_value = 1e-06
f32, bf16 = jnp.float32, jnp.bfloat16
PARAMS = pltpu.CompilerParams(vmem_limit_bytes=50 * 1024 * 1024)
WHOLE = pl.BlockSpec(memory_space=pltpu.VMEM)
SCALARS = pl.BlockSpec(memory_space=pltpu.SMEM)


def blend_kernel(momentum_ref, gradient_ref, new_ref, blended_ref):
    gradient = gradient_ref[0].astype(f32)
    new = momentum_rate * momentum_ref[0] + gradient
    new_ref[0] = new
    blended_ref[0] = (gradient + momentum_rate * new).astype(bf16).T


def blend(momentum, gradient):
    block = pl.BlockSpec((1, LANES, WIDE), lambda e: (e, 0, 0))
    return pl.pallas_call(
        blend_kernel,
        grid=(EXPERTS,),
        in_specs=[block, block],
        out_specs=[block, pl.BlockSpec((1, WIDE, LANES), lambda e: (e, 0, 0))],
        out_shape=[
            jax.ShapeDtypeStruct((EXPERTS, LANES, WIDE), f32),
            jax.ShapeDtypeStruct((EXPERTS, WIDE, LANES), bf16),
        ],
        compiler_params=PARAMS,
    )(momentum, gradient)


def place(half, piece, block):
    folded = 2 * half + piece // 2
    upper = block < 8 - folded
    row = jnp.where(upper, folded, 7 - folded) * BLOCK + (piece % 2) * PIECE
    column = jnp.where(upper, folded + block, block - 1) * BLOCK
    return pl.multiple_of(row, PIECE), pl.multiple_of(column, BLOCK)


def gram_kernel(where_ref, columns_ref, *piece_refs):
    half = where_ref[0]
    for slot, piece_ref in enumerate(piece_refs):
        piece = where_ref[1 + slot]
        folded = 2 * half + piece // 2
        top = columns_ref[2 * folded + piece % 2].T
        low = columns_ref[2 * (7 - folded) + piece % 2].T
        for block in range(9):
            _, column = place(half, piece, block)
            member = column // LANES
            right = jnp.concatenate([columns_ref[member], columns_ref[member + 1]], axis=1)
            left = jnp.where(block < 8 - folded, top, low) if 4 < block < 8 else (top if block <= 4 else low)
            piece_ref[:, block * BLOCK : (block + 1) * BLOCK] = jnp.dot(
                left, right, preferred_element_type=f32
            ).astype(bf16)


def gram_pieces(columns, half, pieces):
    where = jnp.stack([half, *pieces]).astype(jnp.int32)
    return pl.pallas_call(
        gram_kernel,
        in_specs=[SCALARS, WHOLE],
        out_specs=[WHOLE] * len(pieces),
        out_shape=[jax.ShapeDtypeStruct((PIECE, FOLD), bf16)] * len(pieces),
        compiler_params=PARAMS,
        cost_estimate=pl.CostEstimate(flops=2 * 2 * len(pieces) * PIECE * FOLD * 512, bytes_accessed=8_000_000, transcendentals=0),
    )(where, columns)


STEP = 16


def step_kernel(where_ref, columns_ref, *refs):
    piece_refs, out_ref = refs[: CORES * RING], refs[CORES * RING]
    gram, blended, mixed, image = refs[CORES * RING + 1 :]
    for slot, piece_ref in enumerate(piece_refs):
        half, piece = where_ref[2 * slot], where_ref[2 * slot + 1]
        for block in range(9):
            row, column = place(half, piece, block)
            values = piece_ref[:, block * BLOCK : (block + 1) * BLOCK]
            gram[pl.ds(row, PIECE), pl.ds(column, BLOCK)] = values
            gram[pl.ds(column, BLOCK), pl.ds(row, PIECE)] = values.T
    for member in range(MEMBERS):
        blended[:, member * LANES : (member + 1) * LANES] = columns_ref[member]

    def rows_of(step):
        return pl.ds(pl.multiple_of(step * STEP, STEP), STEP)

    def add_rows(step, total):
        return total + gram[rows_of(step), :].astype(f32)

    steps = ROWS // STEP
    total = lax.fori_loop(0, steps, add_rows, jnp.zeros((STEP, ROWS), f32))
    first = jnp.sum(total, axis=0, keepdims=True)
    first = first / jnp.sqrt(jnp.sum(first * first) + epsilon_value)

    def dot_rows(step, squares):
        values = jnp.sum(gram[rows_of(step), :].astype(f32) * first, axis=1, keepdims=True)
        image[rows_of(step), :] = values
        return squares + values * values

    squares = lax.fori_loop(0, steps, dot_rows, jnp.zeros((STEP, 1), f32))
    length = jnp.sqrt(jnp.sum(squares) + epsilon_value)

    def weigh_rows(step, total):
        return total + gram[rows_of(step), :].astype(f32) * (image[rows_of(step), :] / length)

    total = lax.fori_loop(0, steps, weigh_rows, jnp.zeros((STEP, ROWS), f32))
    third = jnp.sum(total, axis=0, keepdims=True)
    length = jnp.sqrt(jnp.sum(third * third) + epsilon_value)
    scale = lax.rsqrt(jnp.full((1, 1), length + epsilon_value, f32))
    square = scale * scale

    for block in range(8):
        at = slice(block * BLOCK, (block + 1) * BLOCK)
        product = jnp.dot(blended[...], gram[:, at], preferred_element_type=f32)
        mixed[:, at] = (second_coef * blended[:, at].astype(f32) + (third_coef * square) * product).astype(bf16)
    for block in range(8):
        at = slice(block * BLOCK, (block + 1) * BLOCK)
        product = jnp.dot(mixed[...], gram[:, at], preferred_element_type=f32)
        update = (math.sqrt(COLS) * scale) * (first_coef * blended[:, at].astype(f32) + square * product)
        update = update.astype(bf16)
        out_ref[2 * block] = update[:, :LANES]
        out_ref[2 * block + 1] = update[:, LANES:]


def newton_step(columns, pieces, where):
    return pl.pallas_call(
        step_kernel,
        in_specs=[SCALARS, WHOLE] + [WHOLE] * len(pieces),
        out_specs=WHOLE,
        out_shape=jax.ShapeDtypeStruct((MEMBERS, HALF, LANES), bf16),
        scratch_shapes=[
            pltpu.VMEM((ROWS, ROWS), bf16),
            pltpu.VMEM((HALF, ROWS), bf16),
            pltpu.VMEM((HALF, ROWS), bf16),
            pltpu.VMEM((ROWS, 1), f32),
        ],
        compiler_params=PARAMS,
        cost_estimate=pl.CostEstimate(flops=4 * ROWS * ROWS * HALF, bytes_accessed=8_000_000, transcendentals=0),
    )(where, columns, *pieces)


def spread_kernel(update_ref, out_ref):
    out_ref[0] = update_ref[0].T


def spread(update):
    return pl.pallas_call(
        spread_kernel,
        grid=(EXPERTS,),
        in_specs=[pl.BlockSpec((1, WIDE, LANES), lambda e: (e, 0, 0))],
        out_specs=pl.BlockSpec((1, LANES, WIDE), lambda e: (e, 0, 0)),
        out_shape=jax.ShapeDtypeStruct((EXPERTS, LANES, WIDE), bf16),
        compiler_params=PARAMS,
    )(update)


def add(*terms):
    total = terms[0].astype(f32)
    for term in terms[1:]:
        total = total + term.astype(f32)
    return total.astype(bf16)


def swap_cores(values):
    return lax.ppermute(values, "fsdp", [(i, i ^ 1) for i in range(CORES * RING)])


def shift(values, distance):
    size = CORES * RING
    return lax.ppermute(values, "fsdp", [(i, (i + CORES * distance) % size) for i in range(size)])


def swap_pair(values):
    return lax.ppermute(values, "mat", [(i, i ^ 1) for i in range(MEMBERS)])


def shards(momentum, gradient):
    index = lax.axis_index("fsdp")
    core, place_y = index % CORES, index // CORES
    order = (2, 1, 3, 0)
    new_momentum, blended = blend(momentum, gradient)
    columns = lax.all_to_all(blended.reshape(MEMBERS, HALF, LANES), "mat", 0, 0)

    wanted = [(place_y + distance) % RING for distance in order]
    away = gram_pieces(columns, 1 - core, wanted)
    kept = gram_pieces(columns, core, wanted)
    summed = [add(mine, swap_cores(theirs)) for mine, theirs in zip(kept, away)]
    arrived = [shift(values, distance) for values, distance in zip(summed, order) if distance]
    part = add(summed[-1], *arrived)
    total = add(part, swap_pair(part))

    own = [total] + [shift(total, distance) for distance in (1, 2, 3)]
    other = [swap_cores(values) for values in own]
    where = []
    for half in (core, 1 - core):
        for distance in range(RING):
            where += [half, (place_y - distance) % RING]
    update = newton_step(columns, own + other, jnp.stack(where).astype(jnp.int32))
    returned = lax.all_to_all(update, "mat", 0, 0)
    return new_momentum, spread(returned.reshape(EXPERTS, WIDE, LANES))


def solution(mesh):
    spec = P(None, "mat", "fsdp")
    return jax.shard_map(shards, mesh=mesh, in_specs=(spec, spec), out_specs=(spec, spec), check_vma=False)
```

time: 721 us -> 205 us (0.28); the launches traced: 711 us -> 205 us
  waiting for transfers between devices: 281 us -> 78.9 us
  local copies, waits for them, and re-layouts: 131 us -> 1.75 us
  blocking collectives: 144 us -> 28.9 us
  other arithmetic: 102 us -> 0.96 us
  Pallas kernels: 0 us -> 56.7 us
  starting transfers between devices: 6.21 us -> 36.8 us
  matrix products: 30.5 us -> 0 us
  between operations: 16.1 us -> 0.82 us
    all_gather x2 -> x0, waiting for transfers between devices: 154 us -> none  [the longest x1 83.7 us: orthogonal_step(): lax.all_gather(gram_low, 'mat', axis=0, tiled=True)]
    reduce_scatter x1 -> x0, waiting for transfers between devices: 108 us -> none  [gram_rows_full(): lax.psum_scatter(lax.dot_general(columns_block, columns_block, (((1,), (1...]
    unnamed x3 -> x0, other arithmetic: 94.8 us -> none
    all_to_all x3 -> x1, blocking collectives: 99.8 us -> 28.9 us  [shards(): returned = lax.all_to_all(update, 'mat', 0, 0)]
    all_to_all x5 -> x0, local copies, waits for them, and re-layouts: 64.5 us -> none  [the longest x3 34.2 us: regroup_out(): lax.all_to_all(values, 'mat', split_axis=1, concat_axis=2, tiled=True)]
    pallas_call x0 -> x5, Pallas kernels: none -> 56.7 us  [the longest x1 40.5 us: newton_step(): pl.pallas_call(step_kernel, in_specs=[SCALARS, WHOLE] + [WHOLE] * len(pie...]
    unnamed x16 -> x2, local copies, waits for them, and re-layouts: 55.5 us -> 1.49 us
    ppermute x0 -> x15, waiting for transfers between devices: none -> 52.3 us  [the longest x6 36.8 us: shift(): lax.ppermute(values, 'fsdp', [(i, (i + CORES * distance) % size) for i in...]
  transfers between devices with their start and end apart: 4 -> 16, of which waited for: 4 -> 7; matrix products, arithmetic and copies ran while one was open for 1% -> 0% of each run, Pallas kernels for 0% -> 1%
where the time goes in v1:
time: 205 us
  waiting for transfers between devices  78.9 us (38%)
  Pallas kernels  56.7 us (28%)
  starting transfers between devices  36.8 us (18%)
  blocking collectives  28.9 us (14%)
    pallas_call x1, Pallas kernels, newton_step(): pl.pallas_call(step_kernel, in_specs=[SCALARS, WHOLE] + [WHOLE] * len(pie...  40.5 us
    ppermute x6, waiting for transfers between devices, shift(): lax.ppermute(values, 'fsdp', [(i, (i + CORES * distance) % size) for i in...  36.8 us
    all_to_all x1, blocking collectives, shards(): returned = lax.all_to_all(update, 'mat', 0, 0)  28.9 us
    all_to_all x1, waiting for transfers between devices, shards(): columns = lax.all_to_all(blended.reshape(MEMBERS, HALF, LANES), 'mat', 0, 0)  26.6 us
    ppermute x8, starting transfers between devices, swap_cores(): lax.ppermute(values, 'fsdp', [(i, i ^ 1) for i in range(CORES * RING)])  18.5 us
    ppermute x1, waiting for transfers between devices, swap_pair(): return lax.ppermute(values, 'mat', [(i, i ^ 1) for i in range(MEMBERS)])  14 us
    ppermute x6, starting transfers between devices, shift(): lax.ppermute(values, 'fsdp', [(i, (i + CORES * distance) % size) for i in...  9.72 us
    all_to_all x1, starting transfers between devices, shards(): columns = lax.all_to_all(blended.reshape(MEMBERS, HALF, LANES), 'mat', 0, 0)  8.47 us
  transfers between devices with their start and end apart: 16, of which 7 were waited for; matrix products, arithmetic and copies ran while one was open for 0% of the time, Pallas kernels for 1%

profile of v1, /device:TPU:1, one launch (start us, length us, event | category | flops | bytes accessed | tf_op | source)
XLA Modules:
  0.0 204.8 jit_solution(455907905935502884)
XLA Ops:
  0.6 0.0 copy-start
  0.6 1.5 copy-done
  2.1 6.8 %shard_map.41 = (f32[8,128,896]{2,1,0:T(8,128)}, bf16[8,896,128]{2,1,0:T(8,128)(2,1)}) custom-call(f32[8,128,896]{2,1,0:T(8,128)} %momentum_ref.1, bf16[8,128,896]{2,1,0:T(8,128)(2,1)S(1)} %copy-done), custom_call_target="tpu_custom_call" | custom-call | tf_op jit(solution)/shard_map/pallas_call | solution.py:40
  9.0 8.5 %all-to-all-start = ((bf16[16,448,128]{2,1,0:T(8,128)(2,1)}), bf16[16,448,128]{2,1,0:T(8,128)(2,1)}, u32[]{:S(2)}, u32[]{:S(2)}) async-start(bf16[16,448,128]{2,1,0:T(8,128)(2,1)} %bitcast.6), calls=%async_computation | async-start | bytes 3670016 | tf_op jit(solution)/shard_map/all_to_all | solution.py:204
  17.5 0.1 stack.64.where_ref
  17.6 26.6 %all-to-all-done.columns_ref = bf16[16,448,128]{2,1,0:T(8,128)(2,1)} async-done(((bf16[16,448,128]{2,1,0:T(8,128)(2,1)}), bf16[16,448,128]{2,1,0:T(8,128)(2,1)}, u32[]{:S(2)}, u32[]{:S(2)}) %all-to-all-start) | async-done | bytes 1835040 | tf_op jit(solution)/shard_map/all_to_all | solution.py:204
  44.3 3.0 %shard_map.43 = (bf16[128,2304]{1,0:T(8,128)(2,1)S(1)}, bf16[128,2304]{1,0:T(8,128)(2,1)S(1)}, bf16[128,2304]{1,0:T(8,128)(2,1)S(1)}, bf16[128,2304]{1,0:T(8,128)(2,1)S(1)}) custom-call(s32[5]{0:T(128)S(1)} %stack.64.where_ref, bf16[16,448,128]{2,1,0:T(8,128)(2,1)} %all-to-all-done.columns_ref), custom_call_target="tpu_custom_call" | custom-call | flops 2415919104 | bytes 8000000 | tf_op jit(solution)/shard_map/pallas_call | solution.py:80
  47.3 2.2 %collective-permute-start.1 = (bf16[128,2304]{1,0:T(8,128)(2,1)S(1)}, bf16[128,2304]{1,0:T(8,128)(2,1)S(1)}, u32[]{:S(2)}, u32[]{:S(2)}) collective-permute-start(bf16[128,2304]{1,0:T(8,128)(2,1)S(1)} %get-tuple-element.17), channel_id=1, source_target_pairs={{0,16},{16,0},{32,48},{48,32},{64,80},{80,64},{96,112},{112,96},{1... | collective-permute-start | bytes 1769480 | tf_op jit(solution)/shard_map/ppermute | solution.py:187
  49.5 0.1 stack.63.where_ref
  49.5 0.0 collective-permute-start
  49.6 0.5 collective-permute-start.3
  50.1 0.1 collective-permute-start.5
  50.2 3.0 %shard_map.42 = (bf16[128,2304]{1,0:T(8,128)(2,1)S(1)}, bf16[128,2304]{1,0:T(8,128)(2,1)S(1)}, bf16[128,2304]{1,0:T(8,128)(2,1)S(1)}, bf16[128,2304]{1,0:T(8,128)(2,1)S(1)}) custom-call(s32[5]{0:T(128)S(1)} %stack.63.where_ref, bf16[16,448,128]{2,1,0:T(8,128)(2,1)} %all-to-all-done.columns_ref), custom_call_target="tpu_custom_call" | custom-call | flops 2415919104 | bytes 8000000 | tf_op jit(solution)/shard_map/pallas_call | solution.py:80
  53.2 0.0 collective-permute-done.1
  53.2 0.2 add_convert_fusion.4
  53.4 3.0 %collective-permute-start.2 = (bf16[128,2304]{1,0:T(8,128)(2,1)S(1)}, bf16[128,2304]{1,0:T(8,128)(2,1)S(1)}, u32[]{:S(2)}, u32[]{:S(2)}) collective-permute-start(bf16[128,2304]{1,0:T(8,128)(2,1)S(1)} %add_convert_fusion.4), channel_id=1, source_target_pairs={{0,64},{16,80},{32,96},{48,112},{64,0},{80,16},{96,32},{112,48},{1... | collective-permute-start | bytes 1769480 | tf_op jit(solution)/shard_map/ppermute | solution.py:192
  56.4 0.0 collective-permute-done.3
  56.4 0.1 add_convert_fusion.3
  56.5 0.5 collective-permute-start.4
  57.0 0.0 collective-permute-done.5
  57.0 0.1 add_convert_fusion.2
  57.1 2.3 %collective-permute-start.6 = (bf16[128,2304]{1,0:T(8,128)(2,1)S(1)}, bf16[128,2304]{1,0:T(8,128)(2,1)S(1)}, u32[]{:S(2)}, u32[]{:S(2)}) collective-permute-start(bf16[128,2304]{1,0:T(8,128)(2,1)S(1)} %add_convert_fusion.2), channel_id=1, source_target_pairs={{0,96},{16,112},{32,0},{48,16},{64,32},{80,48},{96,64},{112,80},{1... | collective-permute-start | bytes 1769480 | tf_op jit(solution)/shard_map/ppermute | solution.py:192
  59.5 0.0 collective-permute-done
  59.5 10.0 %collective-permute-done.2 = bf16[128,2304]{1,0:T(8,128)(2,1)S(1)} collective-permute-done((bf16[128,2304]{1,0:T(8,128)(2,1)S(1)}, bf16[128,2304]{1,0:T(8,128)(2,1)S(1)}, u32[]{:S(2)}, u32[]{:S(2)}) %collective-permute-start.2) | collective-permute-done | bytes 589856 | tf_op jit(solution)/shard_map/ppermute | solution.py:192
  69.5 13.4 %collective-permute-done.4 = bf16[128,2304]{1,0:T(8,128)(2,1)S(1)} collective-permute-done((bf16[128,2304]{1,0:T(8,128)(2,1)S(1)}, bf16[128,2304]{1,0:T(8,128)(2,1)S(1)}, u32[]{:S(2)}, u32[]{:S(2)}) %collective-permute-start.4) | collective-permute-done | bytes 589856 | tf_op jit(solution)/shard_map/ppermute | solution.py:192
  82.8 0.0 collective-permute-done.6
  82.8 0.4 add_convert_fusion.1
  83.2 0.1 collective-permute-start.7
  83.3 14.0 %collective-permute-done.7 = bf16[128,2304]{1,0:T(8,128)(2,1)S(1)} collective-permute-done((bf16[128,2304]{1,0:T(8,128)(2,1)S(1)}, bf16[128,2304]{1,0:T(8,128)(2,1)S(1)}, u32[]{:S(2)}, u32[]{:S(2)}) %collective-permute-start.7) | collective-permute-done | bytes 589856 | tf_op jit(solution)/shard_map/ppermute | solution.py:196
  97.3 0.1 add_convert_fusion.refs_0_
  97.4 3.2 %collective-permute-start.10 = (bf16[128,2304]{1,0:T(8,128)(2,1)S(1)}, bf16[128,2304]{1,0:T(8,128)(2,1)S(1)}, u32[]{:S(2)}, u32[]{:S(2)}) collective-permute-start(bf16[128,2304]{1,0:T(8,128)(2,1)S(1)} %add_convert_fusion.refs_0_), channel_id=1, source_target_pairs={{0,96},{16,112},{32,0},{48,16},{64,32},{80,48},{96,64},{112,80},{1... | collective-permute-start | bytes 1769480 | tf_op jit(solution)/shard_map/ppermute | solution.py:192
  100.6 0.2 collective-permute-start.9
  100.8 0.5 collective-permute-start.8
  101.3 1.9 collective-permute-start.11
  103.2 10.4 %collective-permute-done.10.refs_3_ = bf16[128,2304]{1,0:T(8,128)(2,1)S(1)} collective-permute-done((bf16[128,2304]{1,0:T(8,128)(2,1)S(1)}, bf16[128,2304]{1,0:T(8,128)(2,1)S(1)}, u32[]{:S(2)}, u32[]{:S(2)}) %collective-permute-start.10) | collective-permute-done | bytes 589856 | tf_op jit(solution)/shard_map/ppermute | solution.py:192
  113.6 13.2 %collective-permute-start.14 = (bf16[128,2304]{1,0:T(8,128)(2,1)S(1)}, bf16[128,2304]{1,0:T(8,128)(2,1)}, u32[]{:S(2)}, u32[]{:S(2)}) collective-permute-start(bf16[128,2304]{1,0:T(8,128)(2,1)S(1)} %collective-permute-done.10.refs_3_), channel_id=1, source_target_pairs={{0,16},{16,0},{32,48},{48,32},{64,80},{80,64},{96,112},{112,96},{1... | collective-permute-start | bytes 1769480 | tf_op jit(solution)/shard_map/ppermute | solution.py:187
  126.8 0.0 collective-permute-done.9.refs_2_
  126.8 0.0 collective-permute-start.13
  126.8 3.0 %collective-permute-done.8.refs_1_ = bf16[128,2304]{1,0:T(8,128)(2,1)S(1)} collective-permute-done((bf16[128,2304]{1,0:T(8,128)(2,1)S(1)}, bf16[128,2304]{1,0:T(8,128)(2,1)S(1)}, u32[]{:S(2)}, u32[]{:S(2)}) %collective-permute-start.8) | collective-permute-done | bytes 589856 | tf_op jit(solution)/shard_map/ppermute | solution.py:192
  129.8 0.6 collective-permute-start.12
  130.4 0.1 stack.59.where_ref
  130.5 0.0 collective-permute-done.11.refs_4_
  130.5 0.0 collective-permute-done.14.refs_7_
  130.5 0.0 collective-permute-done.13.refs_6_
  130.5 1.5 collective-permute-done.12.refs_5_
  132.0 40.5 %shard_map.44 = bf16[16,448,128]{2,1,0:T(8,128)(2,1)} custom-call(s32[16]{0:T(128)S(1)} %stack.59.where_ref, bf16[16,448,128]{2,1,0:T(8,128)(2,1)} %all-to-all-done.columns_ref, bf16[128,2304]{1,0:T(8,128)(2,1)S(1)} %add_convert_fusion.refs_0_, bf16[128,2304]{1,0:T(8,128)(2,1)S(1)} %collective-permute-done.8.refs_1_, ...), custom_call_target="tpu_custom_call" | custom-call | flops 7516192768 | bytes 8000000 | tf_op jit(solution)/shard_map/pallas_call | solution.py:148
  172.6 28.9 %all_to_all.10 = bf16[16,448,128]{2,1,0:T(8,128)(2,1)S(1)} all-to-all(bf16[16,448,128]{2,1,0:T(8,128)(2,1)} %shard_map.44), channel_id=1, replica_groups=mesh['fsdp'=8,'mat'=16] {'mat'}, dimensions={0} | all-to-all | bytes 3670016 | tf_op jit(solution)/shard_map/all_to_all | solution.py:221
  201.4 3.4 %shard_map.45 = bf16[8,128,896]{2,1,0:T(8,128)(2,1)} custom-call(bf16[8,896,128]{2,1,0:T(8,128)(2,1)S(1)} %bitcast.11), custom_call_target="tpu_custom_call" | custom-call | tf_op jit(solution)/shard_map/pallas_call | solution.py:169
Async XLA Ops:
  0.6 1.5 copy-start
  9.0 35.3 %all-to-all-start = ((bf16[16,448,128]{2,1,0:T(8,128)(2,1)}), bf16[16,448,128]{2,1,0:T(8,128)(2,1)}, u32[]{:S(2)}, u32[]{:S(2)}) async-start(bf16[16,448,128]{2,1,0:T(8,128)(2,1)} %bitcast.6), calls=%async_computation | async-start | bytes 3670016 | tf_op jit(solution)/shard_map/all_to_all | solution.py:204
  47.3 5.9 %collective-permute-start.1 = (bf16[128,2304]{1,0:T(8,128)(2,1)S(1)}, bf16[128,2304]{1,0:T(8,128)(2,1)S(1)}, u32[]{:S(2)}, u32[]{:S(2)}) collective-permute-start(bf16[128,2304]{1,0:T(8,128)(2,1)S(1)} %get-tuple-element.17), channel_id=1, source_target_pairs={{0,16},{16,0},{32,48},{48,32},{64,80},{80,64},{96,112},{112,96},{1... | collective-permute-start | bytes 1769480 | tf_op jit(solution)/shard_map/ppermute | solution.py:187
  49.5 9.9 %collective-permute-start = (bf16[128,2304]{1,0:T(8,128)(2,1)S(1)}, bf16[128,2304]{1,0:T(8,128)(2,1)S(1)}, u32[]{:S(2)}, u32[]{:S(2)}) collective-permute-start(bf16[128,2304]{1,0:T(8,128)(2,1)S(1)} %get-tuple-element.15), channel_id=1, source_target_pairs={{0,16},{16,0},{32,48},{48,32},{64,80},{80,64},{96,112},{112,96},{1... | collective-permute-start | bytes 1769480 | tf_op jit(solution)/shard_map/ppermute | solution.py:187
  49.6 6.8 %collective-permute-start.3 = (bf16[128,2304]{1,0:T(8,128)(2,1)S(1)}, bf16[128,2304]{1,0:T(8,128)(2,1)S(1)}, u32[]{:S(2)}, u32[]{:S(2)}) collective-permute-start(bf16[128,2304]{1,0:T(8,128)(2,1)S(1)} %get-tuple-element.19), channel_id=1, source_target_pairs={{0,16},{16,0},{32,48},{48,32},{64,80},{80,64},{96,112},{112,96},{1... | collective-permute-start | bytes 1769480 | tf_op jit(solution)/shard_map/ppermute | solution.py:187
  50.1 6.9 %collective-permute-start.5 = (bf16[128,2304]{1,0:T(8,128)(2,1)S(1)}, bf16[128,2304]{1,0:T(8,128)(2,1)S(1)}, u32[]{:S(2)}, u32[]{:S(2)}) collective-permute-start(bf16[128,2304]{1,0:T(8,128)(2,1)S(1)} %get-tuple-element.21), channel_id=1, source_target_pairs={{0,16},{16,0},{32,48},{48,32},{64,80},{80,64},{96,112},{112,96},{1... | collective-permute-start | bytes 1769480 | tf_op jit(solution)/shard_map/ppermute | solution.py:187
  53.4 16.1 %collective-permute-start.2 = (bf16[128,2304]{1,0:T(8,128)(2,1)S(1)}, bf16[128,2304]{1,0:T(8,128)(2,1)S(1)}, u32[]{:S(2)}, u32[]{:S(2)}) collective-permute-start(bf16[128,2304]{1,0:T(8,128)(2,1)S(1)} %add_convert_fusion.4), channel_id=1, source_target_pairs={{0,64},{16,80},{32,96},{48,112},{64,0},{80,16},{96,32},{112,48},{1... | collective-permute-start | bytes 1769480 | tf_op jit(solution)/shard_map/ppermute | solution.py:192
  56.5 26.3 %collective-permute-start.4 = (bf16[128,2304]{1,0:T(8,128)(2,1)S(1)}, bf16[128,2304]{1,0:T(8,128)(2,1)S(1)}, u32[]{:S(2)}, u32[]{:S(2)}) collective-permute-start(bf16[128,2304]{1,0:T(8,128)(2,1)S(1)} %add_convert_fusion.3), channel_id=1, source_target_pairs={{0,32},{16,48},{32,64},{48,80},{64,96},{80,112},{96,0},{112,16},{1... | collective-permute-start | bytes 1769480 | tf_op jit(solution)/shard_map/ppermute | solution.py:192
  57.1 25.7 %collective-permute-start.6 = (bf16[128,2304]{1,0:T(8,128)(2,1)S(1)}, bf16[128,2304]{1,0:T(8,128)(2,1)S(1)}, u32[]{:S(2)}, u32[]{:S(2)}) collective-permute-start(bf16[128,2304]{1,0:T(8,128)(2,1)S(1)} %add_convert_fusion.2), channel_id=1, source_target_pairs={{0,96},{16,112},{32,0},{48,16},{64,32},{80,48},{96,64},{112,80},{1... | collective-permute-start | bytes 1769480 | tf_op jit(solution)/shard_map/ppermute | solution.py:192
  83.2 14.0 %collective-permute-start.7 = (bf16[128,2304]{1,0:T(8,128)(2,1)S(1)}, bf16[128,2304]{1,0:T(8,128)(2,1)S(1)}, u32[]{:S(2)}, u32[]{:S(2)}) collective-permute-start(bf16[128,2304]{1,0:T(8,128)(2,1)S(1)} %add_convert_fusion.1), channel_id=1, source_target_pairs={{0,1},{1,0},{2,3},{3,2},{4,5},{5,4},{6,7},{7,6},{8,9},{9,8},{10,11... | collective-permute-start | bytes 1769480 | tf_op jit(solution)/shard_map/ppermute | solution.py:196
  97.4 16.3 %collective-permute-start.10 = (bf16[128,2304]{1,0:T(8,128)(2,1)S(1)}, bf16[128,2304]{1,0:T(8,128)(2,1)S(1)}, u32[]{:S(2)}, u32[]{:S(2)}) collective-permute-start(bf16[128,2304]{1,0:T(8,128)(2,1)S(1)} %add_convert_fusion.refs_0_), channel_id=1, source_target_pairs={{0,96},{16,112},{32,0},{48,16},{64,32},{80,48},{96,64},{112,80},{1... | collective-permute-start | bytes 1769480 | tf_op jit(solution)/shard_map/ppermute | solution.py:192
  100.6 26.2 %collective-permute-start.9 = (bf16[128,2304]{1,0:T(8,128)(2,1)S(1)}, bf16[128,2304]{1,0:T(8,128)(2,1)S(1)}, u32[]{:S(2)}, u32[]{:S(2)}) collective-permute-start(bf16[128,2304]{1,0:T(8,128)(2,1)S(1)} %add_convert_fusion.refs_0_), channel_id=1, source_target_pairs={{0,64},{16,80},{32,96},{48,112},{64,0},{80,16},{96,32},{112,48},{1... | collective-permute-start | bytes 1769480 | tf_op jit(solution)/shard_map/ppermute | solution.py:192
  100.8 29.0 %collective-permute-start.8 = (bf16[128,2304]{1,0:T(8,128)(2,1)S(1)}, bf16[128,2304]{1,0:T(8,128)(2,1)S(1)}, u32[]{:S(2)}, u32[]{:S(2)}) collective-permute-start(bf16[128,2304]{1,0:T(8,128)(2,1)S(1)} %add_convert_fusion.refs_0_), channel_id=1, source_target_pairs={{0,32},{16,48},{32,64},{48,80},{64,96},{80,112},{96,0},{112,16},{1... | collective-permute-start | bytes 1769480 | tf_op jit(solution)/shard_map/ppermute | solution.py:192
  101.3 29.2 %collective-permute-start.11 = (bf16[128,2304]{1,0:T(8,128)(2,1)S(1)}, bf16[128,2304]{1,0:T(8,128)(2,1)S(1)}, u32[]{:S(2)}, u32[]{:S(2)}) collective-permute-start(bf16[128,2304]{1,0:T(8,128)(2,1)S(1)} %add_convert_fusion.refs_0_), channel_id=1, source_target_pairs={{0,16},{16,0},{32,48},{48,32},{64,80},{80,64},{96,112},{112,96},{1... | collective-permute-start | bytes 1769480 | tf_op jit(solution)/shard_map/ppermute | solution.py:187
  113.6 16.9 %collective-permute-start.14 = (bf16[128,2304]{1,0:T(8,128)(2,1)S(1)}, bf16[128,2304]{1,0:T(8,128)(2,1)}, u32[]{:S(2)}, u32[]{:S(2)}) collective-permute-start(bf16[128,2304]{1,0:T(8,128)(2,1)S(1)} %collective-permute-done.10.refs_3_), channel_id=1, source_target_pairs={{0,16},{16,0},{32,48},{48,32},{64,80},{80,64},{96,112},{112,96},{1... | collective-permute-start | bytes 1769480 | tf_op jit(solution)/shard_map/ppermute | solution.py:187
  126.8 3.7 %collective-permute-start.13 = (bf16[128,2304]{1,0:T(8,128)(2,1)S(1)}, bf16[128,2304]{1,0:T(8,128)(2,1)}, u32[]{:S(2)}, u32[]{:S(2)}) collective-permute-start(bf16[128,2304]{1,0:T(8,128)(2,1)S(1)} %collective-permute-done.9.refs_2_), channel_id=1, source_target_pairs={{0,16},{16,0},{32,48},{48,32},{64,80},{80,64},{96,112},{112,96},{1... | collective-permute-start | bytes 1769480 | tf_op jit(solution)/shard_map/ppermute | solution.py:187
  129.8 2.2 %collective-permute-start.12 = (bf16[128,2304]{1,0:T(8,128)(2,1)S(1)}, bf16[128,2304]{1,0:T(8,128)(2,1)S(1)}, u32[]{:S(2)}, u32[]{:S(2)}) collective-permute-start(bf16[128,2304]{1,0:T(8,128)(2,1)S(1)} %collective-permute-done.8.refs_1_), channel_id=1, source_target_pairs={{0,16},{16,0},{32,48},{48,32},{64,80},{80,64},{96,112},{112,96},{1... | collective-permute-start | bytes 1769480 | tf_op jit(solution)/shard_map/ppermute | solution.py:187

commit v2 on v1

v2 whole, which is shorter than its diff:
```python
import functools
import math

import jax
import jax.numpy as jnp
from jax import lax
from jax.experimental import pallas as pl
from jax.experimental.pallas import tpu as pltpu
from jax.sharding import PartitionSpec as P

EXPERTS, ROWS, COLS = 8, 2048, 7168
CORES, RING, PAIR = 2, 4, 2
MEMBERS = 16
LANES = ROWS // MEMBERS
WIDE = COLS // 8
HALF = WIDE // 2
BLOCK = 256
FOLD = 9 * BLOCK
PIECE = 128

momentum_rate = 0.95
first_coef = 3.4445
second_coef = -4.775
third_coef = 2.0315
epsilon_value = 1e-06
f32, bf16 = jnp.float32, jnp.bfloat16
HALVES = PIECE // PAIR
PARAMS = pltpu.CompilerParams(vmem_limit_bytes=50 * 1024 * 1024)
WHOLE = pl.BlockSpec(memory_space=pltpu.VMEM)
ANYWHERE = pl.BlockSpec(memory_space=pl.ANY)
SCALARS = pl.BlockSpec(memory_space=pltpu.SMEM)


def blend_kernel(momentum_ref, gradient_ref, blended_ref):
    gradient = gradient_ref[0].astype(f32)
    new = momentum_rate * momentum_ref[0] + gradient
    blended_ref[0] = (gradient + momentum_rate * new).astype(bf16).T


def blend(momentum, gradient):
    block = pl.BlockSpec((1, LANES, WIDE), lambda e: (e, 0, 0))
    return pl.pallas_call(
        blend_kernel,
        grid=(EXPERTS,),
        in_specs=[block, block],
        out_specs=pl.BlockSpec((1, WIDE, LANES), lambda e: (e, 0, 0)),
        out_shape=jax.ShapeDtypeStruct((EXPERTS, WIDE, LANES), bf16),
        compiler_params=PARAMS,
    )(momentum, gradient)


def gram_kernel(groups, where_ref, columns_ref, *group_refs):
    half = where_ref[0]
    slot = 0
    for count, group_ref in zip(groups, group_refs):
        for member_slot in range(count):
            slot += 1
            piece = where_ref[slot]
            folded = 2 * half + piece // 2
            top = columns_ref[2 * folded + piece % 2].T
            low = columns_ref[2 * (7 - folded) + piece % 2].T
            for block in range(9):
                member = 2 * jnp.where(block < 8 - folded, folded + block, block - 1)
                right = jnp.concatenate([columns_ref[member], columns_ref[member + 1]], axis=1)
                left = jnp.where(block < 8 - folded, top, low) if 4 < block < 8 else (top if block <= 4 else low)
                values = jnp.dot(left, right, preferred_element_type=f32).astype(bf16)
                group_ref[member_slot, :, block * BLOCK : (block + 1) * BLOCK] = values


def gram_pieces(columns, half, groups, pieces):
    where = jnp.stack([half, *pieces]).astype(jnp.int32)
    return pl.pallas_call(
        functools.partial(gram_kernel, groups),
        in_specs=[SCALARS, WHOLE],
        out_specs=[WHOLE] * len(groups),
        out_shape=[jax.ShapeDtypeStruct((count, PIECE, FOLD), bf16) for count in groups],
        compiler_params=PARAMS,
        cost_estimate=pl.CostEstimate(
            flops=4 * len(pieces) * PIECE * FOLD * 512, bytes_accessed=2_000_000 * len(pieces), transcendentals=0
        ),
    )(where, columns)


STEP = 16


def step_kernel(layout, where_ref, columns_ref, *refs):
    piece_refs, out_ref = refs[: len(set(t[0] for t in layout))], refs[len(set(t[0] for t in layout))]
    parts, columns, staged, gram, blended, mixed, product, image, piece_sems, columns_sem, out_sems = refs[
        len(piece_refs) + 1 :
    ]
    copies = []
    for n, (array, start, rows) in enumerate(layout):
        target = parts.at[where_ref[2 * n], pl.ds(pl.multiple_of(where_ref[2 * n + 1], 32), rows), :]
        copies.append(pltpu.make_async_copy(piece_refs[array].at[pl.ds(start, rows), :], target, piece_sems.at[n]))
    for copy in copies:
        copy.start()
    columns_copy = pltpu.make_async_copy(columns_ref, columns, columns_sem)
    columns_copy.start()
    for copy in copies:
        copy.wait()
    for chunk in range(CORES * RING):
        folded, shifted = chunk // 2, chunk % 2 * PIECE
        for block in range(9):
            upper = block < 8 - folded
            row = (folded if upper else 7 - folded) * BLOCK + shifted
            column = (folded + block if upper else block - 1) * BLOCK
            values = parts[chunk, :, block * BLOCK : (block + 1) * BLOCK]
            gram[row : row + PIECE, column : column + BLOCK] = values
            if row // BLOCK * BLOCK != column:
                gram[column : column + BLOCK, row : row + PIECE] = values.T
    columns_copy.wait()
    for member in range(MEMBERS):
        blended[:, member * LANES : (member + 1) * LANES] = columns[member]

    def image_of(weights, blocks):
        total = jnp.zeros((8, ROWS), f32)
        for step in range(ROWS // STEP):
            if step % 16 == 0 and step // 16 < len(blocks):
                at = slice(blocks[step // 16] * BLOCK, (blocks[step // 16] + 1) * BLOCK)
                product[:, at] = jnp.dot(blended[...], gram[:, at], preferred_element_type=f32)
            at = slice(step * STEP, (step + 1) * STEP)
            values = gram[at, :].astype(f32)
            if weights is not None:
                values = values * weights[at, :]
            total = total + (values[:8] + values[8:])
        return jnp.sum(total, axis=0, keepdims=True)

    def length_of(values):
        return jnp.sqrt(jnp.sum(values * values) + epsilon_value)

    def stand(values):
        for member in range(MEMBERS):
            at = slice(member * LANES, (member + 1) * LANES)
            image[at, :] = jnp.broadcast_to(values[:, at], (8, LANES)).T[:, :1]

    values = image_of(None, (0, 1))
    stand(values / length_of(values))
    values = image_of(image, (2, 3, 4))
    stand(values / length_of(values))
    values = image_of(image, (5, 6, 7))
    scale = lax.rsqrt(jnp.full((1, 1), length_of(values) + epsilon_value, f32))
    square = scale * scale

    for block in range(8):
        at = slice(block * BLOCK, (block + 1) * BLOCK)
        mixed[:, at] = (second_coef * blended[:, at].astype(f32) + (third_coef * square) * product[:, at]).astype(bf16)
    out_copies = []
    for block in range(8):
        at = slice(block * BLOCK, (block + 1) * BLOCK)
        last = jnp.dot(mixed[...], gram[:, at], preferred_element_type=f32)
        update = (math.sqrt(COLS) * scale) * (first_coef * blended[:, at].astype(f32) + square * last)
        update = update.astype(bf16)
        staged[2 * block] = update[:, :LANES]
        staged[2 * block + 1] = update[:, LANES:]
        at = pl.ds(2 * block, 2)
        out_copies.append(pltpu.make_async_copy(staged.at[at], out_ref.at[at], out_sems.at[block]))
        out_copies[-1].start()
    for copy in out_copies:
        copy.wait()


def newton_step(columns, pieces, layout, where):
    matrix = (MEMBERS, HALF, LANES)
    return pl.pallas_call(
        functools.partial(step_kernel, layout),
        in_specs=[SCALARS, ANYWHERE] + [ANYWHERE] * len(pieces),
        out_specs=ANYWHERE,
        out_shape=jax.ShapeDtypeStruct(matrix, bf16),
        scratch_shapes=[
            pltpu.VMEM((CORES * RING, PIECE, FOLD), bf16),
            pltpu.VMEM(matrix, bf16),
            pltpu.VMEM(matrix, bf16),
            pltpu.VMEM((ROWS, ROWS), bf16),
            pltpu.VMEM((HALF, ROWS), bf16),
            pltpu.VMEM((HALF, ROWS), bf16),
            pltpu.VMEM((HALF, ROWS), f32),
            pltpu.VMEM((ROWS, 1), f32),
            pltpu.SemaphoreType.DMA((len(layout),)),
            pltpu.SemaphoreType.DMA,
            pltpu.SemaphoreType.DMA((8,)),
        ],
        compiler_params=PARAMS,
        cost_estimate=pl.CostEstimate(flops=4 * ROWS * ROWS * HALF, bytes_accessed=8_000_000, transcendentals=0),
    )(where, columns, *pieces)


def spread_kernel(update_ref, out_ref):
    out_ref[0] = update_ref[0].T


def spread(update):
    return pl.pallas_call(
        spread_kernel,
        grid=(EXPERTS,),
        in_specs=[pl.BlockSpec((1, WIDE, LANES), lambda e: (e, 0, 0))],
        out_specs=pl.BlockSpec((1, LANES, WIDE), lambda e: (e, 0, 0)),
        out_shape=jax.ShapeDtypeStruct((EXPERTS, LANES, WIDE), bf16),
        compiler_params=PARAMS,
    )(update)


def total_of(*terms):
    total = terms[0].astype(f32)
    for term in terms[1:]:
        total = total + term.astype(f32)
    return total


def add(*terms):
    return total_of(*terms).astype(bf16)


def swap_cores(values):
    return lax.ppermute(values, "fsdp", [(i, i ^ 1) for i in range(CORES * RING)])


def shift(values, distance):
    size = CORES * RING
    return lax.ppermute(values, "fsdp", [(i, (i + CORES * distance) % size) for i in range(size)])


def swap_pair(values):
    return lax.ppermute(values, "mat", [(i, i ^ 1) for i in range(MEMBERS)])


def shards(momentum, gradient):
    index = lax.axis_index("fsdp")
    core, place_y = index % CORES, index // CORES
    side = lax.axis_index("mat") % PAIR
    blended = blend(momentum, gradient)
    columns = lax.all_to_all(blended.reshape(MEMBERS, HALF, LANES), "mat", 0, 0)
    new_momentum = momentum_rate * momentum + gradient.astype(f32)

    far, ahead, behind = [(place_y + distance) % RING for distance in (2, 1, 3)]
    (away_far,) = gram_pieces(columns, 1 - core, (1,), [far])
    away_near, away_own = gram_pieces(columns, 1 - core, (2, 1), [ahead, behind, place_y])
    kept_far, kept_near, kept_own = gram_pieces(columns, core, (1, 2, 1), [far, ahead, behind, place_y])
    got_far = swap_cores(away_far)
    got_near = swap_cores(away_near)
    got_own = swap_cores(away_own)
    first, second = slice(0, HALVES), slice(HALVES, PIECE)
    via_behind = shift(add(kept_far[0, first], got_far[0, first]), 1)
    via_ahead = shift(add(kept_far[0, second], got_far[0, second]), -1)
    second_behind = shift(add(kept_near[0, second], got_near[0, second]), 1)
    first_ahead = shift(add(kept_near[1, first], got_near[1, first]), -1)
    first_behind = shift(add(kept_near[0, first], got_near[0, first], via_behind), 1)
    second_ahead = shift(add(kept_near[1, second], got_near[1, second], via_ahead), -1)
    first_sum = total_of(kept_own[0, first], got_own[0, first], first_ahead, first_behind)
    second_sum = total_of(kept_own[0, second], got_own[0, second], second_behind, second_ahead)
    given = jnp.where(side == 0, second_sum, first_sum).astype(bf16)
    own = add(jnp.where(side == 0, first_sum, second_sum), swap_pair(given))

    pieces, layout, where = [], [], []

    def take(array, *spans):
        swapped = swap_cores(array)
        for values, half in ((array, core), (swapped, 1 - core)):
            start = 0
            for rows, chunk, offset in spans:
                layout.append((len(pieces), start, rows))
                where.extend([half * RING + chunk, offset])
                start += rows
            pieces.append(values)

    opposite = swap_pair(own)
    quarter = HALVES // 2
    offsets = (side * HALVES, (1 - side) * HALVES)
    ends = []
    for half_piece, offset in zip((own, opposite), offsets):
        from_behind, from_ahead = shift(half_piece, 1), shift(half_piece, -1)
        take(half_piece, (HALVES, place_y, offset))
        take(from_behind, (HALVES, behind, offset))
        take(from_ahead, (HALVES, ahead, offset))
        ends += [shift(from_behind[:quarter], 1), shift(from_ahead[quarter:], -1)]
    spans = [(quarter, far, offset + part) for offset in offsets for part in (0, quarter)]
    take(jnp.concatenate(ends, axis=0), *spans)

    update = newton_step(columns, pieces, tuple(layout), jnp.stack(where).astype(jnp.int32))
    returned = lax.all_to_all(update, "mat", 0, 0)
    return new_momentum, spread(returned.reshape(EXPERTS, WIDE, LANES))


def solution(mesh):
    spec = P(None, "mat", "fsdp")
    return jax.shard_map(shards, mesh=mesh, in_specs=(spec, spec), out_specs=(spec, spec), check_vma=False)
```

time: 205 us -> 179 us (0.87)
  blocking collectives: 28.9 us -> 0 us
  Pallas kernels: 56.7 us -> 33.3 us
  waiting for transfers between devices: 78.9 us -> 88.4 us
  other arithmetic: 0.96 us -> 8.71 us
  starting transfers between devices: 36.8 us -> 42.4 us
  local copies, waits for them, and re-layouts: 1.75 us -> 4.43 us
    all_to_all x1 -> x0, blocking collectives: 28.9 us -> none  [shards(): returned = lax.all_to_all(update, 'mat', 0, 0)]
    all_to_all x0 -> x1, waiting for transfers between devices: none -> 24.5 us  [shards(): returned = lax.all_to_all(update, 'mat', 0, 0)]
    pallas_call x3 -> x4, Pallas kernels: 46.5 us -> 23.6 us  [the longest x1 17.9 us: newton_step(): pl.pallas_call(functools.partial(step_kernel, layout), in_specs=[SCALARS,...]
    ppermute x1 -> x2, waiting for transfers between devices: 14 us -> 5.98 us  [swap_pair(): return lax.ppermute(values, 'mat', [(i, i ^ 1) for i in range(MEMBERS)])]
    ppermute x6 -> x14, waiting for transfers between devices: 36.8 us -> 29.2 us  [shift(): lax.ppermute(values, 'fsdp', [(i, (i + CORES * distance) % size) for i in...]
    ppermute x6 -> x14, starting transfers between devices: 9.72 us -> 17 us  [shift(): lax.ppermute(values, 'fsdp', [(i, (i + CORES * distance) % size) for i in...]
    ppermute x8 -> x10, starting transfers between devices: 18.5 us -> 12.9 us  [swap_cores(): lax.ppermute(values, 'fsdp', [(i, i ^ 1) for i in range(CORES * RING)])]
    add x0 -> x1, other arithmetic: none -> 4.86 us  [shards(): new_momentum = momentum_rate * momentum + gradient.astype(f32)]
  transfers between devices with their start and end apart: 16 -> 28, of which waited for: 7 -> 15; matrix products, arithmetic and copies ran while one was open for 0% -> 6% of each run, Pallas kernels for 1% -> 3%
where the time goes in v2:
time: 179 us; the launch traced here: 178 us
  waiting for transfers between devices  88.4 us (49%)
  starting transfers between devices  42.4 us (24%)
  Pallas kernels  33.3 us (19%)
  other arithmetic  8.71 us (5%)
  local copies, waits for them, and re-layouts  4.43 us (2%)
    ppermute x14, waiting for transfers between devices, shift(): lax.ppermute(values, 'fsdp', [(i, (i + CORES * distance) % size) for i in...  29.2 us
    all_to_all x1, waiting for transfers between devices, shards(): columns = lax.all_to_all(blended.reshape(MEMBERS, HALF, LANES), 'mat', 0, 0)  26.6 us
    all_to_all x1, waiting for transfers between devices, shards(): returned = lax.all_to_all(update, 'mat', 0, 0)  24.5 us
    pallas_call x1, Pallas kernels, newton_step(): pl.pallas_call(functools.partial(step_kernel, layout), in_specs=[SCALARS,...  17.9 us
    ppermute x14, starting transfers between devices, shift(): lax.ppermute(values, 'fsdp', [(i, (i + CORES * distance) % size) for i in...  17 us
    ppermute x10, starting transfers between devices, swap_cores(): lax.ppermute(values, 'fsdp', [(i, i ^ 1) for i in range(CORES * RING)])  12.9 us
    all_to_all x1, starting transfers between devices, shards(): columns = lax.all_to_all(blended.reshape(MEMBERS, HALF, LANES), 'mat', 0, 0)  8.43 us
    pallas_call x1, Pallas kernels, blend(): pl.pallas_call(blend_kernel, grid=(EXPERTS,), in_specs=[block, block], ou...  6.36 us
  transfers between devices with their start and end apart: 28, of which 15 were waited for; matrix products, arithmetic and copies ran while one was open for 6% of the time, Pallas kernels for 3%

profile of v2, /device:TPU:1, one launch (start us, length us, event | category | flops | bytes accessed | tf_op | source)
XLA Modules:
  0.0 178.2 jit_solution(14535339517712776587)
XLA Ops:
  0.6 0.0 copy-start.1
  0.6 1.5 copy-done.1
  2.1 6.4 %shard_map.41 = bf16[8,896,128]{2,1,0:T(8,128)(2,1)} custom-call(f32[8,128,896]{2,1,0:T(8,128)} %momentum_ref.1, bf16[8,128,896]{2,1,0:T(8,128)(2,1)S(1)} %copy-done.1), custom_call_target="tpu_custom_call" | custom-call | tf_op jit(solution)/shard_map/pallas_call | solution.py:42
  8.5 8.4 %all-to-all-start = ((bf16[16,448,128]{2,1,0:T(8,128)(2,1)}), bf16[16,448,128]{2,1,0:T(8,128)(2,1)S(1)}, u32[]{:S(2)}, u32[]{:S(2)}) async-start(bf16[16,448,128]{2,1,0:T(8,128)(2,1)} %bitcast.12), calls=%async_computation | async-start | bytes 3670016 | tf_op jit(solution)/shard_map/all_to_all | solution.py:232
  17.0 0.1 pad_add_fusion.1.where_ref
  17.0 26.6 %all-to-all-done.columns_ref = bf16[16,448,128]{2,1,0:T(8,128)(2,1)S(1)} async-done(((bf16[16,448,128]{2,1,0:T(8,128)(2,1)}), bf16[16,448,128]{2,1,0:T(8,128)(2,1)S(1)}, u32[]{:S(2)}, u32[]{:S(2)}) %all-to-all-start) | async-done | bytes 1835040 | tf_op jit(solution)/shard_map/all_to_all | solution.py:232
  43.7 1.1 shard_map.44
  44.7 2.2 %collective-permute-start.3 = (bf16[1,128,2304]{2,1,0:T(8,128)(2,1)S(1)}, bf16[1,128,2304]{2,1,0:T(8,128)(2,1)}, u32[]{:S(2)}, u32[]{:S(2)}) collective-permute-start(bf16[1,128,2304]{2,1,0:T(8,128)(2,1)S(1)} %shard_map.44), channel_id=1, source_target_pairs={{0,16},{16,0},{32,48},{48,32},{64,80},{80,64},{96,112},{112,96},{1... | collective-permute-start | bytes 1769480 | tf_op jit(solution)/shard_map/ppermute | solution.py:215
  47.0 0.1 stack.117.where_ref
  47.0 0.1 pad_add_fusion.where_ref
  47.1 1.7 shard_map.43
  48.8 0.1 collective-permute-start.1
  48.9 3.0 %shard_map.42 = (bf16[1,128,2304]{2,1,0:T(8,128)(2,1)S(1)}, bf16[2,128,2304]{2,1,0:T(8,128)(2,1)S(1)}, bf16[1,128,2304]{2,1,0:T(8,128)(2,1)S(1)}) custom-call(s32[5]{0:T(128)S(1)} %stack.117.where_ref, bf16[16,448,128]{2,1,0:T(8,128)(2,1)} %copy-done), custom_call_target="tpu_custom_call" | custom-call | flops 2415919104 | bytes 8000000 | tf_op jit(solution)/shard_map/pallas_call | solution.py:72
  51.9 0.0 collective-permute-done.3
  51.9 1.2 fusion.7
  53.1 2.8 %collective-permute-start.7 = (bf16[64,2304]{1,0:T(8,128)(2,1)S(1)}, bf16[64,2304]{1,0:T(8,128)(2,1)S(1)}, u32[]{:S(2)}, u32[]{:S(2)}) collective-permute-start(bf16[64,2304]{1,0:T(8,128)(2,1)S(1)} %get-tuple-element.16), channel_id=1, source_target_pairs={{0,96},{16,112},{32,0},{48,16},{64,32},{80,48},{96,64},{112,80},{1... | collective-permute-start | bytes 884744 | tf_op jit(solution)/shard_map/ppermute | solution.py:220
  55.9 0.7 collective-permute-start
  56.6 5.2 %collective-permute-done.7 = bf16[64,2304]{1,0:T(8,128)(2,1)S(1)} collective-permute-done((bf16[64,2304]{1,0:T(8,128)(2,1)S(1)}, bf16[64,2304]{1,0:T(8,128)(2,1)S(1)}, u32[]{:S(2)}, u32[]{:S(2)}) %collective-permute-start.7) | collective-permute-done | bytes 294944 | tf_op jit(solution)/shard_map/ppermute | solution.py:220
  61.8 3.1 %collective-permute-done.4 = bf16[64,2304]{1,0:T(8,128)(2,1)S(1)} collective-permute-done((bf16[64,2304]{1,0:T(8,128)(2,1)S(1)}, bf16[64,2304]{1,0:T(8,128)(2,1)S(1)}, u32[]{:S(2)}, u32[]{:S(2)}) %collective-permute-start.4) | collective-permute-done | bytes 294944 | tf_op jit(solution)/shard_map/ppermute | solution.py:220
  64.9 0.9 fusion
  65.8 0.3 collective-permute-start.8
  66.2 1.1 collective-permute-start.5
  67.3 1.0 fusion.6
  68.3 0.0 collective-permute-start.6
  68.3 2.7 %collective-permute-start.2 = (bf16[64,2304]{1,0:T(8,128)(2,1)}, bf16[64,2304]{1,0:T(8,128)(2,1)S(1)}, u32[]{:S(2)}, u32[]{:S(2)}) collective-permute-start(bf16[64,2304]{1,0:T(8,128)(2,1)} %get-tuple-element.13), channel_id=1, source_target_pairs={{0,96},{16,112},{32,0},{48,16},{64,32},{80,48},{96,64},{112,80},{1... | collective-permute-start | bytes 884744 | tf_op jit(solution)/shard_map/ppermute | solution.py:220
  70.9 2.0 %collective-permute-done.8 = bf16[64,2304]{1,0:T(8,128)(2,1)S(1)} collective-permute-done((bf16[64,2304]{1,0:T(8,128)(2,1)}, bf16[64,2304]{1,0:T(8,128)(2,1)S(1)}, u32[]{:S(2)}, u32[]{:S(2)}) %collective-permute-start.8) | collective-permute-done | bytes 294944 | tf_op jit(solution)/shard_map/ppermute | solution.py:220
  72.9 1.4 collective-permute-done.5
  74.3 6.3 %collective-permute-done.6 = bf16[64,2304]{1,0:T(8,128)(2,1)S(1)} collective-permute-done((bf16[64,2304]{1,0:T(8,128)(2,1)}, bf16[64,2304]{1,0:T(8,128)(2,1)S(1)}, u32[]{:S(2)}, u32[]{:S(2)}) %collective-permute-start.6) | collective-permute-done | bytes 294944 | tf_op jit(solution)/shard_map/ppermute | solution.py:220
  80.6 0.3 select_convert_fusion
  80.9 0.1 collective-permute-start.9
  81.0 6.0 %collective-permute-done.9 = bf16[64,2304]{1,0:T(8,128)(2,1)S(1)} collective-permute-done((bf16[64,2304]{1,0:T(8,128)(2,1)S(1)}, bf16[64,2304]{1,0:T(8,128)(2,1)S(1)}, u32[]{:S(2)}, u32[]{:S(2)}) %collective-permute-start.9) | collective-permute-done | bytes 294944 | tf_op jit(solution)/shard_map/ppermute | solution.py:224
  87.0 0.3 add_convert_fusion.refs_0_
  87.3 0.1 collective-permute-start.11
  87.4 2.7 %collective-permute-start.13 = (bf16[64,2304]{1,0:T(8,128)(2,1)S(1)}, bf16[64,2304]{1,0:T(8,128)(2,1)S(1)}, u32[]{:S(2)}, u32[]{:S(2)}) collective-permute-start(bf16[64,2304]{1,0:T(8,128)(2,1)S(1)} %add_convert_fusion.refs_0_), channel_id=1, source_target_pairs={{0,96},{16,112},{32,0},{48,16},{64,32},{80,48},{96,64},{112,80},{1... | collective-permute-start | bytes 884744 | tf_op jit(solution)/shard_map/ppermute | solution.py:220
  90.1 0.3 collective-permute-start.15
  90.4 3.8 %collective-permute-done.11.refs_2_ = bf16[64,2304]{1,0:T(8,128)(2,1)S(1)} collective-permute-done((bf16[64,2304]{1,0:T(8,128)(2,1)S(1)}, bf16[64,2304]{1,0:T(8,128)(2,1)S(1)}, u32[]{:S(2)}, u32[]{:S(2)}) %collective-permute-start.11) | collective-permute-done | bytes 294944 | tf_op jit(solution)/shard_map/ppermute | solution.py:220
  94.2 0.1 collective-permute-start.21
  94.3 4.8 %collective-permute-start.10 = (bf16[64,2304]{1,0:T(8,128)(2,1)S(1)}, bf16[64,2304]{1,0:T(8,128)(2,1)S(1)}, u32[]{:S(2)}, u32[]{:S(2)}) collective-permute-start(bf16[64,2304]{1,0:T(8,128)(2,1)S(1)} %add_convert_fusion.refs_0_), channel_id=1, source_target_pairs={{0,16},{16,0},{32,48},{48,32},{64,80},{80,64},{96,112},{112,96},{1... | collective-permute-start | bytes 884744 | tf_op jit(solution)/shard_map/ppermute | solution.py:215
  99.1 2.9 %collective-permute-start.22 = (bf16[32,2304]{1,0:T(8,128)(2,1)S(1)}, bf16[32,2304]{1,0:T(8,128)(2,1)S(1)}, u32[]{:S(2)}, u32[]{:S(2)}) collective-permute-start(bf16[32,2304]{1,0:T(8,128)(2,1)S(1)} %slice.89), channel_id=1, source_target_pairs={{0,96},{16,112},{32,0},{48,16},{64,32},{80,48},{96,64},{112,80},{1... | collective-permute-start | bytes 442376 | tf_op jit(solution)/shard_map/ppermute | solution.py:220
  102.0 0.1 collective-permute-start.19
  102.1 1.4 collective-permute-start.17
  103.5 1.8 %collective-permute-start.16 = (bf16[64,2304]{1,0:T(8,128)(2,1)S(1)}, bf16[64,2304]{1,0:T(8,128)(2,1)S(1)}, u32[]{:S(2)}, u32[]{:S(2)}) collective-permute-start(bf16[64,2304]{1,0:T(8,128)(2,1)S(1)} %collective-permute-done.15.refs_6_), channel_id=1, source_target_pairs={{0,16},{16,0},{32,48},{48,32},{64,80},{80,64},{96,112},{112,96},{1... | collective-permute-start | bytes 884744 | tf_op jit(solution)/shard_map/ppermute | solution.py:215
  105.3 0.7 constant_dynamic-update-slice_fusion.3
  106.0 5.6 %collective-permute-done.17.refs_8_ = bf16[64,2304]{1,0:T(8,128)(2,1)S(1)} collective-permute-done((bf16[64,2304]{1,0:T(8,128)(2,1)S(1)}, bf16[64,2304]{1,0:T(8,128)(2,1)S(1)}, u32[]{:S(2)}, u32[]{:S(2)}) %collective-permute-start.17) | collective-permute-done | bytes 294944 | tf_op jit(solution)/shard_map/ppermute | solution.py:220
  111.6 0.1 collective-permute-start.23
  111.7 0.7 constant_dynamic-update-slice_fusion.2
  112.4 2.7 %collective-permute-start.24 = (bf16[32,2304]{1,0:T(8,128)(2,1)S(1)}, bf16[32,2304]{1,0:T(8,128)(2,1)S(1)}, u32[]{:S(2)}, u32[]{:S(2)}) collective-permute-start(bf16[32,2304]{1,0:T(8,128)(2,1)S(1)} %slice.91), channel_id=1, source_target_pairs={{0,96},{16,112},{32,0},{48,16},{64,32},{80,48},{96,64},{112,80},{1... | collective-permute-start | bytes 442376 | tf_op jit(solution)/shard_map/ppermute | solution.py:220
  115.2 1.8 collective-permute-done.23
  116.9 0.7 constant_dynamic-update-slice_fusion.1
  117.6 0.7 constant_dynamic-update-slice_fusion.refs_12_
  118.3 2.3 %collective-permute-start.25 = (bf16[128,2304]{1,0:T(8,128)(2,1)}, bf16[128,2304]{1,0:T(8,128)(2,1)}, u32[]{:S(2)}, u32[]{:S(2)}) collective-permute-start(bf16[128,2304]{1,0:T(8,128)(2,1)} %constant_dynamic-update-slice_fusion.refs_12_), channel_id=1, source_target_pairs={{0,16},{16,0},{32,48},{48,32},{64,80},{80,64},{96,112},{112,96},{1... | collective-permute-start | bytes 1769480 | tf_op jit(solution)/shard_map/ppermute | solution.py:215
  120.5 0.5 collective-permute-start.12
  121.0 0.0 collective-permute-start.20
  121.1 0.5 collective-permute-start.18
  121.6 0.1 stack.111.where_ref
  121.7 0.8 collective-permute-done.14.refs_5_
  122.5 0.6 collective-permute-done.12.refs_3_
  123.0 0.4 collective-permute-done.20.refs_11_
  123.4 0.4 collective-permute-done.18.refs_9_
  123.9 17.9 %shard_map.45 = bf16[16,448,128]{2,1,0:T(8,128)(2,1)} custom-call(s32[40]{0:T(128)S(1)} %stack.111.where_ref, bf16[16,448,128]{2,1,0:T(8,128)(2,1)} %copy-done, bf16[64,2304]{1,0:T(8,128)(2,1)S(1)} %add_convert_fusion.refs_0_, bf16[64,2304]{1,0:T(8,128)(2,1)S(1)} %collective-permute-done.10.refs_1_, bf16[64,2304]{1,0:T(8,128)(2,1)S(1)} %collective-permute-done.11.refs_2_, ...), custom_call_target="tpu_custom_call" | custom-call | flops 7516192768 | bytes 8000000 | tf_op jit(solution)/shard_map/pallas_call | solution.py:165
  141.8 3.7 %all-to-all-start.1 = ((bf16[16,448,128]{2,1,0:T(8,128)(2,1)}), bf16[16,448,128]{2,1,0:T(8,128)(2,1)S(1)}, u32[]{:S(2)}, u32[]{:S(2)}) async-start(bf16[16,448,128]{2,1,0:T(8,128)(2,1)} %shard_map.45), calls=%async_computation.1 | async-start | bytes 3670016 | tf_op jit(solution)/shard_map/all_to_all | solution.py:280
  145.5 4.9 %convert_add_fusion = f32[8,128,896]{2,1,0:T(8,128)} fusion(bf16[8,128,896]{2,1,0:T(8,128)(2,1)} %gradient_ref.1, f32[8,128,896]{2,1,0:T(8,128)} %momentum_ref.1), kind=kLoop, calls=%fused_computation | loop fusion | flops 2752512 | bytes 9175040 | tf_op jit(solution)/shard_map/add | solution.py:233
  150.4 24.5 %all-to-all-done.1 = bf16[16,448,128]{2,1,0:T(8,128)(2,1)S(1)} async-done(((bf16[16,448,128]{2,1,0:T(8,128)(2,1)}), bf16[16,448,128]{2,1,0:T(8,128)(2,1)S(1)}, u32[]{:S(2)}, u32[]{:S(2)}) %all-to-all-start.1) | async-done | bytes 1835040 | tf_op jit(solution)/shard_map/all_to_all | solution.py:280
  174.8 3.4 %shard_map.46 = bf16[8,128,896]{2,1,0:T(8,128)(2,1)} custom-call(bf16[8,896,128]{2,1,0:T(8,128)(2,1)S(1)} %bitcast.52), custom_call_target="tpu_custom_call" | custom-call | tf_op jit(solution)/shard_map/pallas_call | solution.py:193
  (20 shorter events, 0.1 us)
Async XLA Ops:
  0.6 1.5 copy-start.1
  8.5 35.2 %all-to-all-start = ((bf16[16,448,128]{2,1,0:T(8,128)(2,1)}), bf16[16,448,128]{2,1,0:T(8,128)(2,1)S(1)}, u32[]{:S(2)}, u32[]{:S(2)}) async-start(bf16[16,448,128]{2,1,0:T(8,128)(2,1)} %bitcast.12), calls=%async_computation | async-start | bytes 3670016 | tf_op jit(solution)/shard_map/all_to_all | solution.py:232
  43.7 5.1 %copy-start = (bf16[16,448,128]{2,1,0:T(8,128)(2,1)}, bf16[16,448,128]{2,1,0:T(8,128)(2,1)S(1)}, u32[]{:S(2)}) copy-start(bf16[16,448,128]{2,1,0:T(8,128)(2,1)S(1)} %all-to-all-done.columns_ref) | copy-start | bytes 5505028
  44.7 7.2 %collective-permute-start.3 = (bf16[1,128,2304]{2,1,0:T(8,128)(2,1)S(1)}, bf16[1,128,2304]{2,1,0:T(8,128)(2,1)}, u32[]{:S(2)}, u32[]{:S(2)}) collective-permute-start(bf16[1,128,2304]{2,1,0:T(8,128)(2,1)S(1)} %shard_map.44), channel_id=1, source_target_pairs={{0,16},{16,0},{32,48},{48,32},{64,80},{80,64},{96,112},{112,96},{1... | collective-permute-start | bytes 1769480 | tf_op jit(solution)/shard_map/ppermute | solution.py:215
  48.8 16.1 %collective-permute-start.1 = (bf16[2,128,2304]{2,1,0:T(8,128)(2,1)S(1)}, bf16[2,128,2304]{2,1,0:T(8,128)(2,1)S(1)}, u32[]{:S(2)}, u32[]{:S(2)}) collective-permute-start(bf16[2,128,2304]{2,1,0:T(8,128)(2,1)S(1)} %get-tuple-element.10), channel_id=1, source_target_pairs={{0,16},{16,0},{32,48},{48,32},{64,80},{80,64},{96,112},{112,96},{1... | collective-permute-start | bytes 3538952 | tf_op jit(solution)/shard_map/ppermute | solution.py:215
  53.1 8.7 %collective-permute-start.7 = (bf16[64,2304]{1,0:T(8,128)(2,1)S(1)}, bf16[64,2304]{1,0:T(8,128)(2,1)S(1)}, u32[]{:S(2)}, u32[]{:S(2)}) collective-permute-start(bf16[64,2304]{1,0:T(8,128)(2,1)S(1)} %get-tuple-element.16), channel_id=1, source_target_pairs={{0,96},{16,112},{32,0},{48,16},{64,32},{80,48},{96,64},{112,80},{1... | collective-permute-start | bytes 884744 | tf_op jit(solution)/shard_map/ppermute | solution.py:220
  55.9 9.0 %collective-permute-start.4 = (bf16[64,2304]{1,0:T(8,128)(2,1)S(1)}, bf16[64,2304]{1,0:T(8,128)(2,1)S(1)}, u32[]{:S(2)}, u32[]{:S(2)}) collective-permute-start(bf16[64,2304]{1,0:T(8,128)(2,1)S(1)} %get-tuple-element.17), channel_id=1, source_target_pairs={{0,32},{16,48},{32,64},{48,80},{64,96},{80,112},{96,0},{112,16},{1... | collective-permute-start | bytes 884744 | tf_op jit(solution)/shard_map/ppermute | solution.py:220
  55.9 15.0 %collective-permute-start = (bf16[1,128,2304]{2,1,0:T(8,128)(2,1)S(1)}, bf16[1,128,2304]{2,1,0:T(8,128)(2,1)S(1)}, u32[]{:S(2)}, u32[]{:S(2)}) collective-permute-start(bf16[1,128,2304]{2,1,0:T(8,128)(2,1)S(1)} %get-tuple-element.8), channel_id=1, source_target_pairs={{0,16},{16,0},{32,48},{48,32},{64,80},{80,64},{96,112},{112,96},{1... | collective-permute-start | bytes 1769480 | tf_op jit(solution)/shard_map/ppermute | solution.py:215
  65.8 7.1 %collective-permute-start.8 = (bf16[64,2304]{1,0:T(8,128)(2,1)}, bf16[64,2304]{1,0:T(8,128)(2,1)S(1)}, u32[]{:S(2)}, u32[]{:S(2)}) collective-permute-start(bf16[64,2304]{1,0:T(8,128)(2,1)} %get-tuple-element.14), channel_id=1, source_target_pairs={{0,96},{16,112},{32,0},{48,16},{64,32},{80,48},{96,64},{112,80},{1... | collective-permute-start | bytes 884744 | tf_op jit(solution)/shard_map/ppermute | solution.py:220
  66.2 8.1 %collective-permute-start.5 = (bf16[64,2304]{1,0:T(8,128)(2,1)S(1)}, bf16[64,2304]{1,0:T(8,128)(2,1)S(1)}, u32[]{:S(2)}, u32[]{:S(2)}) collective-permute-start(bf16[64,2304]{1,0:T(8,128)(2,1)S(1)} %get-tuple-element.15), channel_id=1, source_target_pairs={{0,32},{16,48},{32,64},{48,80},{64,96},{80,112},{96,0},{112,16},{1... | collective-permute-start | bytes 884744 | tf_op jit(solution)/shard_map/ppermute | solution.py:220
  68.3 12.4 %collective-permute-start.6 = (bf16[64,2304]{1,0:T(8,128)(2,1)}, bf16[64,2304]{1,0:T(8,128)(2,1)S(1)}, u32[]{:S(2)}, u32[]{:S(2)}) collective-permute-start(bf16[64,2304]{1,0:T(8,128)(2,1)} %get-tuple-element.12), channel_id=1, source_target_pairs={{0,32},{16,48},{32,64},{48,80},{64,96},{80,112},{96,0},{112,16},{1... | collective-permute-start | bytes 884744 | tf_op jit(solution)/shard_map/ppermute | solution.py:220
  68.3 12.4 %collective-permute-start.2 = (bf16[64,2304]{1,0:T(8,128)(2,1)}, bf16[64,2304]{1,0:T(8,128)(2,1)S(1)}, u32[]{:S(2)}, u32[]{:S(2)}) collective-permute-start(bf16[64,2304]{1,0:T(8,128)(2,1)} %get-tuple-element.13), channel_id=1, source_target_pairs={{0,96},{16,112},{32,0},{48,16},{64,32},{80,48},{96,64},{112,80},{1... | collective-permute-start | bytes 884744 | tf_op jit(solution)/shard_map/ppermute | solution.py:220
  80.9 6.1 %collective-permute-start.9 = (bf16[64,2304]{1,0:T(8,128)(2,1)S(1)}, bf16[64,2304]{1,0:T(8,128)(2,1)S(1)}, u32[]{:S(2)}, u32[]{:S(2)}) collective-permute-start(bf16[64,2304]{1,0:T(8,128)(2,1)S(1)} %select_convert_fusion), channel_id=1, source_target_pairs={{0,1},{1,0},{2,3},{3,2},{4,5},{5,4},{6,7},{7,6},{8,9},{9,8},{10,11... | collective-permute-start | bytes 884744 | tf_op jit(solution)/shard_map/ppermute | solution.py:224
  87.3 6.9 %collective-permute-start.11 = (bf16[64,2304]{1,0:T(8,128)(2,1)S(1)}, bf16[64,2304]{1,0:T(8,128)(2,1)S(1)}, u32[]{:S(2)}, u32[]{:S(2)}) collective-permute-start(bf16[64,2304]{1,0:T(8,128)(2,1)S(1)} %add_convert_fusion.refs_0_), channel_id=1, source_target_pairs={{0,32},{16,48},{32,64},{48,80},{64,96},{80,112},{96,0},{112,16},{1... | collective-permute-start | bytes 884744 | tf_op jit(solution)/shard_map/ppermute | solution.py:220
  87.4 11.6 %collective-permute-start.13 = (bf16[64,2304]{1,0:T(8,128)(2,1)S(1)}, bf16[64,2304]{1,0:T(8,128)(2,1)S(1)}, u32[]{:S(2)}, u32[]{:S(2)}) collective-permute-start(bf16[64,2304]{1,0:T(8,128)(2,1)S(1)} %add_convert_fusion.refs_0_), channel_id=1, source_target_pairs={{0,96},{16,112},{32,0},{48,16},{64,32},{80,48},{96,64},{112,80},{1... | collective-permute-start | bytes 884744 | tf_op jit(solution)/shard_map/ppermute | solution.py:220
  90.1 11.9 %collective-permute-start.15 = (bf16[64,2304]{1,0:T(8,128)(2,1)S(1)}, bf16[64,2304]{1,0:T(8,128)(2,1)S(1)}, u32[]{:S(2)}, u32[]{:S(2)}) collective-permute-start(bf16[64,2304]{1,0:T(8,128)(2,1)S(1)} %add_convert_fusion.refs_0_), channel_id=1, source_target_pairs={{0,1},{1,0},{2,3},{3,2},{4,5},{5,4},{6,7},{7,6},{8,9},{9,8},{10,11... | collective-permute-start | bytes 884744 | tf_op jit(solution)/shard_map/ppermute | solution.py:224
  94.2 9.3 %collective-permute-start.21 = (bf16[32,2304]{1,0:T(8,128)(2,1)S(1)}, bf16[32,2304]{1,0:T(8,128)(2,1)S(1)}, u32[]{:S(2)}, u32[]{:S(2)}) collective-permute-start(bf16[32,2304]{1,0:T(8,128)(2,1)S(1)} %slice.88), channel_id=1, source_target_pairs={{0,32},{16,48},{32,64},{48,80},{64,96},{80,112},{96,0},{112,16},{1... | collective-permute-start | bytes 442376 | tf_op jit(solution)/shard_map/ppermute | solution.py:220
  94.3 26.8 %collective-permute-start.10 = (bf16[64,2304]{1,0:T(8,128)(2,1)S(1)}, bf16[64,2304]{1,0:T(8,128)(2,1)S(1)}, u32[]{:S(2)}, u32[]{:S(2)}) collective-permute-start(bf16[64,2304]{1,0:T(8,128)(2,1)S(1)} %add_convert_fusion.refs_0_), channel_id=1, source_target_pairs={{0,16},{16,0},{32,48},{48,32},{64,80},{80,64},{96,112},{112,96},{1... | collective-permute-start | bytes 884744 | tf_op jit(solution)/shard_map/ppermute | solution.py:215
  99.1 12.7 %collective-permute-start.22 = (bf16[32,2304]{1,0:T(8,128)(2,1)S(1)}, bf16[32,2304]{1,0:T(8,128)(2,1)S(1)}, u32[]{:S(2)}, u32[]{:S(2)}) collective-permute-start(bf16[32,2304]{1,0:T(8,128)(2,1)S(1)} %slice.89), channel_id=1, source_target_pairs={{0,96},{16,112},{32,0},{48,16},{64,32},{80,48},{96,64},{112,80},{1... | collective-permute-start | bytes 442376 | tf_op jit(solution)/shard_map/ppermute | solution.py:220
  102.0 10.4 %collective-permute-start.19 = (bf16[64,2304]{1,0:T(8,128)(2,1)S(1)}, bf16[64,2304]{1,0:T(8,128)(2,1)S(1)}, u32[]{:S(2)}, u32[]{:S(2)}) collective-permute-start(bf16[64,2304]{1,0:T(8,128)(2,1)S(1)} %collective-permute-done.15.refs_6_), channel_id=1, source_target_pairs={{0,96},{16,112},{32,0},{48,16},{64,32},{80,48},{96,64},{112,80},{1... | collective-permute-start | bytes 884744 | tf_op jit(solution)/shard_map/ppermute | solution.py:220
  102.1 9.5 %collective-permute-start.17 = (bf16[64,2304]{1,0:T(8,128)(2,1)S(1)}, bf16[64,2304]{1,0:T(8,128)(2,1)S(1)}, u32[]{:S(2)}, u32[]{:S(2)}) collective-permute-start(bf16[64,2304]{1,0:T(8,128)(2,1)S(1)} %collective-permute-done.15.refs_6_), channel_id=1, source_target_pairs={{0,32},{16,48},{32,64},{48,80},{64,96},{80,112},{96,0},{112,16},{1... | collective-permute-start | bytes 884744 | tf_op jit(solution)/shard_map/ppermute | solution.py:220
  103.5 17.6 %collective-permute-start.16 = (bf16[64,2304]{1,0:T(8,128)(2,1)S(1)}, bf16[64,2304]{1,0:T(8,128)(2,1)S(1)}, u32[]{:S(2)}, u32[]{:S(2)}) collective-permute-start(bf16[64,2304]{1,0:T(8,128)(2,1)S(1)} %collective-permute-done.15.refs_6_), channel_id=1, source_target_pairs={{0,16},{16,0},{32,48},{48,32},{64,80},{80,64},{96,112},{112,96},{1... | collective-permute-start | bytes 884744 | tf_op jit(solution)/shard_map/ppermute | solution.py:215
  111.6 5.3 %collective-permute-start.23 = (bf16[32,2304]{1,0:T(8,128)(2,1)S(1)}, bf16[32,2304]{1,0:T(8,128)(2,1)S(1)}, u32[]{:S(2)}, u32[]{:S(2)}) collective-permute-start(bf16[32,2304]{1,0:T(8,128)(2,1)S(1)} %slice.90), channel_id=1, source_target_pairs={{0,32},{16,48},{32,64},{48,80},{64,96},{80,112},{96,0},{112,16},{1... | collective-permute-start | bytes 442376 | tf_op jit(solution)/shard_map/ppermute | solution.py:220
  112.4 5.2 %collective-permute-start.24 = (bf16[32,2304]{1,0:T(8,128)(2,1)S(1)}, bf16[32,2304]{1,0:T(8,128)(2,1)S(1)}, u32[]{:S(2)}, u32[]{:S(2)}) collective-permute-start(bf16[32,2304]{1,0:T(8,128)(2,1)S(1)} %slice.91), channel_id=1, source_target_pairs={{0,96},{16,112},{32,0},{48,16},{64,32},{80,48},{96,64},{112,80},{1... | collective-permute-start | bytes 442376 | tf_op jit(solution)/shard_map/ppermute | solution.py:220
  118.3 5.6 %collective-permute-start.25 = (bf16[128,2304]{1,0:T(8,128)(2,1)}, bf16[128,2304]{1,0:T(8,128)(2,1)}, u32[]{:S(2)}, u32[]{:S(2)}) collective-permute-start(bf16[128,2304]{1,0:T(8,128)(2,1)} %constant_dynamic-update-slice_fusion.refs_12_), channel_id=1, source_target_pairs={{0,16},{16,0},{32,48},{48,32},{64,80},{80,64},{96,112},{112,96},{1... | collective-permute-start | bytes 1769480 | tf_op jit(solution)/shard_map/ppermute | solution.py:215
  120.5 1.9 %collective-permute-start.14 = (bf16[64,2304]{1,0:T(8,128)(2,1)S(1)}, bf16[64,2304]{1,0:T(8,128)(2,1)S(1)}, u32[]{:S(2)}, u32[]{:S(2)}) collective-permute-start(bf16[64,2304]{1,0:T(8,128)(2,1)S(1)} %collective-permute-done.13.refs_4_), channel_id=1, source_target_pairs={{0,16},{16,0},{32,48},{48,32},{64,80},{80,64},{96,112},{112,96},{1... | collective-permute-start | bytes 884744 | tf_op jit(solution)/shard_map/ppermute | solution.py:215
  120.5 2.5 %collective-permute-start.12 = (bf16[64,2304]{1,0:T(8,128)(2,1)S(1)}, bf16[64,2304]{1,0:T(8,128)(2,1)S(1)}, u32[]{:S(2)}, u32[]{:S(2)}) collective-permute-start(bf16[64,2304]{1,0:T(8,128)(2,1)S(1)} %collective-permute-done.11.refs_2_), channel_id=1, source_target_pairs={{0,16},{16,0},{32,48},{48,32},{64,80},{80,64},{96,112},{112,96},{1... | collective-permute-start | bytes 884744 | tf_op jit(solution)/shard_map/ppermute | solution.py:215
  121.0 2.4 %collective-permute-start.20 = (bf16[64,2304]{1,0:T(8,128)(2,1)S(1)}, bf16[64,2304]{1,0:T(8,128)(2,1)S(1)}, u32[]{:S(2)}, u32[]{:S(2)}) collective-permute-start(bf16[64,2304]{1,0:T(8,128)(2,1)S(1)} %collective-permute-done.19.refs_10_), channel_id=1, source_target_pairs={{0,16},{16,0},{32,48},{48,32},{64,80},{80,64},{96,112},{112,96},{1... | collective-permute-start | bytes 884744 | tf_op jit(solution)/shard_map/ppermute | solution.py:215
  121.1 2.8 %collective-permute-start.18 = (bf16[64,2304]{1,0:T(8,128)(2,1)S(1)}, bf16[64,2304]{1,0:T(8,128)(2,1)S(1)}, u32[]{:S(2)}, u32[]{:S(2)}) collective-permute-start(bf16[64,2304]{1,0:T(8,128)(2,1)S(1)} %collective-permute-done.17.refs_8_), channel_id=1, source_target_pairs={{0,16},{16,0},{32,48},{48,32},{64,80},{80,64},{96,112},{112,96},{1... | collective-permute-start | bytes 884744 | tf_op jit(solution)/shard_map/ppermute | solution.py:215
  141.8 33.1 %all-to-all-start.1 = ((bf16[16,448,128]{2,1,0:T(8,128)(2,1)}), bf16[16,448,128]{2,1,0:T(8,128)(2,1)S(1)}, u32[]{:S(2)}, u32[]{:S(2)}) async-start(bf16[16,448,128]{2,1,0:T(8,128)(2,1)} %shard_map.45), calls=%async_computation.1 | async-start | bytes 3670016 | tf_op jit(solution)/shard_map/all_to_all | solution.py:280

commit v3 on v2

v3 whole, which is shorter than its diff:
```python
import functools
import math

import jax
import jax.numpy as jnp
from jax import lax
from jax.experimental import pallas as pl
from jax.experimental.pallas import tpu as pltpu
from jax.sharding import PartitionSpec as P

EXPERTS, ROWS, COLS = 8, 2048, 7168
CORES, RING, PAIR = 2, 4, 2
MEMBERS = 16
LANES = ROWS // MEMBERS
WIDE = COLS // 8
HALF = WIDE // 2
BLOCK = 256
TILES = ROWS // LANES
PIECE = LANES
FOLD = (TILES + 1) * LANES
HALVES = PIECE // PAIR
QUARTER = HALVES // PAIR

momentum_rate = 0.95
first_coef = 3.4445
second_coef = -4.775
third_coef = 2.0315
epsilon_value = 1e-06
f32, bf16 = jnp.float32, jnp.bfloat16
PARAMS = pltpu.CompilerParams(vmem_limit_bytes=50 * 1024 * 1024)
ALL_VMEM = pltpu.CompilerParams(vmem_limit_bytes=60 * 1024 * 1024)
WHOLE = pl.BlockSpec(memory_space=pltpu.VMEM)
ANYWHERE = pl.BlockSpec(memory_space=pl.ANY)
SCALARS = pl.BlockSpec(memory_space=pltpu.SMEM)


def blend_kernel(momentum_ref, gradient_ref, out_ref, momentum, gradient, blended, sems):
    copies = []
    for expert in range(EXPERTS):
        copies.append(pltpu.make_async_copy(momentum_ref.at[expert], momentum.at[expert], sems.at[0, expert]))
        copies.append(pltpu.make_async_copy(gradient_ref.at[expert], gradient.at[expert], sems.at[1, expert]))
    for copy in copies:
        copy.start()
    out_copies = []
    for expert in range(EXPERTS):
        copies[2 * expert].wait()
        copies[2 * expert + 1].wait()
        values = gradient[expert].astype(f32)
        new = momentum_rate * momentum[expert] + values
        blended[expert] = (values + momentum_rate * new).astype(bf16).T
        out_copies.append(pltpu.make_async_copy(blended.at[expert], out_ref.at[expert], sems.at[2, expert]))
        out_copies[-1].start()
    for copy in out_copies:
        copy.wait()


def blend(momentum, gradient):
    return pl.pallas_call(
        blend_kernel,
        in_specs=[ANYWHERE, ANYWHERE],
        out_specs=ANYWHERE,
        out_shape=jax.ShapeDtypeStruct((EXPERTS, WIDE, LANES), bf16),
        scratch_shapes=[
            pltpu.VMEM((EXPERTS, LANES, WIDE), f32),
            pltpu.VMEM((EXPERTS, LANES, WIDE), bf16),
            pltpu.VMEM((EXPERTS, WIDE, LANES), bf16),
            pltpu.SemaphoreType.DMA((3, EXPERTS)),
        ],
        compiler_params=ALL_VMEM,
    )(momentum, gradient)


def gram_kernel(where_ref, columns_ref, ring_ref, give_ref, keep_ref):
    half, side = where_ref[0], where_ref[1]
    for slot in range(RING):
        row = RING * half + where_ref[2 + slot]
        odd = row % 2
        count = (TILES - row) // 2
        top, low = columns_ref[row].T, columns_ref[TILES - 1 - row].T

        def put(left, right, at):
            values = jnp.dot(left, right, preferred_element_type=f32).astype(bf16)
            upper, lower = values[HALVES : HALVES + QUARTER], values[HALVES + QUARTER :]
            at = pl.ds(pl.multiple_of(at * LANES, LANES), values.shape[1])
            ring_ref[slot, :, at] = values[:HALVES]
            give_ref[slot, :, at] = jnp.where(side == 0, lower, upper)
            keep_ref[slot, :, at] = jnp.where(side == 0, upper, lower)

        on_top = odd == 1
        put(jnp.where(on_top, top, low), columns_ref[jnp.where(on_top, row, TILES - 1 - row)], jnp.where(on_top, 0, TILES - row))
        for block in range(TILES // 2):
            upper = block < count
            over = TILES - row - odd + 2 * (block - count)
            column = jnp.where(upper, row + odd + 2 * block, over)
            left = top if block < RING else jnp.where(upper, top, low)
            right = jnp.concatenate([columns_ref[column], columns_ref[column + 1]], axis=1)
            put(left, right, jnp.where(upper, odd + 2 * block, over + 1))


def gram_pieces(columns, half, side, pieces):
    where = jnp.stack([half, side, *pieces]).astype(jnp.int32)
    shapes = [(RING, HALVES, FOLD), (RING, QUARTER, FOLD), (RING, QUARTER, FOLD)]
    return pl.pallas_call(
        gram_kernel,
        in_specs=[SCALARS, WHOLE],
        out_specs=[WHOLE] * 3,
        out_shape=[jax.ShapeDtypeStruct(shape, bf16) for shape in shapes],
        compiler_params=PARAMS,
        cost_estimate=pl.CostEstimate(flops=16 * PIECE * FOLD * 512, bytes_accessed=8_000_000, transcendentals=0),
    )(where, columns)


def merge_kernel(where_ref, *refs):
    piece_refs, out_ref = refs[:-1], refs[-1]
    for n, piece_ref in enumerate(piece_refs):
        at = pl.ds(pl.multiple_of(where_ref[n], QUARTER), QUARTER)
        out_ref[at, :] = piece_ref[...]


def merge(pieces, offsets):
    count = len(pieces)
    return pl.pallas_call(
        merge_kernel,
        in_specs=[SCALARS] + [WHOLE] * count,
        out_specs=WHOLE,
        out_shape=jax.ShapeDtypeStruct((count * QUARTER, FOLD), bf16),
        compiler_params=PARAMS,
    )(jnp.stack([jnp.int32(offset) for offset in offsets]), *pieces)


STEP = 16


def step_kernel(layout, where_ref, columns_ref, *refs):
    count = 1 + max(array for array, _, _ in layout)
    piece_refs, out_ref, scratch = refs[:count], refs[count], refs[count + 1 :]
    parts, staged, gram, blended, mixed, product, image, out_sems = scratch
    for n, (array, start, rows) in enumerate(layout):
        at = pl.ds(pl.multiple_of(where_ref[2 * n + 1], QUARTER), rows)
        parts[where_ref[2 * n], at, :] = piece_refs[array][start : start + rows, :]
    for folded in range(TILES // 2):
        for row, start in ((folded, 0), (TILES - 1 - folded, TILES - folded)):
            at = slice(row * LANES, (row + 1) * LANES)
            gram[at, row * LANES :] = parts[folded, :, start * LANES : (start + TILES - row) * LANES]
            for column in range(row + 1, TILES, 2):
                wide = min(2, TILES - column) * LANES
                begin = (start + column - row) * LANES
                gram[column * LANES : column * LANES + wide, at] = parts[folded, :, begin : begin + wide].T
    for member in range(MEMBERS):
        blended[:, member * LANES : (member + 1) * LANES] = columns_ref[member]

    def image_of(weights, blocks):
        total = jnp.zeros((8, ROWS), f32)
        for step in range(ROWS // STEP):
            if step % 16 == 0 and step // 16 < len(blocks):
                at = slice(blocks[step // 16] * BLOCK, (blocks[step // 16] + 1) * BLOCK)
                product[:, at] = jnp.dot(blended[...], gram[:, at], preferred_element_type=f32)
            at = slice(step * STEP, (step + 1) * STEP)
            values = gram[at, :].astype(f32)
            if weights is not None:
                values = values * weights[at, :]
            total = total + (values[:8] + values[8:])
        return jnp.sum(total, axis=0, keepdims=True)

    def length_of(values):
        return jnp.sqrt(jnp.sum(values * values) + epsilon_value)

    def stand(values):
        for member in range(MEMBERS):
            at = slice(member * LANES, (member + 1) * LANES)
            image[at, :] = jnp.broadcast_to(values[:, at], (8, LANES)).T[:, :1]

    values = image_of(None, (0, 1))
    stand(values / length_of(values))
    values = image_of(image, (2, 3, 4))
    stand(values / length_of(values))
    values = image_of(image, (5, 6, 7))
    scale = lax.rsqrt(jnp.full((1, 1), length_of(values) + epsilon_value, f32))
    square = scale * scale

    for block in range(8):
        at = slice(block * BLOCK, (block + 1) * BLOCK)
        mixed[:, at] = (second_coef * blended[:, at].astype(f32) + (third_coef * square) * product[:, at]).astype(bf16)
    out_copies = []
    for block in range(8):
        at = slice(block * BLOCK, (block + 1) * BLOCK)
        last = jnp.dot(mixed[...], gram[:, at], preferred_element_type=f32)
        update = (math.sqrt(COLS) * scale) * (first_coef * blended[:, at].astype(f32) + square * last)
        update = update.astype(bf16)
        staged[2 * block] = update[:, :LANES]
        staged[2 * block + 1] = update[:, LANES:]
        at = pl.ds(2 * block, 2)
        out_copies.append(pltpu.make_async_copy(staged.at[at], out_ref.at[at], out_sems.at[block]))
        out_copies[-1].start()
    for copy in out_copies:
        copy.wait()


def newton_step(columns, pieces, layout, where):
    matrix = (MEMBERS, HALF, LANES)
    return pl.pallas_call(
        functools.partial(step_kernel, layout),
        in_specs=[SCALARS, WHOLE] + [WHOLE] * len(pieces),
        out_specs=ANYWHERE,
        out_shape=jax.ShapeDtypeStruct(matrix, bf16),
        scratch_shapes=[
            pltpu.VMEM((CORES * RING, PIECE, FOLD), bf16),
            pltpu.VMEM(matrix, bf16),
            pltpu.VMEM((ROWS, ROWS), bf16),
            pltpu.VMEM((HALF, ROWS), bf16),
            pltpu.VMEM((HALF, ROWS), bf16),
            pltpu.VMEM((HALF, ROWS), f32),
            pltpu.VMEM((ROWS, 1), f32),
            pltpu.SemaphoreType.DMA((8,)),
        ],
        compiler_params=PARAMS,
        cost_estimate=pl.CostEstimate(flops=4 * ROWS * ROWS * HALF, bytes_accessed=8_000_000, transcendentals=0),
    )(where, columns, *pieces)


def spread_kernel(update_ref, out_ref, turned, sems):
    out_copies = []
    for expert in range(EXPERTS):
        turned[expert] = update_ref[expert].T
        out_copies.append(pltpu.make_async_copy(turned.at[expert], out_ref.at[expert], sems.at[expert]))
        out_copies[-1].start()
    for copy in out_copies:
        copy.wait()


def spread(update):
    return pl.pallas_call(
        spread_kernel,
        in_specs=[WHOLE],
        out_specs=ANYWHERE,
        out_shape=jax.ShapeDtypeStruct((EXPERTS, LANES, WIDE), bf16),
        scratch_shapes=[pltpu.VMEM((EXPERTS, LANES, WIDE), bf16), pltpu.SemaphoreType.DMA((EXPERTS,))],
        compiler_params=PARAMS,
    )(update)


def total_of(*terms):
    total = terms[0].astype(f32)
    for term in terms[1:]:
        total = total + term.astype(f32)
    return total


def add(*terms):
    return total_of(*terms).astype(bf16)


def swap_cores(values):
    return lax.ppermute(values, "fsdp", [(i, i ^ 1) for i in range(CORES * RING)])


def shift(values, distance):
    size = CORES * RING
    return lax.ppermute(values, "fsdp", [(i, (i + CORES * distance) % size) for i in range(size)])


def swap_pair(values):
    return lax.ppermute(values, "mat", [(i, i ^ 1) for i in range(MEMBERS)])


def shards(momentum, gradient):
    index = lax.axis_index("fsdp")
    core, place_y = index % CORES, index // CORES
    side = lax.axis_index("mat") % PAIR
    blended = blend(momentum, gradient)
    columns = lax.all_to_all(blended.reshape(MEMBERS, HALF, LANES), "mat", 0, 0)
    new_momentum = momentum_rate * momentum + gradient.astype(f32)

    far, ahead, behind = [(place_y + distance) % RING for distance in (2, 1, 3)]
    wanted = [far, ahead, behind, place_y]
    away = gram_pieces(columns, 1 - core, side, wanted)
    kept_ring, kept_give, kept_keep = gram_pieces(columns, core, side, wanted)
    got_give, got_ring, got_keep = swap_cores(away[1]), swap_cores(away[0]), swap_cores(away[2])

    def round_ring(pieces):
        return [shift(values, distance) for values, distance in zip(pieces, (2, 1, 3))]

    ring_sums = [add(kept_ring[slot], got_ring[slot]) for slot in range(3)]
    partner = swap_pair(add(kept_give, got_give))
    *arrived, partner = lax.optimization_barrier((*round_ring(ring_sums), partner))
    ring_total = total_of(kept_ring[3], got_ring[3], *arrived)
    upper, lower = ring_total[:QUARTER], ring_total[QUARTER:]
    partner_sums = [add(kept_keep[slot], got_keep[slot], partner[slot]) for slot in range(3)]
    upper_got = swap_pair(jnp.where(side == 0, lower, upper).astype(bf16))
    *arrived, upper_got = lax.optimization_barrier((*round_ring(partner_sums), upper_got))
    first = add(jnp.where(side == 0, upper, lower), upper_got)
    second = add(kept_keep[3], got_keep[3], partner[3], *arrived)

    first_other = swap_pair(first)
    *arrived, first_other = lax.optimization_barrier((*round_ring([second] * 3), first_other))
    first = merge((first, first_other), (side * QUARTER, (1 - side) * QUARTER))
    second = merge((second, *arrived), range(0, PIECE, QUARTER))
    second_other = swap_pair(second)
    pieces, layout, where = [], [], []

    def take(array, rows, chunks, offset):
        for values, half in ((array, core), (swap_cores(array), 1 - core)):
            for n, chunk in enumerate(chunks):
                layout.append((len(pieces), n * rows, rows))
                where.extend([half * RING + chunk, offset])
            pieces.append(values)

    order = [place_y, far, behind, ahead]
    take(first, HALVES, order[:1], 0)
    take(second, QUARTER, order, HALVES + side * QUARTER)
    for values, chunk in zip(round_ring([first] * 3), order[1:]):
        take(values, HALVES, [chunk], 0)
    take(second_other, QUARTER, order, HALVES + (1 - side) * QUARTER)

    update = newton_step(columns, pieces, tuple(layout), jnp.stack(where).astype(jnp.int32))
    returned = lax.all_to_all(update, "mat", 0, 0)
    return new_momentum, spread(returned.reshape(EXPERTS, WIDE, LANES))


def solution(mesh):
    spec = P(None, "mat", "fsdp")
    return jax.shard_map(shards, mesh=mesh, in_specs=(spec, spec), out_specs=(spec, spec), check_vma=False)
```

time: 179 us -> 163 us (0.911)
  waiting for transfers between devices: 88.4 us -> 74.2 us
  starting transfers between devices: 42.4 us -> 48.6 us
  Pallas kernels: 33.3 us -> 27.2 us
  local copies, waits for them, and re-layouts: 4.43 us -> 1.11 us
  other arithmetic: 8.71 us -> 10.9 us
    ppermute x14 -> x12, waiting for transfers between devices: 29.2 us -> 15.8 us  [shift(): lax.ppermute(values, 'fsdp', [(i, (i + CORES * distance) % size) for i in...]
    ppermute x10 -> x9, starting transfers between devices: 12.9 us -> 18.9 us  [swap_cores(): lax.ppermute(values, 'fsdp', [(i, i ^ 1) for i in range(CORES * RING)])]
    pallas_call x5 -> x6, Pallas kernels: 15.4 us -> 11.7 us  [the longest x2 5.23 us: gram_pieces(): pl.pallas_call(gram_kernel, in_specs=[SCALARS, WHOLE], out_specs=[WHOLE]...]
    unnamed x7 -> x8, local copies, waits for them, and re-layouts: 3.51 us -> 0.82 us
    pallas_call x1, Pallas kernels: 17.9 us -> 15.4 us  [newton_step(): pl.pallas_call(functools.partial(step_kernel, layout), in_specs=[SCALARS,...]
    ppermute x2 -> x4, starting transfers between devices: 0.37 us -> 2.81 us  [swap_pair(): return lax.ppermute(values, 'mat', [(i, i ^ 1) for i in range(MEMBERS)])]
    ppermute x14 -> x12, starting transfers between devices: 17 us -> 14.7 us  [shift(): lax.ppermute(values, 'fsdp', [(i, (i + CORES * distance) % size) for i in...]
    convert_element_type x4 -> x5, other arithmetic: 3.4 us -> 4.6 us  [add(): return total_of(*terms).astype(bf16)]
  transfers between devices with their start and end apart: 28 -> 27, of which waited for: 15 -> 12; matrix products, arithmetic and copies ran while one was open for 6% -> 7% of each run, Pallas kernels for 3% -> 2%
where the time goes in v3:
time: 163 us
  waiting for transfers between devices  74.2 us (46%)
  starting transfers between devices  48.6 us (30%)
  Pallas kernels  27.2 us (17%)
  other arithmetic  10.9 us (7%)
    all_to_all x1, waiting for transfers between devices, shards(): columns = lax.all_to_all(blended.reshape(MEMBERS, HALF, LANES), 'mat', 0, 0)  26.6 us
    all_to_all x1, waiting for transfers between devices, shards(): returned = lax.all_to_all(update, 'mat', 0, 0)  24.5 us
    ppermute x9, starting transfers between devices, swap_cores(): lax.ppermute(values, 'fsdp', [(i, i ^ 1) for i in range(CORES * RING)])  18.9 us
    ppermute x12, waiting for transfers between devices, shift(): lax.ppermute(values, 'fsdp', [(i, (i + CORES * distance) % size) for i in...  15.8 us
    pallas_call x1, Pallas kernels, newton_step(): pl.pallas_call(functools.partial(step_kernel, layout), in_specs=[SCALARS,...  15.4 us
    ppermute x12, starting transfers between devices, shift(): lax.ppermute(values, 'fsdp', [(i, (i + CORES * distance) % size) for i in...  14.7 us
    all_to_all x1, starting transfers between devices, shards(): columns = lax.all_to_all(blended.reshape(MEMBERS, HALF, LANES), 'mat', 0, 0)  8.44 us
    ppermute x4, waiting for transfers between devices, swap_pair(): return lax.ppermute(values, 'mat', [(i, i ^ 1) for i in range(MEMBERS)])  5.88 us
  transfers between devices with their start and end apart: 27, of which 12 were waited for; matrix products, arithmetic and copies ran while one was open for 7% of the time, Pallas kernels for 2%

profile of v3, /device:TPU:1, one launch (start us, length us, event | category | flops | bytes accessed | tf_op | source)
XLA Modules:
  0.0 163.0 jit_solution(6526824812800478127)
XLA Ops:
  0.6 3.9 %shard_map.41 = bf16[8,896,128]{2,1,0:T(8,128)(2,1)} custom-call(f32[8,128,896]{2,1,0:T(8,128)} %momentum_ref.1, bf16[8,128,896]{2,1,0:T(8,128)(2,1)} %gradient_ref.1), custom_call_target="tpu_custom_call" | custom-call | tf_op jit(solution)/shard_map/pallas_call | solution.py:58
  4.6 8.4 %all-to-all-start = ((bf16[16,448,128]{2,1,0:T(8,128)(2,1)}), bf16[16,448,128]{2,1,0:T(8,128)(2,1)S(1)}, u32[]{:S(2)}, u32[]{:S(2)}) async-start(bf16[16,448,128]{2,1,0:T(8,128)(2,1)} %bitcast.48), calls=%async_computation | async-start | bytes 3670016 | tf_op jit(solution)/shard_map/all_to_all | solution.py:271
  13.1 0.1 stack.126.where_ref
  13.2 26.6 %all-to-all-done.columns_ref = bf16[16,448,128]{2,1,0:T(8,128)(2,1)S(1)} async-done(((bf16[16,448,128]{2,1,0:T(8,128)(2,1)}), bf16[16,448,128]{2,1,0:T(8,128)(2,1)S(1)}, u32[]{:S(2)}, u32[]{:S(2)}) %all-to-all-start) | async-done | bytes 1835040 | tf_op jit(solution)/shard_map/all_to_all | solution.py:271
  39.8 3.2 %shard_map.43 = (bf16[4,64,2176]{2,1,0:T(8,128)(2,1)}, bf16[4,32,2176]{2,1,0:T(8,128)(2,1)}, bf16[4,32,2176]{2,1,0:T(8,128)(2,1)S(1)}) custom-call(s32[6]{0:T(128)S(1)} %stack.126.where_ref, bf16[16,448,128]{2,1,0:T(8,128)(2,1)S(1)} %all-to-all-done.columns_ref), custom_call_target="tpu_custom_call" | custom-call | flops 2281701376 | bytes 8000000 | tf_op jit(solution)/shard_map/pallas_call | solution.py:103
  43.0 0.8 copy-done.1
  43.8 2.1 %collective-permute-start.4 = (bf16[4,32,2176]{2,1,0:T(8,128)(2,1)}, bf16[4,32,2176]{2,1,0:T(8,128)(2,1)}, u32[]{:S(2)}, u32[]{:S(2)}) collective-permute-start(bf16[4,32,2176]{2,1,0:T(8,128)(2,1)} %get-tuple-element.23), channel_id=1, source_target_pairs={{0,16},{16,0},{32,48},{48,32},{64,80},{80,64},{96,112},{112,96},{1... | collective-permute-start | bytes 1671176 | tf_op jit(solution)/shard_map/ppermute | solution.py:254
  45.9 0.0 collective-permute-start
  45.9 0.1 stack.124.where_ref
  46.0 2.0 %shard_map.42 = (bf16[4,64,2176]{2,1,0:T(8,128)(2,1)S(1)}, bf16[4,32,2176]{2,1,0:T(8,128)(2,1)S(1)}, bf16[4,32,2176]{2,1,0:T(8,128)(2,1)S(1)}) custom-call(s32[6]{0:T(128)S(1)} %stack.124.where_ref, bf16[16,448,128]{2,1,0:T(8,128)(2,1)S(1)} %all-to-all-done.columns_ref), custom_call_target="tpu_custom_call" | custom-call | flops 2281701376 | bytes 8000000 | tf_op jit(solution)/shard_map/pallas_call | solution.py:103
  48.0 0.0 collective-permute-done.4
  48.0 1.2 add_convert_fusion
  49.3 0.1 collective-permute-start.5
  49.4 0.0 collective-permute-done
  49.4 2.1 %fusion.4 = (bf16[64,2176]{1,0:T(8,128)(2,1)}, bf16[64,2176]{1,0:T(8,128)(2,1)}, bf16[64,2176]{1,0:T(8,128)(2,1)}) fusion(bf16[4,64,2176]{2,1,0:T(8,128)(2,1)} %collective-permute-done, bf16[4,64,2176]{2,1,0:T(8,128)(2,1)S(1)} %get-tuple-element.20), kind=kLoop, calls=%fused_computation.10 | loop fusion | flops 1671168 | bytes 2506752 | tf_op jit(solution)/shard_map/convert_element_type | solution.py:250
  51.6 2.7 %collective-permute-start.3 = (bf16[64,2176]{1,0:T(8,128)(2,1)}, bf16[64,2176]{1,0:T(8,128)(2,1)}, u32[]{:S(2)}, u32[]{:S(2)}) collective-permute-start(bf16[64,2176]{1,0:T(8,128)(2,1)} %get-tuple-element.38), channel_id=1, source_target_pairs={{0,96},{16,112},{32,0},{48,16},{64,32},{80,48},{96,64},{112,80},{1... | collective-permute-start | bytes 835592 | tf_op jit(solution)/shard_map/ppermute | solution.py:259
  54.3 0.0 collective-permute-start.2
  54.3 1.6 %collective-permute-start.1 = (bf16[64,2176]{1,0:T(8,128)(2,1)}, bf16[64,2176]{1,0:T(8,128)(2,1)}, u32[]{:S(2)}, u32[]{:S(2)}) collective-permute-start(bf16[64,2176]{1,0:T(8,128)(2,1)} %get-tuple-element.40), channel_id=1, source_target_pairs={{0,64},{16,80},{32,96},{48,112},{64,0},{80,16},{96,32},{112,48},{1... | collective-permute-start | bytes 835592 | tf_op jit(solution)/shard_map/ppermute | solution.py:259
  55.9 1.3 collective-permute-start.6
  57.3 5.9 %collective-permute-done.5 = bf16[4,32,2176]{2,1,0:T(8,128)(2,1)S(1)} collective-permute-done((bf16[4,32,2176]{2,1,0:T(8,128)(2,1)S(1)}, bf16[4,32,2176]{2,1,0:T(8,128)(2,1)S(1)}, u32[]{:S(2)}, u32[]{:S(2)}) %collective-permute-start.5) | collective-permute-done | bytes 557088 | tf_op jit(solution)/shard_map/ppermute | solution.py:263
  63.2 2.8 %collective-permute-done.3 = bf16[64,2176]{1,0:T(8,128)(2,1)} collective-permute-done((bf16[64,2176]{1,0:T(8,128)(2,1)}, bf16[64,2176]{1,0:T(8,128)(2,1)}, u32[]{:S(2)}, u32[]{:S(2)}) %collective-permute-start.3) | collective-permute-done | bytes 278560 | tf_op jit(solution)/shard_map/ppermute | solution.py:259
  66.0 0.0 collective-permute-done.2
  66.0 2.2 %collective-permute-done.1 = bf16[64,2176]{1,0:T(8,128)(2,1)} collective-permute-done((bf16[64,2176]{1,0:T(8,128)(2,1)}, bf16[64,2176]{1,0:T(8,128)(2,1)}, u32[]{:S(2)}, u32[]{:S(2)}) %collective-permute-start.1) | collective-permute-done | bytes 278560 | tf_op jit(solution)/shard_map/ppermute | solution.py:259
  68.2 1.4 fusion.1
  69.6 1.2 collective-permute-start.10
  70.8 0.0 collective-permute-done.6
  70.8 0.2 fusion.10
  71.0 1.4 collective-permute-start.9
  72.4 0.2 collective-permute-start.8
  72.5 1.6 collective-permute-start.7
  74.1 0.0 collective-permute-done.10
  74.1 0.8 collective-permute-done.9
  75.0 4.5 %collective-permute-done.8 = bf16[32,2176]{1,0:T(8,128)(2,1)S(1)} collective-permute-done((bf16[32,2176]{1,0:T(8,128)(2,1)S(1)}, bf16[32,2176]{1,0:T(8,128)(2,1)S(1)}, u32[]{:S(2)}, u32[]{:S(2)}) %collective-permute-start.8) | collective-permute-done | bytes 139296 | tf_op jit(solution)/shard_map/ppermute | solution.py:259
  79.5 0.0 collective-permute-done.7
  79.5 0.7 collective-permute-start.14
  80.2 1.0 fusion.7.refs_0_
  81.2 2.0 %collective-permute-start.13 = (bf16[32,2176]{1,0:T(8,128)(2,1)S(1)}, bf16[32,2176]{1,0:T(8,128)(2,1)S(1)}, u32[]{:S(2)}, u32[]{:S(2)}) collective-permute-start(bf16[32,2176]{1,0:T(8,128)(2,1)S(1)} %fusion.7.refs_0_), channel_id=1, source_target_pairs={{0,96},{16,112},{32,0},{48,16},{64,32},{80,48},{96,64},{112,80},{1... | collective-permute-start | bytes 417800 | tf_op jit(solution)/shard_map/ppermute | solution.py:259
  83.2 0.0 collective-permute-start.12
  83.2 1.3 collective-permute-start.11
  84.5 0.0 collective-permute-done.14.refs_1_
  84.5 0.8 collective-permute-done.13.refs_3_
  85.3 4.6 %collective-permute-done.12.refs_2_ = bf16[32,2176]{1,0:T(8,128)(2,1)S(1)} collective-permute-done((bf16[32,2176]{1,0:T(8,128)(2,1)S(1)}, bf16[32,2176]{1,0:T(8,128)(2,1)S(1)}, u32[]{:S(2)}, u32[]{:S(2)}) %collective-permute-start.12) | collective-permute-done | bytes 139296 | tf_op jit(solution)/shard_map/ppermute | solution.py:259
  89.8 0.0 collective-permute-done.11.refs_1_
  89.8 0.6 shard_map.45.refs_2_
  90.4 0.9 collective-permute-start.23
  91.3 0.1 pad_add_fusion.where_ref
  91.4 0.6 shard_map.44.refs_0_
  92.0 2.6 %collective-permute-start.21 = (bf16[64,2176]{1,0:T(8,128)(2,1)S(1)}, bf16[64,2176]{1,0:T(8,128)(2,1)S(1)}, u32[]{:S(2)}, u32[]{:S(2)}) collective-permute-start(bf16[64,2176]{1,0:T(8,128)(2,1)S(1)} %shard_map.44.refs_0_), channel_id=1, source_target_pairs={{0,96},{16,112},{32,0},{48,16},{64,32},{80,48},{96,64},{112,80},{1... | collective-permute-start | bytes 835592 | tf_op jit(solution)/shard_map/ppermute | solution.py:259
  94.6 1.3 collective-permute-start.17
  95.8 4.5 %collective-permute-start.15 = (bf16[64,2176]{1,0:T(8,128)(2,1)S(1)}, bf16[64,2176]{1,0:T(8,128)(2,1)S(1)}, u32[]{:S(2)}, u32[]{:S(2)}) collective-permute-start(bf16[64,2176]{1,0:T(8,128)(2,1)S(1)} %shard_map.44.refs_0_), channel_id=1, source_target_pairs={{0,16},{16,0},{32,48},{48,32},{64,80},{80,64},{96,112},{112,96},{1... | collective-permute-start | bytes 835592 | tf_op jit(solution)/shard_map/ppermute | solution.py:254
  100.4 7.4 %collective-permute-start.16 = (bf16[128,2176]{1,0:T(8,128)(2,1)S(1)}, bf16[128,2176]{1,0:T(8,128)(2,1)S(1)}, u32[]{:S(2)}, u32[]{:S(2)}) collective-permute-start(bf16[128,2176]{1,0:T(8,128)(2,1)S(1)} %shard_map.45.refs_2_), channel_id=1, source_target_pairs={{0,16},{16,0},{32,48},{48,32},{64,80},{80,64},{96,112},{112,96},{1... | collective-permute-start | bytes 1671176 | tf_op jit(solution)/shard_map/ppermute | solution.py:254
  107.7 0.0 collective-permute-start.24
  107.7 3.1 %collective-permute-start.22 = (bf16[64,2176]{1,0:T(8,128)(2,1)S(1)}, bf16[64,2176]{1,0:T(8,128)(2,1)}, u32[]{:S(2)}, u32[]{:S(2)}) collective-permute-start(bf16[64,2176]{1,0:T(8,128)(2,1)S(1)} %collective-permute-done.21.refs_8_), channel_id=1, source_target_pairs={{0,16},{16,0},{32,48},{48,32},{64,80},{80,64},{96,112},{112,96},{1... | collective-permute-start | bytes 835592 | tf_op jit(solution)/shard_map/ppermute | solution.py:254
  110.8 0.0 collective-permute-start.20
  110.8 0.5 collective-permute-start.18
  111.4 0.1 stack.56.where_ref
  111.5 0.7 collective-permute-done.22.refs_9_
  112.1 0.4 collective-permute-done.20.refs_7_
  112.5 0.4 collective-permute-done.18.refs_5_
  113.0 15.4 %shard_map.46 = bf16[16,448,128]{2,1,0:T(8,128)(2,1)} custom-call(s32[48]{0:T(128)S(1)} %stack.56.where_ref, bf16[16,448,128]{2,1,0:T(8,128)(2,1)} %copy-done, bf16[64,2176]{1,0:T(8,128)(2,1)S(1)} %shard_map.44.refs_0_, bf16[64,2176]{1,0:T(8,128)(2,1)S(1)} %collective-permute-done.15.refs_1_, bf16[128,2176]{1,0:T(8,128)(2,1)S(1)} %shard_map.45.refs_2_, ...), custom_call_target="tpu_custom_call" | custom-call | flops 7516192768 | bytes 8000000 | tf_op jit(solution)/shard_map/pallas_call | solution.py:201
  128.4 3.7 %all-to-all-start.1 = ((bf16[16,448,128]{2,1,0:T(8,128)(2,1)}), bf16[16,448,128]{2,1,0:T(8,128)(2,1)S(1)}, u32[]{:S(2)}, u32[]{:S(2)}) async-start(bf16[16,448,128]{2,1,0:T(8,128)(2,1)} %shard_map.46), calls=%async_computation.1 | async-start | bytes 3670016 | tf_op jit(solution)/shard_map/all_to_all | solution.py:316
  132.1 4.9 %convert_add_fusion = f32[8,128,896]{2,1,0:T(8,128)} fusion(bf16[8,128,896]{2,1,0:T(8,128)(2,1)} %gradient_ref.1, f32[8,128,896]{2,1,0:T(8,128)} %momentum_ref.1), kind=kLoop, calls=%fused_computation | loop fusion | flops 2752512 | bytes 9175040 | tf_op jit(solution)/shard_map/add | solution.py:272
  137.0 24.5 %all-to-all-done.1 = bf16[16,448,128]{2,1,0:T(8,128)(2,1)S(1)} async-done(((bf16[16,448,128]{2,1,0:T(8,128)(2,1)}), bf16[16,448,128]{2,1,0:T(8,128)(2,1)S(1)}, u32[]{:S(2)}, u32[]{:S(2)}) %all-to-all-start.1) | async-done | bytes 1835040 | tf_op jit(solution)/shard_map/all_to_all | solution.py:316
  161.5 1.4 shard_map.47
  (18 shorter events, 0.1 us)
Async XLA Ops:
  4.6 35.2 %all-to-all-start = ((bf16[16,448,128]{2,1,0:T(8,128)(2,1)}), bf16[16,448,128]{2,1,0:T(8,128)(2,1)S(1)}, u32[]{:S(2)}, u32[]{:S(2)}) async-start(bf16[16,448,128]{2,1,0:T(8,128)(2,1)} %bitcast.48), calls=%async_computation | async-start | bytes 3670016 | tf_op jit(solution)/shard_map/all_to_all | solution.py:271
  39.8 6.2 %copy-start = (bf16[16,448,128]{2,1,0:T(8,128)(2,1)}, bf16[16,448,128]{2,1,0:T(8,128)(2,1)S(1)}, u32[]{:S(2)}) copy-start(bf16[16,448,128]{2,1,0:T(8,128)(2,1)S(1)} %all-to-all-done.columns_ref) | copy-start | bytes 5505028
  43.0 0.8 copy-start.1
  43.8 4.3 %collective-permute-start.4 = (bf16[4,32,2176]{2,1,0:T(8,128)(2,1)}, bf16[4,32,2176]{2,1,0:T(8,128)(2,1)}, u32[]{:S(2)}, u32[]{:S(2)}) collective-permute-start(bf16[4,32,2176]{2,1,0:T(8,128)(2,1)} %get-tuple-element.23), channel_id=1, source_target_pairs={{0,16},{16,0},{32,48},{48,32},{64,80},{80,64},{96,112},{112,96},{1... | collective-permute-start | bytes 1671176 | tf_op jit(solution)/shard_map/ppermute | solution.py:254
  45.9 3.5 %collective-permute-start = (bf16[4,64,2176]{2,1,0:T(8,128)(2,1)}, bf16[4,64,2176]{2,1,0:T(8,128)(2,1)}, u32[]{:S(2)}, u32[]{:S(2)}) collective-permute-start(bf16[4,64,2176]{2,1,0:T(8,128)(2,1)} %get-tuple-element.21), channel_id=1, source_target_pairs={{0,16},{16,0},{32,48},{48,32},{64,80},{80,64},{96,112},{112,96},{1... | collective-permute-start | bytes 3342344 | tf_op jit(solution)/shard_map/ppermute | solution.py:254
  48.0 7.9 %copy-start.2 = (bf16[4,32,2176]{2,1,0:T(8,128)(2,1)S(1)}, bf16[4,32,2176]{2,1,0:T(8,128)(2,1)}, u32[]{:S(2)}) copy-start(bf16[4,32,2176]{2,1,0:T(8,128)(2,1)} %copy-done.1) | copy-start | bytes 1671172
  49.3 13.9 %collective-permute-start.5 = (bf16[4,32,2176]{2,1,0:T(8,128)(2,1)S(1)}, bf16[4,32,2176]{2,1,0:T(8,128)(2,1)S(1)}, u32[]{:S(2)}, u32[]{:S(2)}) collective-permute-start(bf16[4,32,2176]{2,1,0:T(8,128)(2,1)S(1)} %add_convert_fusion), channel_id=1, source_target_pairs={{0,1},{1,0},{2,3},{3,2},{4,5},{5,4},{6,7},{7,6},{8,9},{9,8},{10,11... | collective-permute-start | bytes 1671176 | tf_op jit(solution)/shard_map/ppermute | solution.py:263
  51.6 14.4 %collective-permute-start.3 = (bf16[64,2176]{1,0:T(8,128)(2,1)}, bf16[64,2176]{1,0:T(8,128)(2,1)}, u32[]{:S(2)}, u32[]{:S(2)}) collective-permute-start(bf16[64,2176]{1,0:T(8,128)(2,1)} %get-tuple-element.38), channel_id=1, source_target_pairs={{0,96},{16,112},{32,0},{48,16},{64,32},{80,48},{96,64},{112,80},{1... | collective-permute-start | bytes 835592 | tf_op jit(solution)/shard_map/ppermute | solution.py:259
  54.3 11.7 %collective-permute-start.2 = (bf16[64,2176]{1,0:T(8,128)(2,1)}, bf16[64,2176]{1,0:T(8,128)(2,1)}, u32[]{:S(2)}, u32[]{:S(2)}) collective-permute-start(bf16[64,2176]{1,0:T(8,128)(2,1)} %get-tuple-element.39), channel_id=1, source_target_pairs={{0,32},{16,48},{32,64},{48,80},{64,96},{80,112},{96,0},{112,16},{1... | collective-permute-start | bytes 835592 | tf_op jit(solution)/shard_map/ppermute | solution.py:259
  54.3 13.9 %collective-permute-start.1 = (bf16[64,2176]{1,0:T(8,128)(2,1)}, bf16[64,2176]{1,0:T(8,128)(2,1)}, u32[]{:S(2)}, u32[]{:S(2)}) collective-permute-start(bf16[64,2176]{1,0:T(8,128)(2,1)} %get-tuple-element.40), channel_id=1, source_target_pairs={{0,64},{16,80},{32,96},{48,112},{64,0},{80,16},{96,32},{112,48},{1... | collective-permute-start | bytes 835592 | tf_op jit(solution)/shard_map/ppermute | solution.py:259
  55.9 14.9 %collective-permute-start.6 = (bf16[4,32,2176]{2,1,0:T(8,128)(2,1)S(1)}, bf16[4,32,2176]{2,1,0:T(8,128)(2,1)S(1)}, u32[]{:S(2)}, u32[]{:S(2)}) collective-permute-start(bf16[4,32,2176]{2,1,0:T(8,128)(2,1)S(1)} %copy-done.2), channel_id=1, source_target_pairs={{0,16},{16,0},{32,48},{48,32},{64,80},{80,64},{96,112},{112,96},{1... | collective-permute-start | bytes 1671176 | tf_op jit(solution)/shard_map/ppermute | solution.py:254
  63.2 7.8 %copy-start.3 = (bf16[4,32,2176]{2,1,0:T(8,128)(2,1)}, bf16[4,32,2176]{2,1,0:T(8,128)(2,1)S(1)}, u32[]{:S(2)}) copy-start(bf16[4,32,2176]{2,1,0:T(8,128)(2,1)S(1)} %collective-permute-done.5) | copy-start | bytes 1671172
  69.6 4.5 %collective-permute-start.10 = (bf16[32,2176]{1,0:T(8,128)(2,1)S(1)}, bf16[32,2176]{1,0:T(8,128)(2,1)S(1)}, u32[]{:S(2)}, u32[]{:S(2)}) collective-permute-start(bf16[32,2176]{1,0:T(8,128)(2,1)S(1)} %select_convert_fusion), channel_id=1, source_target_pairs={{0,1},{1,0},{2,3},{3,2},{4,5},{5,4},{6,7},{7,6},{8,9},{9,8},{10,11... | collective-permute-start | bytes 417800 | tf_op jit(solution)/shard_map/ppermute | solution.py:263
  71.0 4.0 %collective-permute-start.9 = (bf16[32,2176]{1,0:T(8,128)(2,1)S(1)}, bf16[32,2176]{1,0:T(8,128)(2,1)S(1)}, u32[]{:S(2)}, u32[]{:S(2)}) collective-permute-start(bf16[32,2176]{1,0:T(8,128)(2,1)S(1)} %get-tuple-element.41), channel_id=1, source_target_pairs={{0,96},{16,112},{32,0},{48,16},{64,32},{80,48},{96,64},{112,80},{1... | collective-permute-start | bytes 417800 | tf_op jit(solution)/shard_map/ppermute | solution.py:259
  72.4 7.1 %collective-permute-start.8 = (bf16[32,2176]{1,0:T(8,128)(2,1)S(1)}, bf16[32,2176]{1,0:T(8,128)(2,1)S(1)}, u32[]{:S(2)}, u32[]{:S(2)}) collective-permute-start(bf16[32,2176]{1,0:T(8,128)(2,1)S(1)} %get-tuple-element.42), channel_id=1, source_target_pairs={{0,32},{16,48},{32,64},{48,80},{64,96},{80,112},{96,0},{112,16},{1... | collective-permute-start | bytes 417800 | tf_op jit(solution)/shard_map/ppermute | solution.py:259
  72.5 7.0 %collective-permute-start.7 = (bf16[32,2176]{1,0:T(8,128)(2,1)S(1)}, bf16[32,2176]{1,0:T(8,128)(2,1)S(1)}, u32[]{:S(2)}, u32[]{:S(2)}) collective-permute-start(bf16[32,2176]{1,0:T(8,128)(2,1)S(1)} %get-tuple-element.43), channel_id=1, source_target_pairs={{0,64},{16,80},{32,96},{48,112},{64,0},{80,16},{96,32},{112,48},{1... | collective-permute-start | bytes 417800 | tf_op jit(solution)/shard_map/ppermute | solution.py:259
  79.5 5.0 %collective-permute-start.14 = (bf16[32,2176]{1,0:T(8,128)(2,1)S(1)}, bf16[32,2176]{1,0:T(8,128)(2,1)S(1)}, u32[]{:S(2)}, u32[]{:S(2)}) collective-permute-start(bf16[32,2176]{1,0:T(8,128)(2,1)S(1)} %add_convert_fusion.4.refs_0_), channel_id=1, source_target_pairs={{0,1},{1,0},{2,3},{3,2},{4,5},{5,4},{6,7},{7,6},{8,9},{9,8},{10,11... | collective-permute-start | bytes 417800 | tf_op jit(solution)/shard_map/ppermute | solution.py:263
  81.2 4.0 %collective-permute-start.13 = (bf16[32,2176]{1,0:T(8,128)(2,1)S(1)}, bf16[32,2176]{1,0:T(8,128)(2,1)S(1)}, u32[]{:S(2)}, u32[]{:S(2)}) collective-permute-start(bf16[32,2176]{1,0:T(8,128)(2,1)S(1)} %fusion.7.refs_0_), channel_id=1, source_target_pairs={{0,96},{16,112},{32,0},{48,16},{64,32},{80,48},{96,64},{112,80},{1... | collective-permute-start | bytes 417800 | tf_op jit(solution)/shard_map/ppermute | solution.py:259
  83.2 6.6 %collective-permute-start.12 = (bf16[32,2176]{1,0:T(8,128)(2,1)S(1)}, bf16[32,2176]{1,0:T(8,128)(2,1)S(1)}, u32[]{:S(2)}, u32[]{:S(2)}) collective-permute-start(bf16[32,2176]{1,0:T(8,128)(2,1)S(1)} %fusion.7.refs_0_), channel_id=1, source_target_pairs={{0,32},{16,48},{32,64},{48,80},{64,96},{80,112},{96,0},{112,16},{1... | collective-permute-start | bytes 417800 | tf_op jit(solution)/shard_map/ppermute | solution.py:259
  83.2 6.6 %collective-permute-start.11 = (bf16[32,2176]{1,0:T(8,128)(2,1)S(1)}, bf16[32,2176]{1,0:T(8,128)(2,1)S(1)}, u32[]{:S(2)}, u32[]{:S(2)}) collective-permute-start(bf16[32,2176]{1,0:T(8,128)(2,1)S(1)} %fusion.7.refs_0_), channel_id=1, source_target_pairs={{0,64},{16,80},{32,96},{48,112},{64,0},{80,16},{96,32},{112,48},{1... | collective-permute-start | bytes 417800 | tf_op jit(solution)/shard_map/ppermute | solution.py:259
  90.4 17.3 %collective-permute-start.23 = (bf16[128,2176]{1,0:T(8,128)(2,1)S(1)}, bf16[128,2176]{1,0:T(8,128)(2,1)S(1)}, u32[]{:S(2)}, u32[]{:S(2)}) collective-permute-start(bf16[128,2176]{1,0:T(8,128)(2,1)S(1)} %shard_map.45.refs_2_), channel_id=1, source_target_pairs={{0,1},{1,0},{2,3},{3,2},{4,5},{5,4},{6,7},{7,6},{8,9},{9,8},{10,11... | collective-permute-start | bytes 1671176 | tf_op jit(solution)/shard_map/ppermute | solution.py:263
  92.0 8.4 %collective-permute-start.21 = (bf16[64,2176]{1,0:T(8,128)(2,1)S(1)}, bf16[64,2176]{1,0:T(8,128)(2,1)S(1)}, u32[]{:S(2)}, u32[]{:S(2)}) collective-permute-start(bf16[64,2176]{1,0:T(8,128)(2,1)S(1)} %shard_map.44.refs_0_), channel_id=1, source_target_pairs={{0,96},{16,112},{32,0},{48,16},{64,32},{80,48},{96,64},{112,80},{1... | collective-permute-start | bytes 835592 | tf_op jit(solution)/shard_map/ppermute | solution.py:259
  94.6 13.2 %collective-permute-start.19 = (bf16[64,2176]{1,0:T(8,128)(2,1)S(1)}, bf16[64,2176]{1,0:T(8,128)(2,1)S(1)}, u32[]{:S(2)}, u32[]{:S(2)}) collective-permute-start(bf16[64,2176]{1,0:T(8,128)(2,1)S(1)} %shard_map.44.refs_0_), channel_id=1, source_target_pairs={{0,32},{16,48},{32,64},{48,80},{64,96},{80,112},{96,0},{112,16},{1... | collective-permute-start | bytes 835592 | tf_op jit(solution)/shard_map/ppermute | solution.py:259
  94.6 16.3 %collective-permute-start.17 = (bf16[64,2176]{1,0:T(8,128)(2,1)S(1)}, bf16[64,2176]{1,0:T(8,128)(2,1)S(1)}, u32[]{:S(2)}, u32[]{:S(2)}) collective-permute-start(bf16[64,2176]{1,0:T(8,128)(2,1)S(1)} %shard_map.44.refs_0_), channel_id=1, source_target_pairs={{0,64},{16,80},{32,96},{48,112},{64,0},{80,16},{96,32},{112,48},{1... | collective-permute-start | bytes 835592 | tf_op jit(solution)/shard_map/ppermute | solution.py:259
  95.8 15.0 %collective-permute-start.15 = (bf16[64,2176]{1,0:T(8,128)(2,1)S(1)}, bf16[64,2176]{1,0:T(8,128)(2,1)S(1)}, u32[]{:S(2)}, u32[]{:S(2)}) collective-permute-start(bf16[64,2176]{1,0:T(8,128)(2,1)S(1)} %shard_map.44.refs_0_), channel_id=1, source_target_pairs={{0,16},{16,0},{32,48},{48,32},{64,80},{80,64},{96,112},{112,96},{1... | collective-permute-start | bytes 835592 | tf_op jit(solution)/shard_map/ppermute | solution.py:254
  100.4 12.6 %collective-permute-start.16 = (bf16[128,2176]{1,0:T(8,128)(2,1)S(1)}, bf16[128,2176]{1,0:T(8,128)(2,1)S(1)}, u32[]{:S(2)}, u32[]{:S(2)}) collective-permute-start(bf16[128,2176]{1,0:T(8,128)(2,1)S(1)} %shard_map.45.refs_2_), channel_id=1, source_target_pairs={{0,16},{16,0},{32,48},{48,32},{64,80},{80,64},{96,112},{112,96},{1... | collective-permute-start | bytes 1671176 | tf_op jit(solution)/shard_map/ppermute | solution.py:254
  107.7 5.2 %collective-permute-start.24 = (bf16[128,2176]{1,0:T(8,128)(2,1)S(1)}, bf16[128,2176]{1,0:T(8,128)(2,1)}, u32[]{:S(2)}, u32[]{:S(2)}) collective-permute-start(bf16[128,2176]{1,0:T(8,128)(2,1)S(1)} %collective-permute-done.23.refs_10_), channel_id=1, source_target_pairs={{0,16},{16,0},{32,48},{48,32},{64,80},{80,64},{96,112},{112,96},{1... | collective-permute-start | bytes 1671176 | tf_op jit(solution)/shard_map/ppermute | solution.py:254
  107.7 4.4 %collective-permute-start.22 = (bf16[64,2176]{1,0:T(8,128)(2,1)S(1)}, bf16[64,2176]{1,0:T(8,128)(2,1)}, u32[]{:S(2)}, u32[]{:S(2)}) collective-permute-start(bf16[64,2176]{1,0:T(8,128)(2,1)S(1)} %collective-permute-done.21.refs_8_), channel_id=1, source_target_pairs={{0,16},{16,0},{32,48},{48,32},{64,80},{80,64},{96,112},{112,96},{1... | collective-permute-start | bytes 835592 | tf_op jit(solution)/shard_map/ppermute | solution.py:254
  110.8 1.7 %collective-permute-start.20 = (bf16[64,2176]{1,0:T(8,128)(2,1)S(1)}, bf16[64,2176]{1,0:T(8,128)(2,1)}, u32[]{:S(2)}, u32[]{:S(2)}) collective-permute-start(bf16[64,2176]{1,0:T(8,128)(2,1)S(1)} %collective-permute-done.19.refs_6_), channel_id=1, source_target_pairs={{0,16},{16,0},{32,48},{48,32},{64,80},{80,64},{96,112},{112,96},{1... | collective-permute-start | bytes 835592 | tf_op jit(solution)/shard_map/ppermute | solution.py:254
  110.8 2.1 %collective-permute-start.18 = (bf16[64,2176]{1,0:T(8,128)(2,1)S(1)}, bf16[64,2176]{1,0:T(8,128)(2,1)}, u32[]{:S(2)}, u32[]{:S(2)}) collective-permute-start(bf16[64,2176]{1,0:T(8,128)(2,1)S(1)} %collective-permute-done.17.refs_4_), channel_id=1, source_target_pairs={{0,16},{16,0},{32,48},{48,32},{64,80},{80,64},{96,112},{112,96},{1... | collective-permute-start | bytes 835592 | tf_op jit(solution)/shard_map/ppermute | solution.py:254
  128.4 33.1 %all-to-all-start.1 = ((bf16[16,448,128]{2,1,0:T(8,128)(2,1)}), bf16[16,448,128]{2,1,0:T(8,128)(2,1)S(1)}, u32[]{:S(2)}, u32[]{:S(2)}) async-start(bf16[16,448,128]{2,1,0:T(8,128)(2,1)} %shard_map.46), calls=%async_computation.1 | async-start | bytes 3670016 | tf_op jit(solution)/shard_map/all_to_all | solution.py:316

commit v4 on v3

--- a/solution.py
+++ b/solution.py
@@ -70,41 +70,43 @@
     )(momentum, gradient)
 
 
-def gram_kernel(where_ref, columns_ref, ring_ref, give_ref, keep_ref):
-    half, side = where_ref[0], where_ref[1]
-    for slot in range(RING):
-        row = RING * half + where_ref[2 + slot]
-        odd = row % 2
-        count = (TILES - row) // 2
-        top, low = columns_ref[row].T, columns_ref[TILES - 1 - row].T
-
-        def put(left, right, at):
-            values = jnp.dot(left, right, preferred_element_type=f32).astype(bf16)
-            upper, lower = values[HALVES : HALVES + QUARTER], values[HALVES + QUARTER :]
-            at = pl.ds(pl.multiple_of(at * LANES, LANES), values.shape[1])
-            ring_ref[slot, :, at] = values[:HALVES]
-            give_ref[slot, :, at] = jnp.where(side == 0, lower, upper)
-            keep_ref[slot, :, at] = jnp.where(side == 0, upper, lower)
-
-        on_top = odd == 1
-        put(jnp.where(on_top, top, low), columns_ref[jnp.where(on_top, row, TILES - 1 - row)], jnp.where(on_top, 0, TILES - row))
-        for block in range(TILES // 2):
-            upper = block < count
-            over = TILES - row - odd + 2 * (block - count)
-            column = jnp.where(upper, row + odd + 2 * block, over)
-            left = top if block < RING else jnp.where(upper, top, low)
+def gram_kernel(where_ref, columns_ref, ring_ref, give_ref, keep_ref, turned):
+    side = where_ref[1]
+
+    def half_of(half):
+        folded = range(RING * half, RING * (half + 1))
+        rows = sorted([*folded, *(TILES - 1 - row for row in folded)])
+        for n, row in enumerate(rows):
+            turned[n * LANES : (n + 1) * LANES, :] = columns_ref[row].T
+        for column in range(0, TILES, 2):
+            used = [row for row in rows if row <= column + 1]
             right = jnp.concatenate([columns_ref[column], columns_ref[column + 1]], axis=1)
-            put(left, right, jnp.where(upper, odd + 2 * block, over + 1))
-
-
-def gram_pieces(columns, half, side, pieces):
-    where = jnp.stack([half, side, *pieces]).astype(jnp.int32)
+            product = jnp.dot(turned[: len(used) * LANES, :], right, preferred_element_type=f32)
+            for n, row in enumerate(used):
+                begin = LANES if row > column else 0
+                values = product[n * LANES : (n + 1) * LANES, begin:].astype(bf16)
+                upper, lower = values[HALVES : HALVES + QUARTER], values[HALVES + QUARTER :]
+                top = row in folded
+                slot = where_ref[2 + (row if top else TILES - 1 - row) - RING * half]
+                start = column * LANES + begin + (-row if top else 1) * LANES
+                at = slice(start, start + values.shape[1])
+                ring_ref[slot, :, at] = values[:HALVES]
+                give_ref[slot, :, at] = jnp.where(side == 0, lower, upper)
+                keep_ref[slot, :, at] = jnp.where(side == 0, upper, lower)
+
+    for half in range(CORES):
+        pl.when(where_ref[0] == half)(functools.partial(half_of, half))
+
+
+def gram_pieces(columns, half, side, slots):
+    where = jnp.concatenate([jnp.stack([half, side]), slots]).astype(jnp.int32)
     shapes = [(RING, HALVES, FOLD), (RING, QUARTER, FOLD), (RING, QUARTER, FOLD)]
     return pl.pallas_call(
         gram_kernel,
         in_specs=[SCALARS, WHOLE],
         out_specs=[WHOLE] * 3,
         out_shape=[jax.ShapeDtypeStruct(shape, bf16) for shape in shapes],
+        scratch_shapes=[pltpu.VMEM((ROWS // CORES, HALF), bf16)],
         compiler_params=PARAMS,
         cost_estimate=pl.CostEstimate(flops=16 * PIECE * FOLD * 512, bytes_accessed=8_000_000, transcendentals=0),
     )(where, columns)
@@ -272,9 +274,9 @@
     new_momentum = momentum_rate * momentum + gradient.astype(f32)
 
     far, ahead, behind = [(place_y + distance) % RING for distance in (2, 1, 3)]
-    wanted = [far, ahead, behind, place_y]
-    away = gram_pieces(columns, 1 - core, side, wanted)
-    kept_ring, kept_give, kept_keep = gram_pieces(columns, core, side, wanted)
+    slots = jnp.array([3, 1, 0, 2])[(jnp.arange(RING) - place_y) % RING]
+    away = gram_pieces(columns, 1 - core, side, slots)
+    kept_ring, kept_give, kept_keep = gram_pieces(columns, core, side, slots)
     got_give, got_ring, got_keep = swap_cores(away[1]), swap_cores(away[0]), swap_cores(away[2])
 
     def round_ring(pieces):
@@ -283,18 +285,14 @@
     ring_sums = [add(kept_ring[slot], got_ring[slot]) for slot in range(3)]
     partner = swap_pair(add(kept_give, got_give))
     *arrived, partner = lax.optimization_barrier((*round_ring(ring_sums), partner))
-    ring_total = total_of(kept_ring[3], got_ring[3], *arrived)
-    upper, lower = ring_total[:QUARTER], ring_total[QUARTER:]
+    first = add(kept_ring[3], got_ring[3], *arrived)
     partner_sums = [add(kept_keep[slot], got_keep[slot], partner[slot]) for slot in range(3)]
-    upper_got = swap_pair(jnp.where(side == 0, lower, upper).astype(bf16))
-    *arrived, upper_got = lax.optimization_barrier((*round_ring(partner_sums), upper_got))
-    first = add(jnp.where(side == 0, upper, lower), upper_got)
+    first_got = swap_pair(first)
+    *arrived, first_got = lax.optimization_barrier((*round_ring(partner_sums), first_got))
+    first = add(first, first_got)
     second = add(kept_keep[3], got_keep[3], partner[3], *arrived)
 
-    first_other = swap_pair(first)
-    *arrived, first_other = lax.optimization_barrier((*round_ring([second] * 3), first_other))
-    first = merge((first, first_other), (side * QUARTER, (1 - side) * QUARTER))
-    second = merge((second, *arrived), range(0, PIECE, QUARTER))
+    second = merge((second, *round_ring([second] * 3)), range(0, PIECE, QUARTER))
     second_other = swap_pair(second)
     pieces, layout, where = [], [], []
 

time: 163 us -> 155 us (0.951)
  other arithmetic: 10.9 us -> 5.8 us
  Pallas kernels: 27.2 us -> 25.3 us
    convert_element_type x5 -> x6, other arithmetic: 4.6 us -> 0.84 us  [add(): return total_of(*terms).astype(bf16)]
    ppermute x4 -> x3, waiting for transfers between devices: 5.88 us -> 7.14 us  [swap_pair(): return lax.ppermute(values, 'mat', [(i, i ^ 1) for i in range(MEMBERS)])]
  transfers between devices with their start and end apart: 27 -> 26, of which waited for: 12 -> 13; matrix products, arithmetic and copies ran while one was open for 7% -> 4% of each run, Pallas kernels for 2% -> 1%
where the time goes in v4:
time: 155 us
  waiting for transfers between devices  74.3 us (48%)
  starting transfers between devices  48 us (31%)
  Pallas kernels  25.3 us (16%)
  other arithmetic  5.8 us (4%)
    all_to_all x1, waiting for transfers between devices, shards(): columns = lax.all_to_all(blended.reshape(MEMBERS, HALF, LANES), 'mat', 0, 0)  26 us
    all_to_all x1, waiting for transfers between devices, shards(): returned = lax.all_to_all(update, 'mat', 0, 0)  24.5 us
    ppermute x9, starting transfers between devices, swap_cores(): lax.ppermute(values, 'fsdp', [(i, i ^ 1) for i in range(CORES * RING)])  19 us
    pallas_call x1, Pallas kernels, newton_step(): pl.pallas_call(functools.partial(step_kernel, layout), in_specs=[SCALARS,...  15.3 us
    ppermute x12, starting transfers between devices, shift(): lax.ppermute(values, 'fsdp', [(i, (i + CORES * distance) % size) for i in...  14.9 us
    ppermute x12, waiting for transfers between devices, shift(): lax.ppermute(values, 'fsdp', [(i, (i + CORES * distance) % size) for i in...  14.4 us
    all_to_all x1, starting transfers between devices, shards(): columns = lax.all_to_all(blended.reshape(MEMBERS, HALF, LANES), 'mat', 0, 0)  8.44 us
    ppermute x3, waiting for transfers between devices, swap_pair(): return lax.ppermute(values, 'mat', [(i, i ^ 1) for i in range(MEMBERS)])  7.14 us
  transfers between devices with their start and end apart: 26, of which 13 were waited for; matrix products, arithmetic and copies ran while one was open for 4% of the time, Pallas kernels for 1%

profile of v4, /device:TPU:1, one launch (start us, length us, event | category | flops | bytes accessed | tf_op | source)
XLA Modules:
  0.0 155.2 jit_solution(8988037353502361975)
XLA Ops:
  0.6 3.9 %shard_map.50 = bf16[8,896,128]{2,1,0:T(8,128)(2,1)} custom-call(f32[8,128,896]{2,1,0:T(8,128)} %momentum_ref.1, bf16[8,128,896]{2,1,0:T(8,128)(2,1)} %gradient_ref.1), custom_call_target="tpu_custom_call" | custom-call | tf_op jit(solution)/shard_map/pallas_call | solution.py:58
  4.6 0.0 copy-start.1
  4.6 8.4 %all-to-all-start = ((bf16[16,448,128]{2,1,0:T(8,128)(2,1)}), bf16[16,448,128]{2,1,0:T(8,128)(2,1)S(1)}, u32[]{:S(2)}, u32[]{:S(2)}) async-start(bf16[16,448,128]{2,1,0:T(8,128)(2,1)} %bitcast.46), calls=%async_computation | async-start | bytes 3670016 | tf_op jit(solution)/shard_map/all_to_all | solution.py:273
  13.1 0.6 gather_fusion
  13.7 0.1 add_add_fusion
  13.8 26.0 %all-to-all-done.columns_ref = bf16[16,448,128]{2,1,0:T(8,128)(2,1)S(1)} async-done(((bf16[16,448,128]{2,1,0:T(8,128)(2,1)}), bf16[16,448,128]{2,1,0:T(8,128)(2,1)S(1)}, u32[]{:S(2)}, u32[]{:S(2)}) %all-to-all-start) | async-done | bytes 1835040 | tf_op jit(solution)/shard_map/all_to_all | solution.py:273
  39.8 2.0 %shard_map.52 = (bf16[4,64,2176]{2,1,0:T(8,128)(2,1)S(1)}, bf16[4,32,2176]{2,1,0:T(8,128)(2,1)S(1)}, bf16[4,32,2176]{2,1,0:T(8,128)(2,1)S(1)}) custom-call(s32[6]{0:T(128)S(1)} %get-tuple-element.37.where_ref, bf16[16,448,128]{2,1,0:T(8,128)(2,1)S(1)} %all-to-all-done.columns_ref), custom_call_target="tpu_custom_call" | custom-call | flops 2281701376 | bytes 8000000 | tf_op jit(solution)/shard_map/pallas_call | solution.py:104
  41.8 2.2 %collective-permute-start.4 = (bf16[4,32,2176]{2,1,0:T(8,128)(2,1)S(1)}, bf16[4,32,2176]{2,1,0:T(8,128)(2,1)S(1)}, u32[]{:S(2)}, u32[]{:S(2)}) collective-permute-start(bf16[4,32,2176]{2,1,0:T(8,128)(2,1)S(1)} %get-tuple-element.19), channel_id=1, source_target_pairs={{0,16},{16,0},{32,48},{48,32},{64,80},{80,64},{96,112},{112,96},{1... | collective-permute-start | bytes 1671176 | tf_op jit(solution)/shard_map/ppermute | solution.py:256
  44.0 0.1 collective-permute-start
  44.1 2.0 %shard_map.51 = (bf16[4,64,2176]{2,1,0:T(8,128)(2,1)S(1)}, bf16[4,32,2176]{2,1,0:T(8,128)(2,1)S(1)}, bf16[4,32,2176]{2,1,0:T(8,128)(2,1)S(1)}) custom-call(s32[6]{0:T(128)S(1)} %get-tuple-element.36.where_ref, bf16[16,448,128]{2,1,0:T(8,128)(2,1)S(1)} %all-to-all-done.columns_ref), custom_call_target="tpu_custom_call" | custom-call | flops 2281701376 | bytes 8000000 | tf_op jit(solution)/shard_map/pallas_call | solution.py:104
  46.2 0.0 collective-permute-done.4
  46.2 0.1 add_convert_fusion
  46.3 0.1 collective-permute-start.5
  46.4 0.8 collective-permute-done
  47.2 0.2 fusion.5
  47.4 2.8 %collective-permute-start.3 = (bf16[64,2176]{1,0:T(8,128)(2,1)S(1)}, bf16[64,2176]{1,0:T(8,128)(2,1)S(1)}, u32[]{:S(2)}, u32[]{:S(2)}) collective-permute-start(bf16[64,2176]{1,0:T(8,128)(2,1)S(1)} %get-tuple-element.30), channel_id=1, source_target_pairs={{0,96},{16,112},{32,0},{48,16},{64,32},{80,48},{96,64},{112,80},{1... | collective-permute-start | bytes 835592 | tf_op jit(solution)/shard_map/ppermute | solution.py:261
  50.2 1.6 %collective-permute-start.1 = (bf16[64,2176]{1,0:T(8,128)(2,1)S(1)}, bf16[64,2176]{1,0:T(8,128)(2,1)S(1)}, u32[]{:S(2)}, u32[]{:S(2)}) collective-permute-start(bf16[64,2176]{1,0:T(8,128)(2,1)S(1)} %get-tuple-element.32), channel_id=1, source_target_pairs={{0,64},{16,80},{32,96},{48,112},{64,0},{80,16},{96,32},{112,48},{1... | collective-permute-start | bytes 835592 | tf_op jit(solution)/shard_map/ppermute | solution.py:261
  51.8 1.2 collective-permute-start.6
  53.1 7.1 %collective-permute-done.5 = bf16[4,32,2176]{2,1,0:T(8,128)(2,1)S(1)} collective-permute-done((bf16[4,32,2176]{2,1,0:T(8,128)(2,1)S(1)}, bf16[4,32,2176]{2,1,0:T(8,128)(2,1)S(1)}, u32[]{:S(2)}, u32[]{:S(2)}) %collective-permute-start.5) | collective-permute-done | bytes 557088 | tf_op jit(solution)/shard_map/ppermute | solution.py:265
  60.2 1.5 collective-permute-done.3
  61.7 0.0 collective-permute-done.2
  61.7 2.2 %collective-permute-done.1 = bf16[64,2176]{1,0:T(8,128)(2,1)S(1)} collective-permute-done((bf16[64,2176]{1,0:T(8,128)(2,1)S(1)}, bf16[64,2176]{1,0:T(8,128)(2,1)S(1)}, u32[]{:S(2)}, u32[]{:S(2)}) %collective-permute-start.1) | collective-permute-done | bytes 278560 | tf_op jit(solution)/shard_map/ppermute | solution.py:261
  63.9 0.2 fusion.2
  64.1 0.4 collective-permute-start.10
  64.5 0.2 fusion.11
  64.7 1.4 collective-permute-start.9
  66.1 0.2 collective-permute-start.8
  66.2 1.6 %collective-permute-start.7 = (bf16[32,2176]{1,0:T(8,128)(2,1)S(1)}, bf16[32,2176]{1,0:T(8,128)(2,1)S(1)}, u32[]{:S(2)}, u32[]{:S(2)}) collective-permute-start(bf16[32,2176]{1,0:T(8,128)(2,1)S(1)} %get-tuple-element.35), channel_id=1, source_target_pairs={{0,64},{16,80},{32,96},{48,112},{64,0},{80,16},{96,32},{112,48},{1... | collective-permute-start | bytes 417800 | tf_op jit(solution)/shard_map/ppermute | solution.py:261
  67.8 0.8 collective-permute-done.9
  68.7 4.7 %collective-permute-done.8 = bf16[32,2176]{1,0:T(8,128)(2,1)S(1)} collective-permute-done((bf16[32,2176]{1,0:T(8,128)(2,1)S(1)}, bf16[32,2176]{1,0:T(8,128)(2,1)S(1)}, u32[]{:S(2)}, u32[]{:S(2)}) %collective-permute-start.8) | collective-permute-done | bytes 139296 | tf_op jit(solution)/shard_map/ppermute | solution.py:261
  73.3 0.0 collective-permute-done.7
  73.3 0.0 collective-permute-done.10
  73.3 0.1 fusion.8.refs_0_
  73.4 2.0 %collective-permute-start.14 = (bf16[32,2176]{1,0:T(8,128)(2,1)S(1)}, bf16[32,2176]{1,0:T(8,128)(2,1)S(1)}, u32[]{:S(2)}, u32[]{:S(2)}) collective-permute-start(bf16[32,2176]{1,0:T(8,128)(2,1)S(1)} %fusion.8.refs_0_), channel_id=1, source_target_pairs={{0,96},{16,112},{32,0},{48,16},{64,32},{80,48},{96,64},{112,80},{1... | collective-permute-start | bytes 417800 | tf_op jit(solution)/shard_map/ppermute | solution.py:261
  75.4 0.0 collective-permute-start.13
  75.4 1.4 collective-permute-start.12
  76.9 0.6 collective-permute-done.14.refs_3_
  77.4 4.6 %collective-permute-done.13.refs_2_ = bf16[32,2176]{1,0:T(8,128)(2,1)S(1)} collective-permute-done((bf16[32,2176]{1,0:T(8,128)(2,1)S(1)}, bf16[32,2176]{1,0:T(8,128)(2,1)S(1)}, u32[]{:S(2)}, u32[]{:S(2)}) %collective-permute-start.13) | collective-permute-done | bytes 139296 | tf_op jit(solution)/shard_map/ppermute | solution.py:261
  82.0 0.0 collective-permute-done.12.refs_1_
  82.0 0.6 shard_map.53.refs_2_
  82.6 1.5 collective-permute-start.22
  84.1 0.1 add_convert_fusion.1.refs_0_
  84.2 2.6 %collective-permute-start.20 = (bf16[64,2176]{1,0:T(8,128)(2,1)S(1)}, bf16[64,2176]{1,0:T(8,128)(2,1)S(1)}, u32[]{:S(2)}, u32[]{:S(2)}) collective-permute-start(bf16[64,2176]{1,0:T(8,128)(2,1)S(1)} %add_convert_fusion.1.refs_0_), channel_id=1, source_target_pairs={{0,96},{16,112},{32,0},{48,16},{64,32},{80,48},{96,64},{112,80},{1... | collective-permute-start | bytes 835592 | tf_op jit(solution)/shard_map/ppermute | solution.py:261
  86.8 1.3 collective-permute-start.16
  88.1 3.8 %collective-permute-start.11 = (bf16[64,2176]{1,0:T(8,128)(2,1)S(1)}, bf16[64,2176]{1,0:T(8,128)(2,1)S(1)}, u32[]{:S(2)}, u32[]{:S(2)}) collective-permute-start(bf16[64,2176]{1,0:T(8,128)(2,1)S(1)} %add_convert_fusion.1.refs_0_), channel_id=1, source_target_pairs={{0,16},{16,0},{32,48},{48,32},{64,80},{80,64},{96,112},{112,96},{1... | collective-permute-start | bytes 835592 | tf_op jit(solution)/shard_map/ppermute | solution.py:256
  91.9 8.1 %collective-permute-start.15 = (bf16[128,2176]{1,0:T(8,128)(2,1)S(1)}, bf16[128,2176]{1,0:T(8,128)(2,1)S(1)}, u32[]{:S(2)}, u32[]{:S(2)}) collective-permute-start(bf16[128,2176]{1,0:T(8,128)(2,1)S(1)} %shard_map.53.refs_2_), channel_id=1, source_target_pairs={{0,16},{16,0},{32,48},{48,32},{64,80},{80,64},{96,112},{112,96},{1... | collective-permute-start | bytes 1671176 | tf_op jit(solution)/shard_map/ppermute | solution.py:256
  99.9 0.0 collective-permute-done.22.refs_10_
  99.9 0.0 collective-permute-start.23
  100.0 0.0 collective-permute-done.18.refs_6_
  100.0 3.1 %collective-permute-start.21 = (bf16[64,2176]{1,0:T(8,128)(2,1)S(1)}, bf16[64,2176]{1,0:T(8,128)(2,1)S(1)}, u32[]{:S(2)}, u32[]{:S(2)}) collective-permute-start(bf16[64,2176]{1,0:T(8,128)(2,1)S(1)} %collective-permute-done.20.refs_8_), channel_id=1, source_target_pairs={{0,16},{16,0},{32,48},{48,32},{64,80},{80,64},{96,112},{112,96},{1... | collective-permute-start | bytes 835592 | tf_op jit(solution)/shard_map/ppermute | solution.py:256
  103.1 0.0 collective-permute-done.16.refs_4_
  103.1 0.0 collective-permute-start.19
  103.1 0.0 collective-permute-done.11.refs_1_
  103.1 0.5 collective-permute-start.17
  103.6 0.1 stack.38.where_ref
  103.7 0.9 collective-permute-done.21.refs_9_
  104.6 0.2 collective-permute-done.19.refs_7_
  104.8 0.4 collective-permute-done.17.refs_5_
  105.2 0.0 collective-permute-done.15.refs_3_
  105.2 15.3 %shard_map.54 = bf16[16,448,128]{2,1,0:T(8,128)(2,1)} custom-call(s32[48]{0:T(128)S(1)} %stack.38.where_ref, bf16[16,448,128]{2,1,0:T(8,128)(2,1)} %copy-done, bf16[64,2176]{1,0:T(8,128)(2,1)S(1)} %add_convert_fusion.1.refs_0_, bf16[64,2176]{1,0:T(8,128)(2,1)S(1)} %collective-permute-done.11.refs_1_, bf16[128,2176]{1,0:T(8,128)(2,1)S(1)} %shard_map.53.refs_2_, ...), custom_call_target="tpu_custom_call" | custom-call | flops 7516192768 | bytes 8000000 | tf_op jit(solution)/shard_map/pallas_call | solution.py:203
  120.5 3.7 %all-to-all-start.1 = ((bf16[16,448,128]{2,1,0:T(8,128)(2,1)}), bf16[16,448,128]{2,1,0:T(8,128)(2,1)S(1)}, u32[]{:S(2)}, u32[]{:S(2)}) async-start(bf16[16,448,128]{2,1,0:T(8,128)(2,1)} %shard_map.54), calls=%async_computation.1 | async-start | bytes 3670016 | tf_op jit(solution)/shard_map/all_to_all | solution.py:314
  124.3 4.9 %convert_add_fusion = f32[8,128,896]{2,1,0:T(8,128)} fusion(bf16[8,128,896]{2,1,0:T(8,128)(2,1)} %gradient_ref.1, f32[8,128,896]{2,1,0:T(8,128)} %momentum_ref.1), kind=kLoop, calls=%fused_computation.1 | loop fusion | flops 2752512 | bytes 9175040 | tf_op jit(solution)/shard_map/add | solution.py:274
  129.1 24.5 %all-to-all-done.1 = bf16[16,448,128]{2,1,0:T(8,128)(2,1)S(1)} async-done(((bf16[16,448,128]{2,1,0:T(8,128)(2,1)}), bf16[16,448,128]{2,1,0:T(8,128)(2,1)S(1)}, u32[]{:S(2)}, u32[]{:S(2)}) %all-to-all-start.1) | async-done | bytes 1835040 | tf_op jit(solution)/shard_map/all_to_all | solution.py:314
  153.6 1.4 shard_map.55
  (11 shorter events, 0.0 us)
Async XLA Ops:
  4.6 8.5 %copy-start.1 = (s32[4]{0:T(128)S(1)}, s32[4]{0:T(128)}, u32[]{:S(2)}) copy-start(s32[4]{0:T(128)} %constant.79.clone) | copy-start | bytes 52
  4.6 35.2 %all-to-all-start = ((bf16[16,448,128]{2,1,0:T(8,128)(2,1)}), bf16[16,448,128]{2,1,0:T(8,128)(2,1)S(1)}, u32[]{:S(2)}, u32[]{:S(2)}) async-start(bf16[16,448,128]{2,1,0:T(8,128)(2,1)} %bitcast.46), calls=%async_computation | async-start | bytes 3670016 | tf_op jit(solution)/shard_map/all_to_all | solution.py:273
  39.8 4.3 %copy-start = (bf16[16,448,128]{2,1,0:T(8,128)(2,1)}, bf16[16,448,128]{2,1,0:T(8,128)(2,1)S(1)}, u32[]{:S(2)}) copy-start(bf16[16,448,128]{2,1,0:T(8,128)(2,1)S(1)} %all-to-all-done.columns_ref) | copy-start | bytes 5505028
  41.8 4.4 %collective-permute-start.4 = (bf16[4,32,2176]{2,1,0:T(8,128)(2,1)S(1)}, bf16[4,32,2176]{2,1,0:T(8,128)(2,1)S(1)}, u32[]{:S(2)}, u32[]{:S(2)}) collective-permute-start(bf16[4,32,2176]{2,1,0:T(8,128)(2,1)S(1)} %get-tuple-element.19), channel_id=1, source_target_pairs={{0,16},{16,0},{32,48},{48,32},{64,80},{80,64},{96,112},{112,96},{1... | collective-permute-start | bytes 1671176 | tf_op jit(solution)/shard_map/ppermute | solution.py:256
  44.0 3.2 %collective-permute-start = (bf16[4,64,2176]{2,1,0:T(8,128)(2,1)S(1)}, bf16[4,64,2176]{2,1,0:T(8,128)(2,1)S(1)}, u32[]{:S(2)}, u32[]{:S(2)}) collective-permute-start(bf16[4,64,2176]{2,1,0:T(8,128)(2,1)S(1)} %get-tuple-element.17), channel_id=1, source_target_pairs={{0,16},{16,0},{32,48},{48,32},{64,80},{80,64},{96,112},{112,96},{1... | collective-permute-start | bytes 3342344 | tf_op jit(solution)/shard_map/ppermute | solution.py:256
  46.3 13.9 %collective-permute-start.5 = (bf16[4,32,2176]{2,1,0:T(8,128)(2,1)S(1)}, bf16[4,32,2176]{2,1,0:T(8,128)(2,1)S(1)}, u32[]{:S(2)}, u32[]{:S(2)}) collective-permute-start(bf16[4,32,2176]{2,1,0:T(8,128)(2,1)S(1)} %add_convert_fusion), channel_id=1, source_target_pairs={{0,1},{1,0},{2,3},{3,2},{4,5},{5,4},{6,7},{7,6},{8,9},{9,8},{10,11... | collective-permute-start | bytes 1671176 | tf_op jit(solution)/shard_map/ppermute | solution.py:265
  47.4 14.3 %collective-permute-start.3 = (bf16[64,2176]{1,0:T(8,128)(2,1)S(1)}, bf16[64,2176]{1,0:T(8,128)(2,1)S(1)}, u32[]{:S(2)}, u32[]{:S(2)}) collective-permute-start(bf16[64,2176]{1,0:T(8,128)(2,1)S(1)} %get-tuple-element.30), channel_id=1, source_target_pairs={{0,96},{16,112},{32,0},{48,16},{64,32},{80,48},{96,64},{112,80},{1... | collective-permute-start | bytes 835592 | tf_op jit(solution)/shard_map/ppermute | solution.py:261
  50.2 11.5 %collective-permute-start.2 = (bf16[64,2176]{1,0:T(8,128)(2,1)S(1)}, bf16[64,2176]{1,0:T(8,128)(2,1)S(1)}, u32[]{:S(2)}, u32[]{:S(2)}) collective-permute-start(bf16[64,2176]{1,0:T(8,128)(2,1)S(1)} %get-tuple-element.31), channel_id=1, source_target_pairs={{0,32},{16,48},{32,64},{48,80},{64,96},{80,112},{96,0},{112,16},{1... | collective-permute-start | bytes 835592 | tf_op jit(solution)/shard_map/ppermute | solution.py:261
  50.2 13.7 %collective-permute-start.1 = (bf16[64,2176]{1,0:T(8,128)(2,1)S(1)}, bf16[64,2176]{1,0:T(8,128)(2,1)S(1)}, u32[]{:S(2)}, u32[]{:S(2)}) collective-permute-start(bf16[64,2176]{1,0:T(8,128)(2,1)S(1)} %get-tuple-element.32), channel_id=1, source_target_pairs={{0,64},{16,80},{32,96},{48,112},{64,0},{80,16},{96,32},{112,48},{1... | collective-permute-start | bytes 835592 | tf_op jit(solution)/shard_map/ppermute | solution.py:261
  51.8 12.7 %collective-permute-start.6 = (bf16[4,32,2176]{2,1,0:T(8,128)(2,1)S(1)}, bf16[4,32,2176]{2,1,0:T(8,128)(2,1)S(1)}, u32[]{:S(2)}, u32[]{:S(2)}) collective-permute-start(bf16[4,32,2176]{2,1,0:T(8,128)(2,1)S(1)} %get-tuple-element.24), channel_id=1, source_target_pairs={{0,16},{16,0},{32,48},{48,32},{64,80},{80,64},{96,112},{112,96},{1... | collective-permute-start | bytes 1671176 | tf_op jit(solution)/shard_map/ppermute | solution.py:256
  64.1 9.2 %collective-permute-start.10 = (bf16[64,2176]{1,0:T(8,128)(2,1)S(1)}, bf16[64,2176]{1,0:T(8,128)(2,1)S(1)}, u32[]{:S(2)}, u32[]{:S(2)}) collective-permute-start(bf16[64,2176]{1,0:T(8,128)(2,1)S(1)} %fusion.2), channel_id=1, source_target_pairs={{0,1},{1,0},{2,3},{3,2},{4,5},{5,4},{6,7},{7,6},{8,9},{9,8},{10,11... | collective-permute-start | bytes 835592 | tf_op jit(solution)/shard_map/ppermute | solution.py:265
  64.7 4.0 %collective-permute-start.9 = (bf16[32,2176]{1,0:T(8,128)(2,1)S(1)}, bf16[32,2176]{1,0:T(8,128)(2,1)S(1)}, u32[]{:S(2)}, u32[]{:S(2)}) collective-permute-start(bf16[32,2176]{1,0:T(8,128)(2,1)S(1)} %get-tuple-element.33), channel_id=1, source_target_pairs={{0,96},{16,112},{32,0},{48,16},{64,32},{80,48},{96,64},{112,80},{1... | collective-permute-start | bytes 417800 | tf_op jit(solution)/shard_map/ppermute | solution.py:261
  66.1 7.3 %collective-permute-start.8 = (bf16[32,2176]{1,0:T(8,128)(2,1)S(1)}, bf16[32,2176]{1,0:T(8,128)(2,1)S(1)}, u32[]{:S(2)}, u32[]{:S(2)}) collective-permute-start(bf16[32,2176]{1,0:T(8,128)(2,1)S(1)} %get-tuple-element.34), channel_id=1, source_target_pairs={{0,32},{16,48},{32,64},{48,80},{64,96},{80,112},{96,0},{112,16},{1... | collective-permute-start | bytes 417800 | tf_op jit(solution)/shard_map/ppermute | solution.py:261
  66.2 7.1 %collective-permute-start.7 = (bf16[32,2176]{1,0:T(8,128)(2,1)S(1)}, bf16[32,2176]{1,0:T(8,128)(2,1)S(1)}, u32[]{:S(2)}, u32[]{:S(2)}) collective-permute-start(bf16[32,2176]{1,0:T(8,128)(2,1)S(1)} %get-tuple-element.35), channel_id=1, source_target_pairs={{0,64},{16,80},{32,96},{48,112},{64,0},{80,16},{96,32},{112,48},{1... | collective-permute-start | bytes 417800 | tf_op jit(solution)/shard_map/ppermute | solution.py:261
  73.4 4.0 %collective-permute-start.14 = (bf16[32,2176]{1,0:T(8,128)(2,1)S(1)}, bf16[32,2176]{1,0:T(8,128)(2,1)S(1)}, u32[]{:S(2)}, u32[]{:S(2)}) collective-permute-start(bf16[32,2176]{1,0:T(8,128)(2,1)S(1)} %fusion.8.refs_0_), channel_id=1, source_target_pairs={{0,96},{16,112},{32,0},{48,16},{64,32},{80,48},{96,64},{112,80},{1... | collective-permute-start | bytes 417800 | tf_op jit(solution)/shard_map/ppermute | solution.py:261
  75.4 6.6 %collective-permute-start.13 = (bf16[32,2176]{1,0:T(8,128)(2,1)S(1)}, bf16[32,2176]{1,0:T(8,128)(2,1)S(1)}, u32[]{:S(2)}, u32[]{:S(2)}) collective-permute-start(bf16[32,2176]{1,0:T(8,128)(2,1)S(1)} %fusion.8.refs_0_), channel_id=1, source_target_pairs={{0,32},{16,48},{32,64},{48,80},{64,96},{80,112},{96,0},{112,16},{1... | collective-permute-start | bytes 417800 | tf_op jit(solution)/shard_map/ppermute | solution.py:261
  75.4 6.6 %collective-permute-start.12 = (bf16[32,2176]{1,0:T(8,128)(2,1)S(1)}, bf16[32,2176]{1,0:T(8,128)(2,1)S(1)}, u32[]{:S(2)}, u32[]{:S(2)}) collective-permute-start(bf16[32,2176]{1,0:T(8,128)(2,1)S(1)} %fusion.8.refs_0_), channel_id=1, source_target_pairs={{0,64},{16,80},{32,96},{48,112},{64,0},{80,16},{96,32},{112,48},{1... | collective-permute-start | bytes 417800 | tf_op jit(solution)/shard_map/ppermute | solution.py:261
  82.6 17.3 %collective-permute-start.22 = (bf16[128,2176]{1,0:T(8,128)(2,1)S(1)}, bf16[128,2176]{1,0:T(8,128)(2,1)S(1)}, u32[]{:S(2)}, u32[]{:S(2)}) collective-permute-start(bf16[128,2176]{1,0:T(8,128)(2,1)S(1)} %shard_map.53.refs_2_), channel_id=1, source_target_pairs={{0,1},{1,0},{2,3},{3,2},{4,5},{5,4},{6,7},{7,6},{8,9},{9,8},{10,11... | collective-permute-start | bytes 1671176 | tf_op jit(solution)/shard_map/ppermute | solution.py:265
  84.2 7.7 %collective-permute-start.20 = (bf16[64,2176]{1,0:T(8,128)(2,1)S(1)}, bf16[64,2176]{1,0:T(8,128)(2,1)S(1)}, u32[]{:S(2)}, u32[]{:S(2)}) collective-permute-start(bf16[64,2176]{1,0:T(8,128)(2,1)S(1)} %add_convert_fusion.1.refs_0_), channel_id=1, source_target_pairs={{0,96},{16,112},{32,0},{48,16},{64,32},{80,48},{96,64},{112,80},{1... | collective-permute-start | bytes 835592 | tf_op jit(solution)/shard_map/ppermute | solution.py:261
  86.8 13.2 %collective-permute-start.18 = (bf16[64,2176]{1,0:T(8,128)(2,1)S(1)}, bf16[64,2176]{1,0:T(8,128)(2,1)S(1)}, u32[]{:S(2)}, u32[]{:S(2)}) collective-permute-start(bf16[64,2176]{1,0:T(8,128)(2,1)S(1)} %add_convert_fusion.1.refs_0_), channel_id=1, source_target_pairs={{0,32},{16,48},{32,64},{48,80},{64,96},{80,112},{96,0},{112,16},{1... | collective-permute-start | bytes 835592 | tf_op jit(solution)/shard_map/ppermute | solution.py:261
  86.8 16.3 %collective-permute-start.16 = (bf16[64,2176]{1,0:T(8,128)(2,1)S(1)}, bf16[64,2176]{1,0:T(8,128)(2,1)S(1)}, u32[]{:S(2)}, u32[]{:S(2)}) collective-permute-start(bf16[64,2176]{1,0:T(8,128)(2,1)S(1)} %add_convert_fusion.1.refs_0_), channel_id=1, source_target_pairs={{0,64},{16,80},{32,96},{48,112},{64,0},{80,16},{96,32},{112,48},{1... | collective-permute-start | bytes 835592 | tf_op jit(solution)/shard_map/ppermute | solution.py:261
  88.1 15.0 %collective-permute-start.11 = (bf16[64,2176]{1,0:T(8,128)(2,1)S(1)}, bf16[64,2176]{1,0:T(8,128)(2,1)S(1)}, u32[]{:S(2)}, u32[]{:S(2)}) collective-permute-start(bf16[64,2176]{1,0:T(8,128)(2,1)S(1)} %add_convert_fusion.1.refs_0_), channel_id=1, source_target_pairs={{0,16},{16,0},{32,48},{48,32},{64,80},{80,64},{96,112},{112,96},{1... | collective-permute-start | bytes 835592 | tf_op jit(solution)/shard_map/ppermute | solution.py:256
  91.9 13.3 %collective-permute-start.15 = (bf16[128,2176]{1,0:T(8,128)(2,1)S(1)}, bf16[128,2176]{1,0:T(8,128)(2,1)S(1)}, u32[]{:S(2)}, u32[]{:S(2)}) collective-permute-start(bf16[128,2176]{1,0:T(8,128)(2,1)S(1)} %shard_map.53.refs_2_), channel_id=1, source_target_pairs={{0,16},{16,0},{32,48},{48,32},{64,80},{80,64},{96,112},{112,96},{1... | collective-permute-start | bytes 1671176 | tf_op jit(solution)/shard_map/ppermute | solution.py:256
  99.9 5.2 %collective-permute-start.23 = (bf16[128,2176]{1,0:T(8,128)(2,1)S(1)}, bf16[128,2176]{1,0:T(8,128)(2,1)}, u32[]{:S(2)}, u32[]{:S(2)}) collective-permute-start(bf16[128,2176]{1,0:T(8,128)(2,1)S(1)} %collective-permute-done.22.refs_10_), channel_id=1, source_target_pairs={{0,16},{16,0},{32,48},{48,32},{64,80},{80,64},{96,112},{112,96},{1... | collective-permute-start | bytes 1671176 | tf_op jit(solution)/shard_map/ppermute | solution.py:256
  100.0 4.6 %collective-permute-start.21 = (bf16[64,2176]{1,0:T(8,128)(2,1)S(1)}, bf16[64,2176]{1,0:T(8,128)(2,1)S(1)}, u32[]{:S(2)}, u32[]{:S(2)}) collective-permute-start(bf16[64,2176]{1,0:T(8,128)(2,1)S(1)} %collective-permute-done.20.refs_8_), channel_id=1, source_target_pairs={{0,16},{16,0},{32,48},{48,32},{64,80},{80,64},{96,112},{112,96},{1... | collective-permute-start | bytes 835592 | tf_op jit(solution)/shard_map/ppermute | solution.py:256
  103.1 1.7 %collective-permute-start.19 = (bf16[64,2176]{1,0:T(8,128)(2,1)S(1)}, bf16[64,2176]{1,0:T(8,128)(2,1)}, u32[]{:S(2)}, u32[]{:S(2)}) collective-permute-start(bf16[64,2176]{1,0:T(8,128)(2,1)S(1)} %collective-permute-done.18.refs_6_), channel_id=1, source_target_pairs={{0,16},{16,0},{32,48},{48,32},{64,80},{80,64},{96,112},{112,96},{1... | collective-permute-start | bytes 835592 | tf_op jit(solution)/shard_map/ppermute | solution.py:256
  103.1 2.1 %collective-permute-start.17 = (bf16[64,2176]{1,0:T(8,128)(2,1)S(1)}, bf16[64,2176]{1,0:T(8,128)(2,1)}, u32[]{:S(2)}, u32[]{:S(2)}) collective-permute-start(bf16[64,2176]{1,0:T(8,128)(2,1)S(1)} %collective-permute-done.16.refs_4_), channel_id=1, source_target_pairs={{0,16},{16,0},{32,48},{48,32},{64,80},{80,64},{96,112},{112,96},{1... | collective-permute-start | bytes 835592 | tf_op jit(solution)/shard_map/ppermute | solution.py:256
  120.5 33.1 %all-to-all-start.1 = ((bf16[16,448,128]{2,1,0:T(8,128)(2,1)}), bf16[16,448,128]{2,1,0:T(8,128)(2,1)S(1)}, u32[]{:S(2)}, u32[]{:S(2)}) async-start(bf16[16,448,128]{2,1,0:T(8,128)(2,1)} %shard_map.54), calls=%async_computation.1 | async-start | bytes 3670016 | tf_op jit(solution)/shard_map/all_to_all | solution.py:314

commit v5 on v4

--- a/solution.py
+++ b/solution.py
@@ -284,11 +284,11 @@
 
     ring_sums = [add(kept_ring[slot], got_ring[slot]) for slot in range(3)]
     partner = swap_pair(add(kept_give, got_give))
-    *arrived, partner = lax.optimization_barrier((*round_ring(ring_sums), partner))
+    arrived = round_ring(ring_sums)
     first = add(kept_ring[3], got_ring[3], *arrived)
     partner_sums = [add(kept_keep[slot], got_keep[slot], partner[slot]) for slot in range(3)]
     first_got = swap_pair(first)
-    *arrived, first_got = lax.optimization_barrier((*round_ring(partner_sums), first_got))
+    arrived = round_ring(partner_sums)
     first = add(first, first_got)
     second = add(kept_keep[3], got_keep[3], partner[3], *arrived)
 

time: 155 us -> 153 us (0.987)
  starting transfers between devices: 48 us -> 42.6 us
  waiting for transfers between devices: 74.3 us -> 77.1 us
    ppermute x9, starting transfers between devices: 19 us -> 13.9 us  [swap_cores(): lax.ppermute(values, 'fsdp', [(i, i ^ 1) for i in range(CORES * RING)])]
    ppermute x3, waiting for transfers between devices: 7.14 us -> 10.3 us  [swap_pair(): return lax.ppermute(values, 'mat', [(i, i ^ 1) for i in range(MEMBERS)])]
  transfers between devices with their start and end apart: 26 -> 26, of which waited for: 13 -> 13; matrix products, arithmetic and copies ran while one was open for 4% -> 4% of each run, Pallas kernels for 1% -> 2%
where the time goes in v5:
time: 153 us
  waiting for transfers between devices  77.1 us (50%)
  starting transfers between devices  42.6 us (28%)
  Pallas kernels  25.3 us (17%)
  other arithmetic  5.8 us (4%)
    all_to_all x1, waiting for transfers between devices, shards(): columns = lax.all_to_all(blended.reshape(MEMBERS, HALF, LANES), 'mat', 0, 0)  26 us
    all_to_all x1, waiting for transfers between devices, shards(): returned = lax.all_to_all(update, 'mat', 0, 0)  24.4 us
    ppermute x12, starting transfers between devices, shift(): lax.ppermute(values, 'fsdp', [(i, (i + CORES * distance) % size) for i in...  15.7 us
    pallas_call x1, Pallas kernels, newton_step(): pl.pallas_call(functools.partial(step_kernel, layout), in_specs=[SCALARS,...  15.3 us
    ppermute x12, waiting for transfers between devices, shift(): lax.ppermute(values, 'fsdp', [(i, (i + CORES * distance) % size) for i in...  14.7 us
    ppermute x9, starting transfers between devices, swap_cores(): lax.ppermute(values, 'fsdp', [(i, i ^ 1) for i in range(CORES * RING)])  13.9 us
    ppermute x3, waiting for transfers between devices, swap_pair(): return lax.ppermute(values, 'mat', [(i, i ^ 1) for i in range(MEMBERS)])  10.3 us
    all_to_all x1, starting transfers between devices, shards(): columns = lax.all_to_all(blended.reshape(MEMBERS, HALF, LANES), 'mat', 0, 0)  8.44 us
  transfers between devices with their start and end apart: 26, of which 13 were waited for; matrix products, arithmetic and copies ran while one was open for 4% of the time, Pallas kernels for 2%

profile of v5, /device:TPU:1, one launch (start us, length us, event | category | flops | bytes accessed | tf_op | source)
XLA Modules:
  0.0 152.6 jit_solution(10305577077440620311)
XLA Ops:
  0.6 3.9 %shard_map.50 = bf16[8,896,128]{2,1,0:T(8,128)(2,1)} custom-call(f32[8,128,896]{2,1,0:T(8,128)} %momentum_ref.1, bf16[8,128,896]{2,1,0:T(8,128)(2,1)} %gradient_ref.1), custom_call_target="tpu_custom_call" | custom-call | tf_op jit(solution)/shard_map/pallas_call | solution.py:58
  4.6 0.0 copy-start.1
  4.6 8.4 %all-to-all-start = ((bf16[16,448,128]{2,1,0:T(8,128)(2,1)}), bf16[16,448,128]{2,1,0:T(8,128)(2,1)S(1)}, u32[]{:S(2)}, u32[]{:S(2)}) async-start(bf16[16,448,128]{2,1,0:T(8,128)(2,1)} %bitcast.46), calls=%async_computation | async-start | bytes 3670016 | tf_op jit(solution)/shard_map/all_to_all | solution.py:273
  13.1 0.6 gather_fusion
  13.7 0.1 add_add_fusion
  13.8 26.0 %all-to-all-done.columns_ref = bf16[16,448,128]{2,1,0:T(8,128)(2,1)S(1)} async-done(((bf16[16,448,128]{2,1,0:T(8,128)(2,1)}), bf16[16,448,128]{2,1,0:T(8,128)(2,1)S(1)}, u32[]{:S(2)}, u32[]{:S(2)}) %all-to-all-start) | async-done | bytes 1835040 | tf_op jit(solution)/shard_map/all_to_all | solution.py:273
  39.8 2.0 %shard_map.52 = (bf16[4,64,2176]{2,1,0:T(8,128)(2,1)S(1)}, bf16[4,32,2176]{2,1,0:T(8,128)(2,1)S(1)}, bf16[4,32,2176]{2,1,0:T(8,128)(2,1)S(1)}) custom-call(s32[6]{0:T(128)S(1)} %get-tuple-element.21.where_ref, bf16[16,448,128]{2,1,0:T(8,128)(2,1)S(1)} %all-to-all-done.columns_ref), custom_call_target="tpu_custom_call" | custom-call | flops 2281701376 | bytes 8000000 | tf_op jit(solution)/shard_map/pallas_call | solution.py:104
  41.8 2.2 %collective-permute-start.7 = (bf16[4,32,2176]{2,1,0:T(8,128)(2,1)S(1)}, bf16[4,32,2176]{2,1,0:T(8,128)(2,1)S(1)}, u32[]{:S(2)}, u32[]{:S(2)}) collective-permute-start(bf16[4,32,2176]{2,1,0:T(8,128)(2,1)S(1)} %get-tuple-element.13), channel_id=1, source_target_pairs={{0,16},{16,0},{32,48},{48,32},{64,80},{80,64},{96,112},{112,96},{1... | collective-permute-start | bytes 1671176 | tf_op jit(solution)/shard_map/ppermute | solution.py:256
  44.0 0.1 collective-permute-start
  44.1 0.4 collective-permute-start.6
  44.5 2.0 %shard_map.51 = (bf16[4,64,2176]{2,1,0:T(8,128)(2,1)S(1)}, bf16[4,32,2176]{2,1,0:T(8,128)(2,1)S(1)}, bf16[4,32,2176]{2,1,0:T(8,128)(2,1)S(1)}) custom-call(s32[6]{0:T(128)S(1)} %get-tuple-element.20.where_ref, bf16[16,448,128]{2,1,0:T(8,128)(2,1)S(1)} %all-to-all-done.columns_ref), custom_call_target="tpu_custom_call" | custom-call | flops 2281701376 | bytes 8000000 | tf_op jit(solution)/shard_map/pallas_call | solution.py:104
  46.6 0.1 add_convert_fusion
  46.7 0.1 collective-permute-start.8
  46.8 0.4 collective-permute-done
  47.2 0.2 fusion.3
  47.4 3.0 %collective-permute-start.1 = (bf16[64,2176]{1,0:T(8,128)(2,1)S(1)}, bf16[64,2176]{1,0:T(8,128)(2,1)S(1)}, u32[]{:S(2)}, u32[]{:S(2)}) collective-permute-start(bf16[64,2176]{1,0:T(8,128)(2,1)S(1)} %get-tuple-element.14), channel_id=1, source_target_pairs={{0,64},{16,80},{32,96},{48,112},{64,0},{80,16},{96,32},{112,48},{1... | collective-permute-start | bytes 835592 | tf_op jit(solution)/shard_map/ppermute | solution.py:261
  50.4 0.8 collective-permute-start.3
  51.2 0.7 collective-permute-start.2
  51.9 0.0 collective-permute-done.6
  51.9 9.1 %collective-permute-done.8 = bf16[4,32,2176]{2,1,0:T(8,128)(2,1)S(1)} collective-permute-done((bf16[4,32,2176]{2,1,0:T(8,128)(2,1)S(1)}, bf16[4,32,2176]{2,1,0:T(8,128)(2,1)S(1)}, u32[]{:S(2)}, u32[]{:S(2)}) %collective-permute-start.8) | collective-permute-done | bytes 557088 | tf_op jit(solution)/shard_map/ppermute | solution.py:265
  61.0 0.2 fusion.9
  61.1 3.0 %collective-permute-start.9 = (bf16[32,2176]{1,0:T(8,128)(2,1)S(1)}, bf16[32,2176]{1,0:T(8,128)(2,1)S(1)}, u32[]{:S(2)}, u32[]{:S(2)}) collective-permute-start(bf16[32,2176]{1,0:T(8,128)(2,1)S(1)} %get-tuple-element.17), channel_id=1, source_target_pairs={{0,64},{16,80},{32,96},{48,112},{64,0},{80,16},{96,32},{112,48},{1... | collective-permute-start | bytes 417800 | tf_op jit(solution)/shard_map/ppermute | solution.py:261
  64.1 0.8 collective-permute-start.11
  64.9 0.7 collective-permute-start.10
  65.6 0.0 collective-permute-done.3
  65.6 0.0 collective-permute-done.2
  65.6 0.2 fusion.2
  65.8 0.3 collective-permute-start.4
  66.1 1.0 collective-permute-done.9
  67.0 3.4 %collective-permute-done.11 = bf16[32,2176]{1,0:T(8,128)(2,1)S(1)} collective-permute-done((bf16[32,2176]{1,0:T(8,128)(2,1)S(1)}, bf16[32,2176]{1,0:T(8,128)(2,1)S(1)}, u32[]{:S(2)}, u32[]{:S(2)}) %collective-permute-start.11) | collective-permute-done | bytes 139296 | tf_op jit(solution)/shard_map/ppermute | solution.py:261
  70.4 0.0 collective-permute-done.10
  70.4 0.1 fusion.8.refs_0_
  70.5 3.5 %collective-permute-start.14 = (bf16[32,2176]{1,0:T(8,128)(2,1)S(1)}, bf16[32,2176]{1,0:T(8,128)(2,1)S(1)}, u32[]{:S(2)}, u32[]{:S(2)}) collective-permute-start(bf16[32,2176]{1,0:T(8,128)(2,1)S(1)} %fusion.8.refs_0_), channel_id=1, source_target_pairs={{0,96},{16,112},{32,0},{48,16},{64,32},{80,48},{96,64},{112,80},{1... | collective-permute-start | bytes 417800 | tf_op jit(solution)/shard_map/ppermute | solution.py:261
  74.0 0.0 collective-permute-start.13
  74.0 1.4 collective-permute-start.12
  75.5 0.9 collective-permute-done.14.refs_3_
  76.3 6.7 %collective-permute-done.13.refs_2_ = bf16[32,2176]{1,0:T(8,128)(2,1)S(1)} collective-permute-done((bf16[32,2176]{1,0:T(8,128)(2,1)S(1)}, bf16[32,2176]{1,0:T(8,128)(2,1)S(1)}, u32[]{:S(2)}, u32[]{:S(2)}) %collective-permute-start.13) | collective-permute-done | bytes 139296 | tf_op jit(solution)/shard_map/ppermute | solution.py:261
  83.0 0.6 shard_map.53.refs_2_
  83.6 0.5 collective-permute-start.22
  84.2 0.0 collective-permute-done.4
  84.2 0.1 add_convert_fusion.1.refs_0_
  84.2 0.1 collective-permute-start.20
  84.3 1.5 collective-permute-start.18
  85.8 2.1 %collective-permute-start.15 = (bf16[128,2176]{1,0:T(8,128)(2,1)S(1)}, bf16[128,2176]{1,0:T(8,128)(2,1)S(1)}, u32[]{:S(2)}, u32[]{:S(2)}) collective-permute-start(bf16[128,2176]{1,0:T(8,128)(2,1)S(1)} %shard_map.53.refs_2_), channel_id=1, source_target_pairs={{0,16},{16,0},{32,48},{48,32},{64,80},{80,64},{96,112},{112,96},{1... | collective-permute-start | bytes 1671176 | tf_op jit(solution)/shard_map/ppermute | solution.py:256
  87.9 0.3 collective-permute-start.16
  88.2 2.8 %collective-permute-done.20.refs_8_ = bf16[64,2176]{1,0:T(8,128)(2,1)S(1)} collective-permute-done((bf16[64,2176]{1,0:T(8,128)(2,1)S(1)}, bf16[64,2176]{1,0:T(8,128)(2,1)S(1)}, u32[]{:S(2)}, u32[]{:S(2)}) %collective-permute-start.20) | collective-permute-done | bytes 278560 | tf_op jit(solution)/shard_map/ppermute | solution.py:261
  90.9 4.5 %collective-permute-start.5 = (bf16[64,2176]{1,0:T(8,128)(2,1)S(1)}, bf16[64,2176]{1,0:T(8,128)(2,1)S(1)}, u32[]{:S(2)}, u32[]{:S(2)}) collective-permute-start(bf16[64,2176]{1,0:T(8,128)(2,1)S(1)} %add_convert_fusion.1.refs_0_), channel_id=1, source_target_pairs={{0,16},{16,0},{32,48},{48,32},{64,80},{80,64},{96,112},{112,96},{1... | collective-permute-start | bytes 835592 | tf_op jit(solution)/shard_map/ppermute | solution.py:256
  95.4 1.1 collective-permute-done.22.refs_10_
  96.6 2.2 %collective-permute-start.23 = (bf16[128,2176]{1,0:T(8,128)(2,1)S(1)}, bf16[128,2176]{1,0:T(8,128)(2,1)}, u32[]{:S(2)}, u32[]{:S(2)}) collective-permute-start(bf16[128,2176]{1,0:T(8,128)(2,1)S(1)} %collective-permute-done.22.refs_10_), channel_id=1, source_target_pairs={{0,16},{16,0},{32,48},{48,32},{64,80},{80,64},{96,112},{112,96},{1... | collective-permute-start | bytes 1671176 | tf_op jit(solution)/shard_map/ppermute | solution.py:256
  98.8 1.9 %collective-permute-start.21 = (bf16[64,2176]{1,0:T(8,128)(2,1)S(1)}, bf16[64,2176]{1,0:T(8,128)(2,1)S(1)}, u32[]{:S(2)}, u32[]{:S(2)}) collective-permute-start(bf16[64,2176]{1,0:T(8,128)(2,1)S(1)} %collective-permute-done.20.refs_8_), channel_id=1, source_target_pairs={{0,16},{16,0},{32,48},{48,32},{64,80},{80,64},{96,112},{112,96},{1... | collective-permute-start | bytes 835592 | tf_op jit(solution)/shard_map/ppermute | solution.py:256
  100.6 0.0 collective-permute-done.16.refs_4_
  100.6 0.0 collective-permute-start.19
  100.6 0.0 collective-permute-done.5.refs_1_
  100.6 0.5 collective-permute-start.17
  101.2 0.1 stack.38.where_ref
  101.3 0.0 collective-permute-done.15.refs_3_
  101.3 0.8 collective-permute-done.21.refs_9_
  102.1 0.2 collective-permute-done.19.refs_7_
  102.4 0.4 collective-permute-done.17.refs_5_
  102.8 15.3 %shard_map.54 = bf16[16,448,128]{2,1,0:T(8,128)(2,1)} custom-call(s32[48]{0:T(128)S(1)} %stack.38.where_ref, bf16[16,448,128]{2,1,0:T(8,128)(2,1)} %copy-done, bf16[64,2176]{1,0:T(8,128)(2,1)S(1)} %add_convert_fusion.1.refs_0_, bf16[64,2176]{1,0:T(8,128)(2,1)S(1)} %collective-permute-done.5.refs_1_, bf16[128,2176]{1,0:T(8,128)(2,1)S(1)} %shard_map.53.refs_2_, ...), custom_call_target="tpu_custom_call" | custom-call | flops 7516192768 | bytes 8000000 | tf_op jit(solution)/shard_map/pallas_call | solution.py:203
  118.1 3.7 %all-to-all-start.1 = ((bf16[16,448,128]{2,1,0:T(8,128)(2,1)}), bf16[16,448,128]{2,1,0:T(8,128)(2,1)S(1)}, u32[]{:S(2)}, u32[]{:S(2)}) async-start(bf16[16,448,128]{2,1,0:T(8,128)(2,1)} %shard_map.54), calls=%async_computation.1 | async-start | bytes 3670016 | tf_op jit(solution)/shard_map/all_to_all | solution.py:314
  121.8 4.9 %convert_add_fusion = f32[8,128,896]{2,1,0:T(8,128)} fusion(bf16[8,128,896]{2,1,0:T(8,128)(2,1)} %gradient_ref.1, f32[8,128,896]{2,1,0:T(8,128)} %momentum_ref.1), kind=kLoop, calls=%fused_computation.1 | loop fusion | flops 2752512 | bytes 9175040 | tf_op jit(solution)/shard_map/add | solution.py:274
  126.7 24.4 %all-to-all-done.1 = bf16[16,448,128]{2,1,0:T(8,128)(2,1)S(1)} async-done(((bf16[16,448,128]{2,1,0:T(8,128)(2,1)}), bf16[16,448,128]{2,1,0:T(8,128)(2,1)S(1)}, u32[]{:S(2)}, u32[]{:S(2)}) %all-to-all-start.1) | async-done | bytes 1835040 | tf_op jit(solution)/shard_map/all_to_all | solution.py:314
  151.1 1.4 shard_map.55
  (11 shorter events, 0.0 us)
Async XLA Ops:
  4.6 8.5 %copy-start.1 = (s32[4]{0:T(128)S(1)}, s32[4]{0:T(128)}, u32[]{:S(2)}) copy-start(s32[4]{0:T(128)} %constant.79.clone) | copy-start | bytes 52
  4.6 35.2 %all-to-all-start = ((bf16[16,448,128]{2,1,0:T(8,128)(2,1)}), bf16[16,448,128]{2,1,0:T(8,128)(2,1)S(1)}, u32[]{:S(2)}, u32[]{:S(2)}) async-start(bf16[16,448,128]{2,1,0:T(8,128)(2,1)} %bitcast.46), calls=%async_computation | async-start | bytes 3670016 | tf_op jit(solution)/shard_map/all_to_all | solution.py:273
  39.8 4.7 %copy-start = (bf16[16,448,128]{2,1,0:T(8,128)(2,1)}, bf16[16,448,128]{2,1,0:T(8,128)(2,1)S(1)}, u32[]{:S(2)}) copy-start(bf16[16,448,128]{2,1,0:T(8,128)(2,1)S(1)} %all-to-all-done.columns_ref) | copy-start | bytes 5505028
  41.8 4.8 %collective-permute-start.7 = (bf16[4,32,2176]{2,1,0:T(8,128)(2,1)S(1)}, bf16[4,32,2176]{2,1,0:T(8,128)(2,1)S(1)}, u32[]{:S(2)}, u32[]{:S(2)}) collective-permute-start(bf16[4,32,2176]{2,1,0:T(8,128)(2,1)S(1)} %get-tuple-element.13), channel_id=1, source_target_pairs={{0,16},{16,0},{32,48},{48,32},{64,80},{80,64},{96,112},{112,96},{1... | collective-permute-start | bytes 1671176 | tf_op jit(solution)/shard_map/ppermute | solution.py:256
  44.0 3.2 %collective-permute-start = (bf16[4,64,2176]{2,1,0:T(8,128)(2,1)S(1)}, bf16[4,64,2176]{2,1,0:T(8,128)(2,1)S(1)}, u32[]{:S(2)}, u32[]{:S(2)}) collective-permute-start(bf16[4,64,2176]{2,1,0:T(8,128)(2,1)S(1)} %get-tuple-element.9), channel_id=1, source_target_pairs={{0,16},{16,0},{32,48},{48,32},{64,80},{80,64},{96,112},{112,96},{1... | collective-permute-start | bytes 3342344 | tf_op jit(solution)/shard_map/ppermute | solution.py:256
  44.1 7.8 %collective-permute-start.6 = (bf16[4,32,2176]{2,1,0:T(8,128)(2,1)S(1)}, bf16[4,32,2176]{2,1,0:T(8,128)(2,1)S(1)}, u32[]{:S(2)}, u32[]{:S(2)}) collective-permute-start(bf16[4,32,2176]{2,1,0:T(8,128)(2,1)S(1)} %get-tuple-element.11), channel_id=1, source_target_pairs={{0,16},{16,0},{32,48},{48,32},{64,80},{80,64},{96,112},{112,96},{1... | collective-permute-start | bytes 1671176 | tf_op jit(solution)/shard_map/ppermute | solution.py:256
  46.7 14.3 %collective-permute-start.8 = (bf16[4,32,2176]{2,1,0:T(8,128)(2,1)S(1)}, bf16[4,32,2176]{2,1,0:T(8,128)(2,1)S(1)}, u32[]{:S(2)}, u32[]{:S(2)}) collective-permute-start(bf16[4,32,2176]{2,1,0:T(8,128)(2,1)S(1)} %add_convert_fusion), channel_id=1, source_target_pairs={{0,1},{1,0},{2,3},{3,2},{4,5},{5,4},{6,7},{7,6},{8,9},{9,8},{10,11... | collective-permute-start | bytes 1671176 | tf_op jit(solution)/shard_map/ppermute | solution.py:265
  47.4 17.5 %collective-permute-start.1 = (bf16[64,2176]{1,0:T(8,128)(2,1)S(1)}, bf16[64,2176]{1,0:T(8,128)(2,1)S(1)}, u32[]{:S(2)}, u32[]{:S(2)}) collective-permute-start(bf16[64,2176]{1,0:T(8,128)(2,1)S(1)} %get-tuple-element.14), channel_id=1, source_target_pairs={{0,64},{16,80},{32,96},{48,112},{64,0},{80,16},{96,32},{112,48},{1... | collective-permute-start | bytes 835592 | tf_op jit(solution)/shard_map/ppermute | solution.py:261
  50.4 15.2 %collective-permute-start.3 = (bf16[64,2176]{1,0:T(8,128)(2,1)S(1)}, bf16[64,2176]{1,0:T(8,128)(2,1)S(1)}, u32[]{:S(2)}, u32[]{:S(2)}) collective-permute-start(bf16[64,2176]{1,0:T(8,128)(2,1)S(1)} %get-tuple-element.15), channel_id=1, source_target_pairs={{0,96},{16,112},{32,0},{48,16},{64,32},{80,48},{96,64},{112,80},{1... | collective-permute-start | bytes 835592 | tf_op jit(solution)/shard_map/ppermute | solution.py:261
  51.2 14.4 %collective-permute-start.2 = (bf16[64,2176]{1,0:T(8,128)(2,1)S(1)}, bf16[64,2176]{1,0:T(8,128)(2,1)S(1)}, u32[]{:S(2)}, u32[]{:S(2)}) collective-permute-start(bf16[64,2176]{1,0:T(8,128)(2,1)S(1)} %get-tuple-element.16), channel_id=1, source_target_pairs={{0,32},{16,48},{32,64},{48,80},{64,96},{80,112},{96,0},{112,16},{1... | collective-permute-start | bytes 835592 | tf_op jit(solution)/shard_map/ppermute | solution.py:261
  61.1 5.9 %collective-permute-start.9 = (bf16[32,2176]{1,0:T(8,128)(2,1)S(1)}, bf16[32,2176]{1,0:T(8,128)(2,1)S(1)}, u32[]{:S(2)}, u32[]{:S(2)}) collective-permute-start(bf16[32,2176]{1,0:T(8,128)(2,1)S(1)} %get-tuple-element.17), channel_id=1, source_target_pairs={{0,64},{16,80},{32,96},{48,112},{64,0},{80,16},{96,32},{112,48},{1... | collective-permute-start | bytes 417800 | tf_op jit(solution)/shard_map/ppermute | solution.py:261
  64.1 6.3 %collective-permute-start.11 = (bf16[32,2176]{1,0:T(8,128)(2,1)S(1)}, bf16[32,2176]{1,0:T(8,128)(2,1)S(1)}, u32[]{:S(2)}, u32[]{:S(2)}) collective-permute-start(bf16[32,2176]{1,0:T(8,128)(2,1)S(1)} %get-tuple-element.18), channel_id=1, source_target_pairs={{0,96},{16,112},{32,0},{48,16},{64,32},{80,48},{96,64},{112,80},{1... | collective-permute-start | bytes 417800 | tf_op jit(solution)/shard_map/ppermute | solution.py:261
  64.9 5.5 %collective-permute-start.10 = (bf16[32,2176]{1,0:T(8,128)(2,1)S(1)}, bf16[32,2176]{1,0:T(8,128)(2,1)S(1)}, u32[]{:S(2)}, u32[]{:S(2)}) collective-permute-start(bf16[32,2176]{1,0:T(8,128)(2,1)S(1)} %get-tuple-element.19), channel_id=1, source_target_pairs={{0,32},{16,48},{32,64},{48,80},{64,96},{80,112},{96,0},{112,16},{1... | collective-permute-start | bytes 417800 | tf_op jit(solution)/shard_map/ppermute | solution.py:261
  65.8 18.4 %collective-permute-start.4 = (bf16[64,2176]{1,0:T(8,128)(2,1)S(1)}, bf16[64,2176]{1,0:T(8,128)(2,1)S(1)}, u32[]{:S(2)}, u32[]{:S(2)}) collective-permute-start(bf16[64,2176]{1,0:T(8,128)(2,1)S(1)} %fusion.2), channel_id=1, source_target_pairs={{0,1},{1,0},{2,3},{3,2},{4,5},{5,4},{6,7},{7,6},{8,9},{9,8},{10,11... | collective-permute-start | bytes 835592 | tf_op jit(solution)/shard_map/ppermute | solution.py:265
  70.5 5.8 %collective-permute-start.14 = (bf16[32,2176]{1,0:T(8,128)(2,1)S(1)}, bf16[32,2176]{1,0:T(8,128)(2,1)S(1)}, u32[]{:S(2)}, u32[]{:S(2)}) collective-permute-start(bf16[32,2176]{1,0:T(8,128)(2,1)S(1)} %fusion.8.refs_0_), channel_id=1, source_target_pairs={{0,96},{16,112},{32,0},{48,16},{64,32},{80,48},{96,64},{112,80},{1... | collective-permute-start | bytes 417800 | tf_op jit(solution)/shard_map/ppermute | solution.py:261
  74.0 9.0 %collective-permute-start.13 = (bf16[32,2176]{1,0:T(8,128)(2,1)S(1)}, bf16[32,2176]{1,0:T(8,128)(2,1)S(1)}, u32[]{:S(2)}, u32[]{:S(2)}) collective-permute-start(bf16[32,2176]{1,0:T(8,128)(2,1)S(1)} %fusion.8.refs_0_), channel_id=1, source_target_pairs={{0,32},{16,48},{32,64},{48,80},{64,96},{80,112},{96,0},{112,16},{1... | collective-permute-start | bytes 417800 | tf_op jit(solution)/shard_map/ppermute | solution.py:261
  74.0 9.0 %collective-permute-start.12 = (bf16[32,2176]{1,0:T(8,128)(2,1)S(1)}, bf16[32,2176]{1,0:T(8,128)(2,1)S(1)}, u32[]{:S(2)}, u32[]{:S(2)}) collective-permute-start(bf16[32,2176]{1,0:T(8,128)(2,1)S(1)} %fusion.8.refs_0_), channel_id=1, source_target_pairs={{0,64},{16,80},{32,96},{48,112},{64,0},{80,16},{96,32},{112,48},{1... | collective-permute-start | bytes 417800 | tf_op jit(solution)/shard_map/ppermute | solution.py:261
  83.6 12.9 %collective-permute-start.22 = (bf16[128,2176]{1,0:T(8,128)(2,1)S(1)}, bf16[128,2176]{1,0:T(8,128)(2,1)S(1)}, u32[]{:S(2)}, u32[]{:S(2)}) collective-permute-start(bf16[128,2176]{1,0:T(8,128)(2,1)S(1)} %shard_map.53.refs_2_), channel_id=1, source_target_pairs={{0,1},{1,0},{2,3},{3,2},{4,5},{5,4},{6,7},{7,6},{8,9},{9,8},{10,11... | collective-permute-start | bytes 1671176 | tf_op jit(solution)/shard_map/ppermute | solution.py:265
  84.2 6.7 %collective-permute-start.20 = (bf16[64,2176]{1,0:T(8,128)(2,1)S(1)}, bf16[64,2176]{1,0:T(8,128)(2,1)S(1)}, u32[]{:S(2)}, u32[]{:S(2)}) collective-permute-start(bf16[64,2176]{1,0:T(8,128)(2,1)S(1)} %add_convert_fusion.1.refs_0_), channel_id=1, source_target_pairs={{0,96},{16,112},{32,0},{48,16},{64,32},{80,48},{96,64},{112,80},{1... | collective-permute-start | bytes 835592 | tf_op jit(solution)/shard_map/ppermute | solution.py:261
  84.3 14.4 %collective-permute-start.18 = (bf16[64,2176]{1,0:T(8,128)(2,1)S(1)}, bf16[64,2176]{1,0:T(8,128)(2,1)S(1)}, u32[]{:S(2)}, u32[]{:S(2)}) collective-permute-start(bf16[64,2176]{1,0:T(8,128)(2,1)S(1)} %add_convert_fusion.1.refs_0_), channel_id=1, source_target_pairs={{0,32},{16,48},{32,64},{48,80},{64,96},{80,112},{96,0},{112,16},{1... | collective-permute-start | bytes 835592 | tf_op jit(solution)/shard_map/ppermute | solution.py:261
  85.8 15.5 %collective-permute-start.15 = (bf16[128,2176]{1,0:T(8,128)(2,1)S(1)}, bf16[128,2176]{1,0:T(8,128)(2,1)S(1)}, u32[]{:S(2)}, u32[]{:S(2)}) collective-permute-start(bf16[128,2176]{1,0:T(8,128)(2,1)S(1)} %shard_map.53.refs_2_), channel_id=1, source_target_pairs={{0,16},{16,0},{32,48},{48,32},{64,80},{80,64},{96,112},{112,96},{1... | collective-permute-start | bytes 1671176 | tf_op jit(solution)/shard_map/ppermute | solution.py:256
  87.9 12.8 %collective-permute-start.16 = (bf16[64,2176]{1,0:T(8,128)(2,1)S(1)}, bf16[64,2176]{1,0:T(8,128)(2,1)S(1)}, u32[]{:S(2)}, u32[]{:S(2)}) collective-permute-start(bf16[64,2176]{1,0:T(8,128)(2,1)S(1)} %add_convert_fusion.1.refs_0_), channel_id=1, source_target_pairs={{0,64},{16,80},{32,96},{48,112},{64,0},{80,16},{96,32},{112,48},{1... | collective-permute-start | bytes 835592 | tf_op jit(solution)/shard_map/ppermute | solution.py:261
  90.9 9.7 %collective-permute-start.5 = (bf16[64,2176]{1,0:T(8,128)(2,1)S(1)}, bf16[64,2176]{1,0:T(8,128)(2,1)S(1)}, u32[]{:S(2)}, u32[]{:S(2)}) collective-permute-start(bf16[64,2176]{1,0:T(8,128)(2,1)S(1)} %add_convert_fusion.1.refs_0_), channel_id=1, source_target_pairs={{0,16},{16,0},{32,48},{48,32},{64,80},{80,64},{96,112},{112,96},{1... | collective-permute-start | bytes 835592 | tf_op jit(solution)/shard_map/ppermute | solution.py:256
  96.6 6.2 %collective-permute-start.23 = (bf16[128,2176]{1,0:T(8,128)(2,1)S(1)}, bf16[128,2176]{1,0:T(8,128)(2,1)}, u32[]{:S(2)}, u32[]{:S(2)}) collective-permute-start(bf16[128,2176]{1,0:T(8,128)(2,1)S(1)} %collective-permute-done.22.refs_10_), channel_id=1, source_target_pairs={{0,16},{16,0},{32,48},{48,32},{64,80},{80,64},{96,112},{112,96},{1... | collective-permute-start | bytes 1671176 | tf_op jit(solution)/shard_map/ppermute | solution.py:256
  98.8 3.4 %collective-permute-start.21 = (bf16[64,2176]{1,0:T(8,128)(2,1)S(1)}, bf16[64,2176]{1,0:T(8,128)(2,1)S(1)}, u32[]{:S(2)}, u32[]{:S(2)}) collective-permute-start(bf16[64,2176]{1,0:T(8,128)(2,1)S(1)} %collective-permute-done.20.refs_8_), channel_id=1, source_target_pairs={{0,16},{16,0},{32,48},{48,32},{64,80},{80,64},{96,112},{112,96},{1... | collective-permute-start | bytes 835592 | tf_op jit(solution)/shard_map/ppermute | solution.py:256
  100.6 1.7 %collective-permute-start.19 = (bf16[64,2176]{1,0:T(8,128)(2,1)S(1)}, bf16[64,2176]{1,0:T(8,128)(2,1)}, u32[]{:S(2)}, u32[]{:S(2)}) collective-permute-start(bf16[64,2176]{1,0:T(8,128)(2,1)S(1)} %collective-permute-done.18.refs_6_), channel_id=1, source_target_pairs={{0,16},{16,0},{32,48},{48,32},{64,80},{80,64},{96,112},{112,96},{1... | collective-permute-start | bytes 835592 | tf_op jit(solution)/shard_map/ppermute | solution.py:256
  100.6 2.1 %collective-permute-start.17 = (bf16[64,2176]{1,0:T(8,128)(2,1)S(1)}, bf16[64,2176]{1,0:T(8,128)(2,1)}, u32[]{:S(2)}, u32[]{:S(2)}) collective-permute-start(bf16[64,2176]{1,0:T(8,128)(2,1)S(1)} %collective-permute-done.16.refs_4_), channel_id=1, source_target_pairs={{0,16},{16,0},{32,48},{48,32},{64,80},{80,64},{96,112},{112,96},{1... | collective-permute-start | bytes 835592 | tf_op jit(solution)/shard_map/ppermute | solution.py:256
  118.1 33.0 %all-to-all-start.1 = ((bf16[16,448,128]{2,1,0:T(8,128)(2,1)}), bf16[16,448,128]{2,1,0:T(8,128)(2,1)S(1)}, u32[]{:S(2)}, u32[]{:S(2)}) async-start(bf16[16,448,128]{2,1,0:T(8,128)(2,1)} %shard_map.54), calls=%async_computation.1 | async-start | bytes 3670016 | tf_op jit(solution)/shard_map/all_to_all | solution.py:314

commit v6 on v5

--- a/solution.py
+++ b/solution.py
@@ -280,13 +280,13 @@
     got_give, got_ring, got_keep = swap_cores(away[1]), swap_cores(away[0]), swap_cores(away[2])
 
     def round_ring(pieces):
-        return [shift(values, distance) for values, distance in zip(pieces, (2, 1, 3))]
-
-    ring_sums = [add(kept_ring[slot], got_ring[slot]) for slot in range(3)]
+        return [shift(values, distance) for values, distance in zip(pieces, (1, 3, 2))]
+
+    ring_sums = [add(kept_ring[slot], got_ring[slot]) for slot in (1, 2, 0)]
     partner = swap_pair(add(kept_give, got_give))
     arrived = round_ring(ring_sums)
     first = add(kept_ring[3], got_ring[3], *arrived)
-    partner_sums = [add(kept_keep[slot], got_keep[slot], partner[slot]) for slot in range(3)]
+    partner_sums = [add(kept_keep[slot], got_keep[slot], partner[slot]) for slot in (1, 2, 0)]
     first_got = swap_pair(first)
     arrived = round_ring(partner_sums)
     first = add(first, first_got)
@@ -303,7 +303,7 @@
                 where.extend([half * RING + chunk, offset])
             pieces.append(values)
 
-    order = [place_y, far, behind, ahead]
+    order = [place_y, behind, ahead, far]
     take(first, HALVES, order[:1], 0)
     take(second, QUARTER, order, HALVES + side * QUARTER)
     for values, chunk in zip(round_ring([first] * 3), order[1:]):

time: 153 us -> 151 us (0.987)
  waiting for transfers between devices: 77.1 us -> 73 us
  starting transfers between devices: 42.6 us -> 44.8 us
    ppermute x12, waiting for transfers between devices: 14.7 us -> 12 us  [shift(): lax.ppermute(values, 'fsdp', [(i, (i + CORES * distance) % size) for i in...]
    ppermute x12, starting transfers between devices: 15.7 us -> 17.7 us  [shift(): lax.ppermute(values, 'fsdp', [(i, (i + CORES * distance) % size) for i in...]
    ppermute x3, waiting for transfers between devices: 10.3 us -> 8.52 us  [swap_pair(): return lax.ppermute(values, 'mat', [(i, i ^ 1) for i in range(MEMBERS)])]
  transfers between devices with their start and end apart: 26 -> 26, of which waited for: 13 -> 14; matrix products, arithmetic and copies ran while one was open for 4% -> 4% of each run, Pallas kernels for 2% -> 2%
where the time goes in v6:
time: 151 us
  waiting for transfers between devices  73 us (48%)
  starting transfers between devices  44.8 us (30%)
  Pallas kernels  25.3 us (17%)
  other arithmetic  5.8 us (4%)
    all_to_all x1, waiting for transfers between devices, shards(): columns = lax.all_to_all(blended.reshape(MEMBERS, HALF, LANES), 'mat', 0, 0)  26 us
    all_to_all x1, waiting for transfers between devices, shards(): returned = lax.all_to_all(update, 'mat', 0, 0)  24.5 us
    ppermute x12, starting transfers between devices, shift(): lax.ppermute(values, 'fsdp', [(i, (i + CORES * distance) % size) for i in...  17.7 us
    pallas_call x1, Pallas kernels, newton_step(): pl.pallas_call(functools.partial(step_kernel, layout), in_specs=[SCALARS,...  15.3 us
    ppermute x9, starting transfers between devices, swap_cores(): lax.ppermute(values, 'fsdp', [(i, i ^ 1) for i in range(CORES * RING)])  14.1 us
    ppermute x12, waiting for transfers between devices, shift(): lax.ppermute(values, 'fsdp', [(i, (i + CORES * distance) % size) for i in...  12 us
    ppermute x3, waiting for transfers between devices, swap_pair(): return lax.ppermute(values, 'mat', [(i, i ^ 1) for i in range(MEMBERS)])  8.52 us
    all_to_all x1, starting transfers between devices, shards(): columns = lax.all_to_all(blended.reshape(MEMBERS, HALF, LANES), 'mat', 0, 0)  8.44 us
  transfers between devices with their start and end apart: 26, of which 14 were waited for; matrix products, arithmetic and copies ran while one was open for 4% of the time, Pallas kernels for 2%

profile of v6, /device:TPU:1, one launch (start us, length us, event | category | flops | bytes accessed | tf_op | source)
XLA Modules:
  0.0 150.6 jit_solution(4663626640381262766)
XLA Ops:
  0.6 3.9 %shard_map.50 = bf16[8,896,128]{2,1,0:T(8,128)(2,1)} custom-call(f32[8,128,896]{2,1,0:T(8,128)} %momentum_ref.1, bf16[8,128,896]{2,1,0:T(8,128)(2,1)} %gradient_ref.1), custom_call_target="tpu_custom_call" | custom-call | tf_op jit(solution)/shard_map/pallas_call | solution.py:58
  4.6 0.0 copy-start.1
  4.6 8.4 %all-to-all-start = ((bf16[16,448,128]{2,1,0:T(8,128)(2,1)}), bf16[16,448,128]{2,1,0:T(8,128)(2,1)S(1)}, u32[]{:S(2)}, u32[]{:S(2)}) async-start(bf16[16,448,128]{2,1,0:T(8,128)(2,1)} %bitcast.46), calls=%async_computation | async-start | bytes 3670016 | tf_op jit(solution)/shard_map/all_to_all | solution.py:273
  13.1 0.6 gather_fusion
  13.7 0.1 add_add_fusion
  13.8 26.0 %all-to-all-done.columns_ref = bf16[16,448,128]{2,1,0:T(8,128)(2,1)S(1)} async-done(((bf16[16,448,128]{2,1,0:T(8,128)(2,1)}), bf16[16,448,128]{2,1,0:T(8,128)(2,1)S(1)}, u32[]{:S(2)}, u32[]{:S(2)}) %all-to-all-start) | async-done | bytes 1835040 | tf_op jit(solution)/shard_map/all_to_all | solution.py:273
  39.8 2.0 %shard_map.52 = (bf16[4,64,2176]{2,1,0:T(8,128)(2,1)S(1)}, bf16[4,32,2176]{2,1,0:T(8,128)(2,1)S(1)}, bf16[4,32,2176]{2,1,0:T(8,128)(2,1)S(1)}) custom-call(s32[6]{0:T(128)S(1)} %get-tuple-element.21.where_ref, bf16[16,448,128]{2,1,0:T(8,128)(2,1)S(1)} %all-to-all-done.columns_ref), custom_call_target="tpu_custom_call" | custom-call | flops 2281701376 | bytes 8000000 | tf_op jit(solution)/shard_map/pallas_call | solution.py:104
  41.8 2.2 %collective-permute-start.7 = (bf16[4,32,2176]{2,1,0:T(8,128)(2,1)S(1)}, bf16[4,32,2176]{2,1,0:T(8,128)(2,1)S(1)}, u32[]{:S(2)}, u32[]{:S(2)}) collective-permute-start(bf16[4,32,2176]{2,1,0:T(8,128)(2,1)S(1)} %get-tuple-element.13), channel_id=1, source_target_pairs={{0,16},{16,0},{32,48},{48,32},{64,80},{80,64},{96,112},{112,96},{1... | collective-permute-start | bytes 1671176 | tf_op jit(solution)/shard_map/ppermute | solution.py:256
  44.0 0.1 collective-permute-start
  44.1 0.4 collective-permute-start.6
  44.5 2.0 %shard_map.51 = (bf16[4,64,2176]{2,1,0:T(8,128)(2,1)S(1)}, bf16[4,32,2176]{2,1,0:T(8,128)(2,1)S(1)}, bf16[4,32,2176]{2,1,0:T(8,128)(2,1)S(1)}) custom-call(s32[6]{0:T(128)S(1)} %get-tuple-element.20.where_ref, bf16[16,448,128]{2,1,0:T(8,128)(2,1)S(1)} %all-to-all-done.columns_ref), custom_call_target="tpu_custom_call" | custom-call | flops 2281701376 | bytes 8000000 | tf_op jit(solution)/shard_map/pallas_call | solution.py:104
  46.6 0.1 add_convert_fusion
  46.7 0.1 collective-permute-start.8
  46.8 0.4 collective-permute-done
  47.2 0.2 fusion.3
  47.4 1.4 collective-permute-start.1
  48.8 2.6 %collective-permute-start.3 = (bf16[64,2176]{1,0:T(8,128)(2,1)S(1)}, bf16[64,2176]{1,0:T(8,128)(2,1)S(1)}, u32[]{:S(2)}, u32[]{:S(2)}) collective-permute-start(bf16[64,2176]{1,0:T(8,128)(2,1)S(1)} %get-tuple-element.15), channel_id=1, source_target_pairs={{0,64},{16,80},{32,96},{48,112},{64,0},{80,16},{96,32},{112,48},{1... | collective-permute-start | bytes 835592 | tf_op jit(solution)/shard_map/ppermute | solution.py:261
  51.4 1.1 collective-permute-start.2
  52.5 0.0 collective-permute-done.6
  52.5 8.5 %collective-permute-done.8 = bf16[4,32,2176]{2,1,0:T(8,128)(2,1)S(1)} collective-permute-done((bf16[4,32,2176]{2,1,0:T(8,128)(2,1)S(1)}, bf16[4,32,2176]{2,1,0:T(8,128)(2,1)S(1)}, u32[]{:S(2)}, u32[]{:S(2)}) %collective-permute-start.8) | collective-permute-done | bytes 557088 | tf_op jit(solution)/shard_map/ppermute | solution.py:265
  61.0 0.2 fusion.9
  61.1 1.4 collective-permute-start.9
  62.5 2.6 %collective-permute-start.11 = (bf16[32,2176]{1,0:T(8,128)(2,1)S(1)}, bf16[32,2176]{1,0:T(8,128)(2,1)S(1)}, u32[]{:S(2)}, u32[]{:S(2)}) collective-permute-start(bf16[32,2176]{1,0:T(8,128)(2,1)S(1)} %get-tuple-element.18), channel_id=1, source_target_pairs={{0,64},{16,80},{32,96},{48,112},{64,0},{80,16},{96,32},{112,48},{1... | collective-permute-start | bytes 417800 | tf_op jit(solution)/shard_map/ppermute | solution.py:261
  65.1 0.0 collective-permute-done.1
  65.1 1.1 collective-permute-start.10
  66.2 0.0 collective-permute-done.3
  66.2 0.0 collective-permute-done.2
  66.2 0.2 fusion.2
  66.4 0.3 collective-permute-start.4
  66.7 0.2 collective-permute-done.9
  66.9 4.1 %collective-permute-done.11 = bf16[32,2176]{1,0:T(8,128)(2,1)S(1)} collective-permute-done((bf16[32,2176]{1,0:T(8,128)(2,1)S(1)}, bf16[32,2176]{1,0:T(8,128)(2,1)S(1)}, u32[]{:S(2)}, u32[]{:S(2)}) %collective-permute-start.11) | collective-permute-done | bytes 139296 | tf_op jit(solution)/shard_map/ppermute | solution.py:261
  71.0 0.0 collective-permute-done.10
  71.0 0.1 fusion.8.refs_0_
  71.1 2.1 %collective-permute-start.14 = (bf16[32,2176]{1,0:T(8,128)(2,1)S(1)}, bf16[32,2176]{1,0:T(8,128)(2,1)S(1)}, u32[]{:S(2)}, u32[]{:S(2)}) collective-permute-start(bf16[32,2176]{1,0:T(8,128)(2,1)S(1)} %fusion.8.refs_0_), channel_id=1, source_target_pairs={{0,64},{16,80},{32,96},{48,112},{64,0},{80,16},{96,32},{112,48},{1... | collective-permute-start | bytes 417800 | tf_op jit(solution)/shard_map/ppermute | solution.py:261
  73.2 1.6 %collective-permute-start.13 = (bf16[32,2176]{1,0:T(8,128)(2,1)S(1)}, bf16[32,2176]{1,0:T(8,128)(2,1)S(1)}, u32[]{:S(2)}, u32[]{:S(2)}) collective-permute-start(bf16[32,2176]{1,0:T(8,128)(2,1)S(1)} %fusion.8.refs_0_), channel_id=1, source_target_pairs={{0,96},{16,112},{32,0},{48,16},{64,32},{80,48},{96,64},{112,80},{1... | collective-permute-start | bytes 417800 | tf_op jit(solution)/shard_map/ppermute | solution.py:261
  74.8 0.0 collective-permute-start.12
  74.8 1.8 %collective-permute-done.14.refs_3_ = bf16[32,2176]{1,0:T(8,128)(2,1)S(1)} collective-permute-done((bf16[32,2176]{1,0:T(8,128)(2,1)S(1)}, bf16[32,2176]{1,0:T(8,128)(2,1)S(1)}, u32[]{:S(2)}, u32[]{:S(2)}) %collective-permute-start.14) | collective-permute-done | bytes 139296 | tf_op jit(solution)/shard_map/ppermute | solution.py:261
  76.6 2.7 %collective-permute-done.13.refs_2_ = bf16[32,2176]{1,0:T(8,128)(2,1)S(1)} collective-permute-done((bf16[32,2176]{1,0:T(8,128)(2,1)S(1)}, bf16[32,2176]{1,0:T(8,128)(2,1)S(1)}, u32[]{:S(2)}, u32[]{:S(2)}) %collective-permute-start.13) | collective-permute-done | bytes 139296 | tf_op jit(solution)/shard_map/ppermute | solution.py:261
  79.3 1.5 collective-permute-done.12.refs_1_
  80.8 0.6 shard_map.53.refs_2_
  81.4 0.4 collective-permute-start.22
  81.9 0.1 add_convert_fusion.1.refs_0_
  81.9 1.4 collective-permute-start.20
  83.4 2.4 %collective-permute-start.18 = (bf16[64,2176]{1,0:T(8,128)(2,1)S(1)}, bf16[64,2176]{1,0:T(8,128)(2,1)S(1)}, u32[]{:S(2)}, u32[]{:S(2)}) collective-permute-start(bf16[64,2176]{1,0:T(8,128)(2,1)S(1)} %add_convert_fusion.1.refs_0_), channel_id=1, source_target_pairs={{0,96},{16,112},{32,0},{48,16},{64,32},{80,48},{96,64},{112,80},{1... | collective-permute-start | bytes 835592 | tf_op jit(solution)/shard_map/ppermute | solution.py:261
  85.8 1.7 %collective-permute-start.15 = (bf16[128,2176]{1,0:T(8,128)(2,1)S(1)}, bf16[128,2176]{1,0:T(8,128)(2,1)S(1)}, u32[]{:S(2)}, u32[]{:S(2)}) collective-permute-start(bf16[128,2176]{1,0:T(8,128)(2,1)S(1)} %shard_map.53.refs_2_), channel_id=1, source_target_pairs={{0,16},{16,0},{32,48},{48,32},{64,80},{80,64},{96,112},{112,96},{1... | collective-permute-start | bytes 1671176 | tf_op jit(solution)/shard_map/ppermute | solution.py:256
  87.5 1.4 collective-permute-done.20.refs_8_
  88.9 5.1 %collective-permute-start.5 = (bf16[64,2176]{1,0:T(8,128)(2,1)S(1)}, bf16[64,2176]{1,0:T(8,128)(2,1)S(1)}, u32[]{:S(2)}, u32[]{:S(2)}) collective-permute-start(bf16[64,2176]{1,0:T(8,128)(2,1)S(1)} %add_convert_fusion.1.refs_0_), channel_id=1, source_target_pairs={{0,16},{16,0},{32,48},{48,32},{64,80},{80,64},{96,112},{112,96},{1... | collective-permute-start | bytes 835592 | tf_op jit(solution)/shard_map/ppermute | solution.py:256
  94.0 0.0 collective-permute-done.22.refs_10_
  94.0 2.5 %collective-permute-start.23 = (bf16[128,2176]{1,0:T(8,128)(2,1)S(1)}, bf16[128,2176]{1,0:T(8,128)(2,1)}, u32[]{:S(2)}, u32[]{:S(2)}) collective-permute-start(bf16[128,2176]{1,0:T(8,128)(2,1)S(1)} %collective-permute-done.22.refs_10_), channel_id=1, source_target_pairs={{0,16},{16,0},{32,48},{48,32},{64,80},{80,64},{96,112},{112,96},{1... | collective-permute-start | bytes 1671176 | tf_op jit(solution)/shard_map/ppermute | solution.py:256
  96.5 0.0 collective-permute-done.18.refs_6_
  96.5 1.4 collective-permute-start.21
  97.9 0.3 collective-permute-done.16.refs_4_
  98.2 0.6 collective-permute-start.19
  98.9 0.0 collective-permute-done.5.refs_1_
  98.9 0.0 collective-permute-start.17
  98.9 0.1 stack.38.where_ref
  99.0 0.1 collective-permute-done.21.refs_9_
  99.1 1.1 collective-permute-done.19.refs_7_
  100.2 0.4 collective-permute-done.17.refs_5_
  100.6 15.3 %shard_map.54 = bf16[16,448,128]{2,1,0:T(8,128)(2,1)} custom-call(s32[48]{0:T(128)S(1)} %stack.38.where_ref, bf16[16,448,128]{2,1,0:T(8,128)(2,1)} %copy-done, bf16[64,2176]{1,0:T(8,128)(2,1)S(1)} %add_convert_fusion.1.refs_0_, bf16[64,2176]{1,0:T(8,128)(2,1)S(1)} %collective-permute-done.5.refs_1_, bf16[128,2176]{1,0:T(8,128)(2,1)S(1)} %shard_map.53.refs_2_, ...), custom_call_target="tpu_custom_call" | custom-call | flops 7516192768 | bytes 8000000 | tf_op jit(solution)/shard_map/pallas_call | solution.py:203
  115.9 3.7 %all-to-all-start.1 = ((bf16[16,448,128]{2,1,0:T(8,128)(2,1)}), bf16[16,448,128]{2,1,0:T(8,128)(2,1)S(1)}, u32[]{:S(2)}, u32[]{:S(2)}) async-start(bf16[16,448,128]{2,1,0:T(8,128)(2,1)} %shard_map.54), calls=%async_computation.1 | async-start | bytes 3670016 | tf_op jit(solution)/shard_map/all_to_all | solution.py:314
  119.7 4.9 %convert_add_fusion = f32[8,128,896]{2,1,0:T(8,128)} fusion(bf16[8,128,896]{2,1,0:T(8,128)(2,1)} %gradient_ref.1, f32[8,128,896]{2,1,0:T(8,128)} %momentum_ref.1), kind=kLoop, calls=%fused_computation.1 | loop fusion | flops 2752512 | bytes 9175040 | tf_op jit(solution)/shard_map/add | solution.py:274
  124.5 24.5 %all-to-all-done.1 = bf16[16,448,128]{2,1,0:T(8,128)(2,1)S(1)} async-done(((bf16[16,448,128]{2,1,0:T(8,128)(2,1)}), bf16[16,448,128]{2,1,0:T(8,128)(2,1)S(1)}, u32[]{:S(2)}, u32[]{:S(2)}) %all-to-all-start.1) | async-done | bytes 1835040 | tf_op jit(solution)/shard_map/all_to_all | solution.py:314
  149.0 1.4 shard_map.55
  (11 shorter events, 0.0 us)
Async XLA Ops:
  4.6 8.5 %copy-start.1 = (s32[4]{0:T(128)S(1)}, s32[4]{0:T(128)}, u32[]{:S(2)}) copy-start(s32[4]{0:T(128)} %constant.79.clone) | copy-start | bytes 52
  4.6 35.2 %all-to-all-start = ((bf16[16,448,128]{2,1,0:T(8,128)(2,1)}), bf16[16,448,128]{2,1,0:T(8,128)(2,1)S(1)}, u32[]{:S(2)}, u32[]{:S(2)}) async-start(bf16[16,448,128]{2,1,0:T(8,128)(2,1)} %bitcast.46), calls=%async_computation | async-start | bytes 3670016 | tf_op jit(solution)/shard_map/all_to_all | solution.py:273
  39.8 4.7 %copy-start = (bf16[16,448,128]{2,1,0:T(8,128)(2,1)}, bf16[16,448,128]{2,1,0:T(8,128)(2,1)S(1)}, u32[]{:S(2)}) copy-start(bf16[16,448,128]{2,1,0:T(8,128)(2,1)S(1)} %all-to-all-done.columns_ref) | copy-start | bytes 5505028
  41.8 4.8 %collective-permute-start.7 = (bf16[4,32,2176]{2,1,0:T(8,128)(2,1)S(1)}, bf16[4,32,2176]{2,1,0:T(8,128)(2,1)S(1)}, u32[]{:S(2)}, u32[]{:S(2)}) collective-permute-start(bf16[4,32,2176]{2,1,0:T(8,128)(2,1)S(1)} %get-tuple-element.13), channel_id=1, source_target_pairs={{0,16},{16,0},{32,48},{48,32},{64,80},{80,64},{96,112},{112,96},{1... | collective-permute-start | bytes 1671176 | tf_op jit(solution)/shard_map/ppermute | solution.py:256
  44.0 3.2 %collective-permute-start = (bf16[4,64,2176]{2,1,0:T(8,128)(2,1)S(1)}, bf16[4,64,2176]{2,1,0:T(8,128)(2,1)S(1)}, u32[]{:S(2)}, u32[]{:S(2)}) collective-permute-start(bf16[4,64,2176]{2,1,0:T(8,128)(2,1)S(1)} %get-tuple-element.9), channel_id=1, source_target_pairs={{0,16},{16,0},{32,48},{48,32},{64,80},{80,64},{96,112},{112,96},{1... | collective-permute-start | bytes 3342344 | tf_op jit(solution)/shard_map/ppermute | solution.py:256
  44.1 8.3 %collective-permute-start.6 = (bf16[4,32,2176]{2,1,0:T(8,128)(2,1)S(1)}, bf16[4,32,2176]{2,1,0:T(8,128)(2,1)S(1)}, u32[]{:S(2)}, u32[]{:S(2)}) collective-permute-start(bf16[4,32,2176]{2,1,0:T(8,128)(2,1)S(1)} %get-tuple-element.11), channel_id=1, source_target_pairs={{0,16},{16,0},{32,48},{48,32},{64,80},{80,64},{96,112},{112,96},{1... | collective-permute-start | bytes 1671176 | tf_op jit(solution)/shard_map/ppermute | solution.py:256
  46.7 14.3 %collective-permute-start.8 = (bf16[4,32,2176]{2,1,0:T(8,128)(2,1)S(1)}, bf16[4,32,2176]{2,1,0:T(8,128)(2,1)S(1)}, u32[]{:S(2)}, u32[]{:S(2)}) collective-permute-start(bf16[4,32,2176]{2,1,0:T(8,128)(2,1)S(1)} %add_convert_fusion), channel_id=1, source_target_pairs={{0,1},{1,0},{2,3},{3,2},{4,5},{5,4},{6,7},{7,6},{8,9},{9,8},{10,11... | collective-permute-start | bytes 1671176 | tf_op jit(solution)/shard_map/ppermute | solution.py:265
  47.4 17.7 %collective-permute-start.1 = (bf16[64,2176]{1,0:T(8,128)(2,1)S(1)}, bf16[64,2176]{1,0:T(8,128)(2,1)S(1)}, u32[]{:S(2)}, u32[]{:S(2)}) collective-permute-start(bf16[64,2176]{1,0:T(8,128)(2,1)S(1)} %get-tuple-element.14), channel_id=1, source_target_pairs={{0,32},{16,48},{32,64},{48,80},{64,96},{80,112},{96,0},{112,16},{1... | collective-permute-start | bytes 835592 | tf_op jit(solution)/shard_map/ppermute | solution.py:261
  48.8 17.4 %collective-permute-start.3 = (bf16[64,2176]{1,0:T(8,128)(2,1)S(1)}, bf16[64,2176]{1,0:T(8,128)(2,1)S(1)}, u32[]{:S(2)}, u32[]{:S(2)}) collective-permute-start(bf16[64,2176]{1,0:T(8,128)(2,1)S(1)} %get-tuple-element.15), channel_id=1, source_target_pairs={{0,64},{16,80},{32,96},{48,112},{64,0},{80,16},{96,32},{112,48},{1... | collective-permute-start | bytes 835592 | tf_op jit(solution)/shard_map/ppermute | solution.py:261
  51.4 14.8 %collective-permute-start.2 = (bf16[64,2176]{1,0:T(8,128)(2,1)S(1)}, bf16[64,2176]{1,0:T(8,128)(2,1)S(1)}, u32[]{:S(2)}, u32[]{:S(2)}) collective-permute-start(bf16[64,2176]{1,0:T(8,128)(2,1)S(1)} %get-tuple-element.16), channel_id=1, source_target_pairs={{0,96},{16,112},{32,0},{48,16},{64,32},{80,48},{96,64},{112,80},{1... | collective-permute-start | bytes 835592 | tf_op jit(solution)/shard_map/ppermute | solution.py:261
  61.1 5.8 %collective-permute-start.9 = (bf16[32,2176]{1,0:T(8,128)(2,1)S(1)}, bf16[32,2176]{1,0:T(8,128)(2,1)S(1)}, u32[]{:S(2)}, u32[]{:S(2)}) collective-permute-start(bf16[32,2176]{1,0:T(8,128)(2,1)S(1)} %get-tuple-element.17), channel_id=1, source_target_pairs={{0,32},{16,48},{32,64},{48,80},{64,96},{80,112},{96,0},{112,16},{1... | collective-permute-start | bytes 417800 | tf_op jit(solution)/shard_map/ppermute | solution.py:261
  62.5 8.5 %collective-permute-start.11 = (bf16[32,2176]{1,0:T(8,128)(2,1)S(1)}, bf16[32,2176]{1,0:T(8,128)(2,1)S(1)}, u32[]{:S(2)}, u32[]{:S(2)}) collective-permute-start(bf16[32,2176]{1,0:T(8,128)(2,1)S(1)} %get-tuple-element.18), channel_id=1, source_target_pairs={{0,64},{16,80},{32,96},{48,112},{64,0},{80,16},{96,32},{112,48},{1... | collective-permute-start | bytes 417800 | tf_op jit(solution)/shard_map/ppermute | solution.py:261
  65.1 5.9 %collective-permute-start.10 = (bf16[32,2176]{1,0:T(8,128)(2,1)S(1)}, bf16[32,2176]{1,0:T(8,128)(2,1)S(1)}, u32[]{:S(2)}, u32[]{:S(2)}) collective-permute-start(bf16[32,2176]{1,0:T(8,128)(2,1)S(1)} %get-tuple-element.19), channel_id=1, source_target_pairs={{0,96},{16,112},{32,0},{48,16},{64,32},{80,48},{96,64},{112,80},{1... | collective-permute-start | bytes 417800 | tf_op jit(solution)/shard_map/ppermute | solution.py:261
  66.4 15.5 %collective-permute-start.4 = (bf16[64,2176]{1,0:T(8,128)(2,1)S(1)}, bf16[64,2176]{1,0:T(8,128)(2,1)S(1)}, u32[]{:S(2)}, u32[]{:S(2)}) collective-permute-start(bf16[64,2176]{1,0:T(8,128)(2,1)S(1)} %fusion.2), channel_id=1, source_target_pairs={{0,1},{1,0},{2,3},{3,2},{4,5},{5,4},{6,7},{7,6},{8,9},{9,8},{10,11... | collective-permute-start | bytes 835592 | tf_op jit(solution)/shard_map/ppermute | solution.py:265
  71.1 5.5 %collective-permute-start.14 = (bf16[32,2176]{1,0:T(8,128)(2,1)S(1)}, bf16[32,2176]{1,0:T(8,128)(2,1)S(1)}, u32[]{:S(2)}, u32[]{:S(2)}) collective-permute-start(bf16[32,2176]{1,0:T(8,128)(2,1)S(1)} %fusion.8.refs_0_), channel_id=1, source_target_pairs={{0,64},{16,80},{32,96},{48,112},{64,0},{80,16},{96,32},{112,48},{1... | collective-permute-start | bytes 417800 | tf_op jit(solution)/shard_map/ppermute | solution.py:261
  73.2 6.1 %collective-permute-start.13 = (bf16[32,2176]{1,0:T(8,128)(2,1)S(1)}, bf16[32,2176]{1,0:T(8,128)(2,1)S(1)}, u32[]{:S(2)}, u32[]{:S(2)}) collective-permute-start(bf16[32,2176]{1,0:T(8,128)(2,1)S(1)} %fusion.8.refs_0_), channel_id=1, source_target_pairs={{0,96},{16,112},{32,0},{48,16},{64,32},{80,48},{96,64},{112,80},{1... | collective-permute-start | bytes 417800 | tf_op jit(solution)/shard_map/ppermute | solution.py:261
  74.8 6.0 %collective-permute-start.12 = (bf16[32,2176]{1,0:T(8,128)(2,1)S(1)}, bf16[32,2176]{1,0:T(8,128)(2,1)S(1)}, u32[]{:S(2)}, u32[]{:S(2)}) collective-permute-start(bf16[32,2176]{1,0:T(8,128)(2,1)S(1)} %fusion.8.refs_0_), channel_id=1, source_target_pairs={{0,32},{16,48},{32,64},{48,80},{64,96},{80,112},{96,0},{112,16},{1... | collective-permute-start | bytes 417800 | tf_op jit(solution)/shard_map/ppermute | solution.py:261
  81.4 12.6 %collective-permute-start.22 = (bf16[128,2176]{1,0:T(8,128)(2,1)S(1)}, bf16[128,2176]{1,0:T(8,128)(2,1)S(1)}, u32[]{:S(2)}, u32[]{:S(2)}) collective-permute-start(bf16[128,2176]{1,0:T(8,128)(2,1)S(1)} %shard_map.53.refs_2_), channel_id=1, source_target_pairs={{0,1},{1,0},{2,3},{3,2},{4,5},{5,4},{6,7},{7,6},{8,9},{9,8},{10,11... | collective-permute-start | bytes 1671176 | tf_op jit(solution)/shard_map/ppermute | solution.py:265
  81.9 7.0 %collective-permute-start.20 = (bf16[64,2176]{1,0:T(8,128)(2,1)S(1)}, bf16[64,2176]{1,0:T(8,128)(2,1)S(1)}, u32[]{:S(2)}, u32[]{:S(2)}) collective-permute-start(bf16[64,2176]{1,0:T(8,128)(2,1)S(1)} %add_convert_fusion.1.refs_0_), channel_id=1, source_target_pairs={{0,64},{16,80},{32,96},{48,112},{64,0},{80,16},{96,32},{112,48},{1... | collective-permute-start | bytes 835592 | tf_op jit(solution)/shard_map/ppermute | solution.py:261
  83.4 13.2 %collective-permute-start.18 = (bf16[64,2176]{1,0:T(8,128)(2,1)S(1)}, bf16[64,2176]{1,0:T(8,128)(2,1)S(1)}, u32[]{:S(2)}, u32[]{:S(2)}) collective-permute-start(bf16[64,2176]{1,0:T(8,128)(2,1)S(1)} %add_convert_fusion.1.refs_0_), channel_id=1, source_target_pairs={{0,96},{16,112},{32,0},{48,16},{64,32},{80,48},{96,64},{112,80},{1... | collective-permute-start | bytes 835592 | tf_op jit(solution)/shard_map/ppermute | solution.py:261
  85.8 13.2 %collective-permute-start.15 = (bf16[128,2176]{1,0:T(8,128)(2,1)S(1)}, bf16[128,2176]{1,0:T(8,128)(2,1)S(1)}, u32[]{:S(2)}, u32[]{:S(2)}) collective-permute-start(bf16[128,2176]{1,0:T(8,128)(2,1)S(1)} %shard_map.53.refs_2_), channel_id=1, source_target_pairs={{0,16},{16,0},{32,48},{48,32},{64,80},{80,64},{96,112},{112,96},{1... | collective-permute-start | bytes 1671176 | tf_op jit(solution)/shard_map/ppermute | solution.py:256
  87.5 10.8 %collective-permute-start.16 = (bf16[64,2176]{1,0:T(8,128)(2,1)S(1)}, bf16[64,2176]{1,0:T(8,128)(2,1)S(1)}, u32[]{:S(2)}, u32[]{:S(2)}) collective-permute-start(bf16[64,2176]{1,0:T(8,128)(2,1)S(1)} %add_convert_fusion.1.refs_0_), channel_id=1, source_target_pairs={{0,32},{16,48},{32,64},{48,80},{64,96},{80,112},{96,0},{112,16},{1... | collective-permute-start | bytes 835592 | tf_op jit(solution)/shard_map/ppermute | solution.py:261
  88.9 10.0 %collective-permute-start.5 = (bf16[64,2176]{1,0:T(8,128)(2,1)S(1)}, bf16[64,2176]{1,0:T(8,128)(2,1)S(1)}, u32[]{:S(2)}, u32[]{:S(2)}) collective-permute-start(bf16[64,2176]{1,0:T(8,128)(2,1)S(1)} %add_convert_fusion.1.refs_0_), channel_id=1, source_target_pairs={{0,16},{16,0},{32,48},{48,32},{64,80},{80,64},{96,112},{112,96},{1... | collective-permute-start | bytes 835592 | tf_op jit(solution)/shard_map/ppermute | solution.py:256
  94.0 6.6 %collective-permute-start.23 = (bf16[128,2176]{1,0:T(8,128)(2,1)S(1)}, bf16[128,2176]{1,0:T(8,128)(2,1)}, u32[]{:S(2)}, u32[]{:S(2)}) collective-permute-start(bf16[128,2176]{1,0:T(8,128)(2,1)S(1)} %collective-permute-done.22.refs_10_), channel_id=1, source_target_pairs={{0,16},{16,0},{32,48},{48,32},{64,80},{80,64},{96,112},{112,96},{1... | collective-permute-start | bytes 1671176 | tf_op jit(solution)/shard_map/ppermute | solution.py:256
  96.5 2.6 %collective-permute-start.21 = (bf16[64,2176]{1,0:T(8,128)(2,1)S(1)}, bf16[64,2176]{1,0:T(8,128)(2,1)S(1)}, u32[]{:S(2)}, u32[]{:S(2)}) collective-permute-start(bf16[64,2176]{1,0:T(8,128)(2,1)S(1)} %collective-permute-done.20.refs_8_), channel_id=1, source_target_pairs={{0,16},{16,0},{32,48},{48,32},{64,80},{80,64},{96,112},{112,96},{1... | collective-permute-start | bytes 835592 | tf_op jit(solution)/shard_map/ppermute | solution.py:256
  98.2 1.9 %collective-permute-start.19 = (bf16[64,2176]{1,0:T(8,128)(2,1)S(1)}, bf16[64,2176]{1,0:T(8,128)(2,1)}, u32[]{:S(2)}, u32[]{:S(2)}) collective-permute-start(bf16[64,2176]{1,0:T(8,128)(2,1)S(1)} %collective-permute-done.18.refs_6_), channel_id=1, source_target_pairs={{0,16},{16,0},{32,48},{48,32},{64,80},{80,64},{96,112},{112,96},{1... | collective-permute-start | bytes 835592 | tf_op jit(solution)/shard_map/ppermute | solution.py:256
  98.9 1.7 %collective-permute-start.17 = (bf16[64,2176]{1,0:T(8,128)(2,1)S(1)}, bf16[64,2176]{1,0:T(8,128)(2,1)}, u32[]{:S(2)}, u32[]{:S(2)}) collective-permute-start(bf16[64,2176]{1,0:T(8,128)(2,1)S(1)} %collective-permute-done.16.refs_4_), channel_id=1, source_target_pairs={{0,16},{16,0},{32,48},{48,32},{64,80},{80,64},{96,112},{112,96},{1... | collective-permute-start | bytes 835592 | tf_op jit(solution)/shard_map/ppermute | solution.py:256
  115.9 33.1 %all-to-all-start.1 = ((bf16[16,448,128]{2,1,0:T(8,128)(2,1)}), bf16[16,448,128]{2,1,0:T(8,128)(2,1)S(1)}, u32[]{:S(2)}, u32[]{:S(2)}) async-start(bf16[16,448,128]{2,1,0:T(8,128)(2,1)} %shard_map.54), calls=%async_computation.1 | async-start | bytes 3670016 | tf_op jit(solution)/shard_map/all_to_all | solution.py:314

commit v7 on v6

--- a/solution.py
+++ b/solution.py
@@ -115,17 +115,17 @@
 def merge_kernel(where_ref, *refs):
     piece_refs, out_ref = refs[:-1], refs[-1]
     for n, piece_ref in enumerate(piece_refs):
-        at = pl.ds(pl.multiple_of(where_ref[n], QUARTER), QUARTER)
-        out_ref[at, :] = piece_ref[...]
+        rows = piece_ref.shape[0]
+        out_ref[pl.ds(pl.multiple_of(where_ref[n], QUARTER), rows), :] = piece_ref[...]
 
 
 def merge(pieces, offsets):
-    count = len(pieces)
+    count, rows = len(pieces), sum(piece.shape[0] for piece in pieces)
     return pl.pallas_call(
         merge_kernel,
         in_specs=[SCALARS] + [WHOLE] * count,
         out_specs=WHOLE,
-        out_shape=jax.ShapeDtypeStruct((count * QUARTER, FOLD), bf16),
+        out_shape=jax.ShapeDtypeStruct((rows, FOLD), bf16),
         compiler_params=PARAMS,
     )(jnp.stack([jnp.int32(offset) for offset in offsets]), *pieces)
 
@@ -306,8 +306,7 @@
     order = [place_y, behind, ahead, far]
     take(first, HALVES, order[:1], 0)
     take(second, QUARTER, order, HALVES + side * QUARTER)
-    for values, chunk in zip(round_ring([first] * 3), order[1:]):
-        take(values, HALVES, [chunk], 0)
+    take(merge(round_ring([first] * 3), range(0, 3 * HALVES, HALVES)), HALVES, order[1:], 0)
     take(second_other, QUARTER, order, HALVES + (1 - side) * QUARTER)
 
     update = newton_step(columns, pieces, tuple(layout), jnp.stack(where).astype(jnp.int32))

time: 151 us -> 154 us (1.020)
  waiting for transfers between devices: 73 us -> 84.4 us
  starting transfers between devices: 44.8 us -> 35.6 us
    ppermute x12, waiting for transfers between devices: 12 us -> 21.8 us  [shift(): lax.ppermute(values, 'fsdp', [(i, (i + CORES * distance) % size) for i in...]
    ppermute x9 -> x7, starting transfers between devices: 14.1 us -> 4.96 us  [swap_cores(): lax.ppermute(values, 'fsdp', [(i, i ^ 1) for i in range(CORES * RING)])]
    ppermute x9 -> x7, waiting for transfers between devices: 1.97 us -> 3.63 us  [swap_cores(): lax.ppermute(values, 'fsdp', [(i, i ^ 1) for i in range(CORES * RING)])]
  transfers between devices with their start and end apart: 26 -> 24, of which waited for: 14 -> 14; matrix products, arithmetic and copies ran while one was open for 4% -> 4% of each run, Pallas kernels for 2% -> 2%
where the time goes in v7:
time: 154 us
  waiting for transfers between devices  84.4 us (55%)
  starting transfers between devices  35.6 us (23%)
  Pallas kernels  25.9 us (17%)
  other arithmetic  5.81 us (4%)
    all_to_all x1, waiting for transfers between devices, shards(): columns = lax.all_to_all(blended.reshape(MEMBERS, HALF, LANES), 'mat', 0, 0)  26 us
    all_to_all x1, waiting for transfers between devices, shards(): returned = lax.all_to_all(update, 'mat', 0, 0)  24.5 us
    ppermute x12, waiting for transfers between devices, shift(): lax.ppermute(values, 'fsdp', [(i, (i + CORES * distance) % size) for i in...  21.8 us
    ppermute x12, starting transfers between devices, shift(): lax.ppermute(values, 'fsdp', [(i, (i + CORES * distance) % size) for i in...  17.7 us
    pallas_call x1, Pallas kernels, newton_step(): pl.pallas_call(functools.partial(step_kernel, layout), in_specs=[SCALARS,...  15.4 us
    ppermute x3, waiting for transfers between devices, swap_pair(): return lax.ppermute(values, 'mat', [(i, i ^ 1) for i in range(MEMBERS)])  8.52 us
    all_to_all x1, starting transfers between devices, shards(): columns = lax.all_to_all(blended.reshape(MEMBERS, HALF, LANES), 'mat', 0, 0)  8.44 us
    ppermute x7, starting transfers between devices, swap_cores(): lax.ppermute(values, 'fsdp', [(i, i ^ 1) for i in range(CORES * RING)])  4.96 us
  transfers between devices with their start and end apart: 24, of which 14 were waited for; matrix products, arithmetic and copies ran while one was open for 4% of the time, Pallas kernels for 2%

profile of v7, /device:TPU:1, one launch (start us, length us, event | category | flops | bytes accessed | tf_op | source)
XLA Modules:
  0.0 153.5 jit_solution(4207212242202399415)
XLA Ops:
  0.6 3.9 %shard_map.50 = bf16[8,896,128]{2,1,0:T(8,128)(2,1)} custom-call(f32[8,128,896]{2,1,0:T(8,128)} %momentum_ref.1, bf16[8,128,896]{2,1,0:T(8,128)(2,1)} %gradient_ref.1), custom_call_target="tpu_custom_call" | custom-call | tf_op jit(solution)/shard_map/pallas_call | solution.py:58
  4.6 0.0 copy-start.1
  4.6 8.4 %all-to-all-start = ((bf16[16,448,128]{2,1,0:T(8,128)(2,1)}), bf16[16,448,128]{2,1,0:T(8,128)(2,1)S(1)}, u32[]{:S(2)}, u32[]{:S(2)}) async-start(bf16[16,448,128]{2,1,0:T(8,128)(2,1)} %bitcast.46), calls=%async_computation | async-start | bytes 3670016 | tf_op jit(solution)/shard_map/all_to_all | solution.py:273
  13.1 0.6 gather_fusion
  13.7 0.1 add_add_fusion
  13.8 26.0 %all-to-all-done.columns_ref = bf16[16,448,128]{2,1,0:T(8,128)(2,1)S(1)} async-done(((bf16[16,448,128]{2,1,0:T(8,128)(2,1)}), bf16[16,448,128]{2,1,0:T(8,128)(2,1)S(1)}, u32[]{:S(2)}, u32[]{:S(2)}) %all-to-all-start) | async-done | bytes 1835040 | tf_op jit(solution)/shard_map/all_to_all | solution.py:273
  39.8 2.0 %shard_map.52 = (bf16[4,64,2176]{2,1,0:T(8,128)(2,1)S(1)}, bf16[4,32,2176]{2,1,0:T(8,128)(2,1)S(1)}, bf16[4,32,2176]{2,1,0:T(8,128)(2,1)S(1)}) custom-call(s32[6]{0:T(128)S(1)} %get-tuple-element.21.where_ref, bf16[16,448,128]{2,1,0:T(8,128)(2,1)S(1)} %all-to-all-done.columns_ref), custom_call_target="tpu_custom_call" | custom-call | flops 2281701376 | bytes 8000000 | tf_op jit(solution)/shard_map/pallas_call | solution.py:104
  41.8 2.2 %collective-permute-start.7 = (bf16[4,32,2176]{2,1,0:T(8,128)(2,1)S(1)}, bf16[4,32,2176]{2,1,0:T(8,128)(2,1)S(1)}, u32[]{:S(2)}, u32[]{:S(2)}) collective-permute-start(bf16[4,32,2176]{2,1,0:T(8,128)(2,1)S(1)} %get-tuple-element.13), channel_id=1, source_target_pairs={{0,16},{16,0},{32,48},{48,32},{64,80},{80,64},{96,112},{112,96},{1... | collective-permute-start | bytes 1671176 | tf_op jit(solution)/shard_map/ppermute | solution.py:256
  44.0 0.1 collective-permute-start
  44.1 0.4 collective-permute-start.6
  44.5 2.0 %shard_map.51 = (bf16[4,64,2176]{2,1,0:T(8,128)(2,1)S(1)}, bf16[4,32,2176]{2,1,0:T(8,128)(2,1)S(1)}, bf16[4,32,2176]{2,1,0:T(8,128)(2,1)S(1)}) custom-call(s32[6]{0:T(128)S(1)} %get-tuple-element.20.where_ref, bf16[16,448,128]{2,1,0:T(8,128)(2,1)S(1)} %all-to-all-done.columns_ref), custom_call_target="tpu_custom_call" | custom-call | flops 2281701376 | bytes 8000000 | tf_op jit(solution)/shard_map/pallas_call | solution.py:104
  46.6 0.0 collective-permute-done.7
  46.6 0.1 add_convert_fusion
  46.7 0.1 collective-permute-start.8
  46.8 0.4 collective-permute-done
  47.2 0.2 fusion.3
  47.4 1.4 collective-permute-start.1
  48.8 2.6 %collective-permute-start.3 = (bf16[64,2176]{1,0:T(8,128)(2,1)S(1)}, bf16[64,2176]{1,0:T(8,128)(2,1)S(1)}, u32[]{:S(2)}, u32[]{:S(2)}) collective-permute-start(bf16[64,2176]{1,0:T(8,128)(2,1)S(1)} %get-tuple-element.15), channel_id=1, source_target_pairs={{0,64},{16,80},{32,96},{48,112},{64,0},{80,16},{96,32},{112,48},{1... | collective-permute-start | bytes 835592 | tf_op jit(solution)/shard_map/ppermute | solution.py:261
  51.4 1.1 collective-permute-start.2
  52.5 0.0 collective-permute-done.6
  52.5 8.5 %collective-permute-done.8 = bf16[4,32,2176]{2,1,0:T(8,128)(2,1)S(1)} collective-permute-done((bf16[4,32,2176]{2,1,0:T(8,128)(2,1)S(1)}, bf16[4,32,2176]{2,1,0:T(8,128)(2,1)S(1)}, u32[]{:S(2)}, u32[]{:S(2)}) %collective-permute-start.8) | collective-permute-done | bytes 557088 | tf_op jit(solution)/shard_map/ppermute | solution.py:265
  61.0 0.2 fusion.9
  61.1 1.4 collective-permute-start.9
  62.5 2.6 %collective-permute-start.11 = (bf16[32,2176]{1,0:T(8,128)(2,1)S(1)}, bf16[32,2176]{1,0:T(8,128)(2,1)S(1)}, u32[]{:S(2)}, u32[]{:S(2)}) collective-permute-start(bf16[32,2176]{1,0:T(8,128)(2,1)S(1)} %get-tuple-element.18), channel_id=1, source_target_pairs={{0,64},{16,80},{32,96},{48,112},{64,0},{80,16},{96,32},{112,48},{1... | collective-permute-start | bytes 417800 | tf_op jit(solution)/shard_map/ppermute | solution.py:261
  65.1 0.0 collective-permute-done.1
  65.1 1.1 collective-permute-start.10
  66.2 0.0 collective-permute-done.2
  66.2 0.2 fusion.2
  66.4 0.3 collective-permute-start.4
  66.7 0.2 collective-permute-done.9
  66.9 4.1 %collective-permute-done.11 = bf16[32,2176]{1,0:T(8,128)(2,1)S(1)} collective-permute-done((bf16[32,2176]{1,0:T(8,128)(2,1)S(1)}, bf16[32,2176]{1,0:T(8,128)(2,1)S(1)}, u32[]{:S(2)}, u32[]{:S(2)}) %collective-permute-start.11) | collective-permute-done | bytes 139296 | tf_op jit(solution)/shard_map/ppermute | solution.py:261
  71.0 0.1 fusion.8.refs_0_
  71.1 2.1 %collective-permute-start.14 = (bf16[32,2176]{1,0:T(8,128)(2,1)S(1)}, bf16[32,2176]{1,0:T(8,128)(2,1)S(1)}, u32[]{:S(2)}, u32[]{:S(2)}) collective-permute-start(bf16[32,2176]{1,0:T(8,128)(2,1)S(1)} %fusion.8.refs_0_), channel_id=1, source_target_pairs={{0,64},{16,80},{32,96},{48,112},{64,0},{80,16},{96,32},{112,48},{1... | collective-permute-start | bytes 417800 | tf_op jit(solution)/shard_map/ppermute | solution.py:261
  73.2 1.6 %collective-permute-start.13 = (bf16[32,2176]{1,0:T(8,128)(2,1)S(1)}, bf16[32,2176]{1,0:T(8,128)(2,1)S(1)}, u32[]{:S(2)}, u32[]{:S(2)}) collective-permute-start(bf16[32,2176]{1,0:T(8,128)(2,1)S(1)} %fusion.8.refs_0_), channel_id=1, source_target_pairs={{0,96},{16,112},{32,0},{48,16},{64,32},{80,48},{96,64},{112,80},{1... | collective-permute-start | bytes 417800 | tf_op jit(solution)/shard_map/ppermute | solution.py:261
  74.8 0.0 collective-permute-start.12
  74.8 1.8 %collective-permute-done.14.refs_3_ = bf16[32,2176]{1,0:T(8,128)(2,1)S(1)} collective-permute-done((bf16[32,2176]{1,0:T(8,128)(2,1)S(1)}, bf16[32,2176]{1,0:T(8,128)(2,1)S(1)}, u32[]{:S(2)}, u32[]{:S(2)}) %collective-permute-start.14) | collective-permute-done | bytes 139296 | tf_op jit(solution)/shard_map/ppermute | solution.py:261
  76.6 2.7 %collective-permute-done.13.refs_2_ = bf16[32,2176]{1,0:T(8,128)(2,1)S(1)} collective-permute-done((bf16[32,2176]{1,0:T(8,128)(2,1)S(1)}, bf16[32,2176]{1,0:T(8,128)(2,1)S(1)}, u32[]{:S(2)}, u32[]{:S(2)}) %collective-permute-start.13) | collective-permute-done | bytes 139296 | tf_op jit(solution)/shard_map/ppermute | solution.py:261
  79.3 1.5 collective-permute-done.12.refs_1_
  80.8 0.6 shard_map.53.refs_2_
  81.4 0.4 collective-permute-start.20
  81.9 0.0 collective-permute-done.4
  81.9 0.1 add_convert_fusion.1.refs_0_
  81.9 1.4 collective-permute-start.18
  83.4 2.4 %collective-permute-start.17 = (bf16[64,2176]{1,0:T(8,128)(2,1)S(1)}, bf16[64,2176]{1,0:T(8,128)(2,1)S(1)}, u32[]{:S(2)}, u32[]{:S(2)}) collective-permute-start(bf16[64,2176]{1,0:T(8,128)(2,1)S(1)} %add_convert_fusion.1.refs_0_), channel_id=1, source_target_pairs={{0,96},{16,112},{32,0},{48,16},{64,32},{80,48},{96,64},{112,80},{1... | collective-permute-start | bytes 835592 | tf_op jit(solution)/shard_map/ppermute | solution.py:261
  85.8 0.0 collective-permute-start.16
  85.8 3.1 %collective-permute-done.18.refs_2_ = bf16[64,2176]{1,0:T(8,128)(2,1)S(1)} collective-permute-done((bf16[64,2176]{1,0:T(8,128)(2,1)S(1)}, bf16[64,2176]{1,0:T(8,128)(2,1)S(1)}, u32[]{:S(2)}, u32[]{:S(2)}) %collective-permute-start.18) | collective-permute-done | bytes 278560 | tf_op jit(solution)/shard_map/ppermute | solution.py:261
  88.9 7.5 %collective-permute-done.17.refs_1_ = bf16[64,2176]{1,0:T(8,128)(2,1)S(1)} collective-permute-done((bf16[64,2176]{1,0:T(8,128)(2,1)S(1)}, bf16[64,2176]{1,0:T(8,128)(2,1)S(1)}, u32[]{:S(2)}, u32[]{:S(2)}) %collective-permute-start.17) | collective-permute-done | bytes 278560 | tf_op jit(solution)/shard_map/ppermute | solution.py:261
  96.4 0.9 collective-permute-done.16.refs_0_
  97.3 0.6 shard_map.54.refs_4_
  97.9 1.6 %collective-permute-start.19 = (bf16[192,2176]{1,0:T(8,128)(2,1)S(1)}, bf16[192,2176]{1,0:T(8,128)(2,1)}, u32[]{:S(2)}, u32[]{:S(2)}) collective-permute-start(bf16[192,2176]{1,0:T(8,128)(2,1)S(1)} %shard_map.54.refs_4_), channel_id=1, source_target_pairs={{0,16},{16,0},{32,48},{48,32},{64,80},{80,64},{96,112},{112,96},{1... | collective-permute-start | bytes 2506760 | tf_op jit(solution)/shard_map/ppermute | solution.py:256
  99.5 0.1 collective-permute-start.15
  99.6 0.0 collective-permute-done.20.refs_6_
  99.6 0.4 collective-permute-start.21
  100.0 0.1 collective-permute-start.5
  100.1 0.1 stack.38.where_ref
  100.2 2.4 %collective-permute-done.5.refs_1_ = bf16[64,2176]{1,0:T(8,128)(2,1)} collective-permute-done((bf16[64,2176]{1,0:T(8,128)(2,1)S(1)}, bf16[64,2176]{1,0:T(8,128)(2,1)}, u32[]{:S(2)}, u32[]{:S(2)}) %collective-permute-start.5) | collective-permute-done | bytes 278560 | tf_op jit(solution)/shard_map/ppermute | solution.py:256
  102.7 0.0 collective-permute-done.15.refs_3_
  102.7 0.8 collective-permute-done.21.refs_7_
  103.5 0.0 collective-permute-done.19.refs_5_
  103.5 15.4 %shard_map.55 = bf16[16,448,128]{2,1,0:T(8,128)(2,1)} custom-call(s32[48]{0:T(128)S(1)} %stack.38.where_ref, bf16[16,448,128]{2,1,0:T(8,128)(2,1)} %copy-done, bf16[64,2176]{1,0:T(8,128)(2,1)S(1)} %add_convert_fusion.1.refs_0_, bf16[64,2176]{1,0:T(8,128)(2,1)} %collective-permute-done.5.refs_1_, bf16[128,2176]{1,0:T(8,128)(2,1)S(1)} %shard_map.53.refs_2_, ...), custom_call_target="tpu_custom_call" | custom-call | flops 7516192768 | bytes 8000000 | tf_op jit(solution)/shard_map/pallas_call | solution.py:203
  118.9 3.7 %all-to-all-start.1 = ((bf16[16,448,128]{2,1,0:T(8,128)(2,1)}), bf16[16,448,128]{2,1,0:T(8,128)(2,1)S(1)}, u32[]{:S(2)}, u32[]{:S(2)}) async-start(bf16[16,448,128]{2,1,0:T(8,128)(2,1)} %shard_map.55), calls=%async_computation.1 | async-start | bytes 3670016 | tf_op jit(solution)/shard_map/all_to_all | solution.py:313
  122.6 4.9 %convert_add_fusion = f32[8,128,896]{2,1,0:T(8,128)} fusion(bf16[8,128,896]{2,1,0:T(8,128)(2,1)} %gradient_ref.1, f32[8,128,896]{2,1,0:T(8,128)} %momentum_ref.1), kind=kLoop, calls=%fused_computation.1 | loop fusion | flops 2752512 | bytes 9175040 | tf_op jit(solution)/shard_map/add | solution.py:274
  127.4 24.5 %all-to-all-done.1 = bf16[16,448,128]{2,1,0:T(8,128)(2,1)S(1)} async-done(((bf16[16,448,128]{2,1,0:T(8,128)(2,1)}), bf16[16,448,128]{2,1,0:T(8,128)(2,1)S(1)}, u32[]{:S(2)}, u32[]{:S(2)}) %all-to-all-start.1) | async-done | bytes 1835040 | tf_op jit(solution)/shard_map/all_to_all | solution.py:313
  152.0 1.4 shard_map.56
  (9 shorter events, 0.0 us)
Async XLA Ops:
  4.6 8.5 %copy-start.1 = (s32[4]{0:T(128)S(1)}, s32[4]{0:T(128)}, u32[]{:S(2)}) copy-start(s32[4]{0:T(128)} %constant.81.clone) | copy-start | bytes 52
  4.6 35.2 %all-to-all-start = ((bf16[16,448,128]{2,1,0:T(8,128)(2,1)}), bf16[16,448,128]{2,1,0:T(8,128)(2,1)S(1)}, u32[]{:S(2)}, u32[]{:S(2)}) async-start(bf16[16,448,128]{2,1,0:T(8,128)(2,1)} %bitcast.46), calls=%async_computation | async-start | bytes 3670016 | tf_op jit(solution)/shard_map/all_to_all | solution.py:273
  39.8 4.7 %copy-start = (bf16[16,448,128]{2,1,0:T(8,128)(2,1)}, bf16[16,448,128]{2,1,0:T(8,128)(2,1)S(1)}, u32[]{:S(2)}) copy-start(bf16[16,448,128]{2,1,0:T(8,128)(2,1)S(1)} %all-to-all-done.columns_ref) | copy-start | bytes 5505028
  41.8 4.8 %collective-permute-start.7 = (bf16[4,32,2176]{2,1,0:T(8,128)(2,1)S(1)}, bf16[4,32,2176]{2,1,0:T(8,128)(2,1)S(1)}, u32[]{:S(2)}, u32[]{:S(2)}) collective-permute-start(bf16[4,32,2176]{2,1,0:T(8,128)(2,1)S(1)} %get-tuple-element.13), channel_id=1, source_target_pairs={{0,16},{16,0},{32,48},{48,32},{64,80},{80,64},{96,112},{112,96},{1... | collective-permute-start | bytes 1671176 | tf_op jit(solution)/shard_map/ppermute | solution.py:256
  44.0 3.2 %collective-permute-start = (bf16[4,64,2176]{2,1,0:T(8,128)(2,1)S(1)}, bf16[4,64,2176]{2,1,0:T(8,128)(2,1)S(1)}, u32[]{:S(2)}, u32[]{:S(2)}) collective-permute-start(bf16[4,64,2176]{2,1,0:T(8,128)(2,1)S(1)} %get-tuple-element.9), channel_id=1, source_target_pairs={{0,16},{16,0},{32,48},{48,32},{64,80},{80,64},{96,112},{112,96},{1... | collective-permute-start | bytes 3342344 | tf_op jit(solution)/shard_map/ppermute | solution.py:256
  44.1 8.3 %collective-permute-start.6 = (bf16[4,32,2176]{2,1,0:T(8,128)(2,1)S(1)}, bf16[4,32,2176]{2,1,0:T(8,128)(2,1)S(1)}, u32[]{:S(2)}, u32[]{:S(2)}) collective-permute-start(bf16[4,32,2176]{2,1,0:T(8,128)(2,1)S(1)} %get-tuple-element.11), channel_id=1, source_target_pairs={{0,16},{16,0},{32,48},{48,32},{64,80},{80,64},{96,112},{112,96},{1... | collective-permute-start | bytes 1671176 | tf_op jit(solution)/shard_map/ppermute | solution.py:256
  46.7 14.3 %collective-permute-start.8 = (bf16[4,32,2176]{2,1,0:T(8,128)(2,1)S(1)}, bf16[4,32,2176]{2,1,0:T(8,128)(2,1)S(1)}, u32[]{:S(2)}, u32[]{:S(2)}) collective-permute-start(bf16[4,32,2176]{2,1,0:T(8,128)(2,1)S(1)} %add_convert_fusion), channel_id=1, source_target_pairs={{0,1},{1,0},{2,3},{3,2},{4,5},{5,4},{6,7},{7,6},{8,9},{9,8},{10,11... | collective-permute-start | bytes 1671176 | tf_op jit(solution)/shard_map/ppermute | solution.py:265
  47.4 17.7 %collective-permute-start.1 = (bf16[64,2176]{1,0:T(8,128)(2,1)S(1)}, bf16[64,2176]{1,0:T(8,128)(2,1)S(1)}, u32[]{:S(2)}, u32[]{:S(2)}) collective-permute-start(bf16[64,2176]{1,0:T(8,128)(2,1)S(1)} %get-tuple-element.14), channel_id=1, source_target_pairs={{0,32},{16,48},{32,64},{48,80},{64,96},{80,112},{96,0},{112,16},{1... | collective-permute-start | bytes 835592 | tf_op jit(solution)/shard_map/ppermute | solution.py:261
  48.8 17.4 %collective-permute-start.3 = (bf16[64,2176]{1,0:T(8,128)(2,1)S(1)}, bf16[64,2176]{1,0:T(8,128)(2,1)S(1)}, u32[]{:S(2)}, u32[]{:S(2)}) collective-permute-start(bf16[64,2176]{1,0:T(8,128)(2,1)S(1)} %get-tuple-element.15), channel_id=1, source_target_pairs={{0,64},{16,80},{32,96},{48,112},{64,0},{80,16},{96,32},{112,48},{1... | collective-permute-start | bytes 835592 | tf_op jit(solution)/shard_map/ppermute | solution.py:261
  51.4 14.8 %collective-permute-start.2 = (bf16[64,2176]{1,0:T(8,128)(2,1)S(1)}, bf16[64,2176]{1,0:T(8,128)(2,1)S(1)}, u32[]{:S(2)}, u32[]{:S(2)}) collective-permute-start(bf16[64,2176]{1,0:T(8,128)(2,1)S(1)} %get-tuple-element.16), channel_id=1, source_target_pairs={{0,96},{16,112},{32,0},{48,16},{64,32},{80,48},{96,64},{112,80},{1... | collective-permute-start | bytes 835592 | tf_op jit(solution)/shard_map/ppermute | solution.py:261
  61.1 5.8 %collective-permute-start.9 = (bf16[32,2176]{1,0:T(8,128)(2,1)S(1)}, bf16[32,2176]{1,0:T(8,128)(2,1)S(1)}, u32[]{:S(2)}, u32[]{:S(2)}) collective-permute-start(bf16[32,2176]{1,0:T(8,128)(2,1)S(1)} %get-tuple-element.17), channel_id=1, source_target_pairs={{0,32},{16,48},{32,64},{48,80},{64,96},{80,112},{96,0},{112,16},{1... | collective-permute-start | bytes 417800 | tf_op jit(solution)/shard_map/ppermute | solution.py:261
  62.5 8.5 %collective-permute-start.11 = (bf16[32,2176]{1,0:T(8,128)(2,1)S(1)}, bf16[32,2176]{1,0:T(8,128)(2,1)S(1)}, u32[]{:S(2)}, u32[]{:S(2)}) collective-permute-start(bf16[32,2176]{1,0:T(8,128)(2,1)S(1)} %get-tuple-element.18), channel_id=1, source_target_pairs={{0,64},{16,80},{32,96},{48,112},{64,0},{80,16},{96,32},{112,48},{1... | collective-permute-start | bytes 417800 | tf_op jit(solution)/shard_map/ppermute | solution.py:261
  65.1 5.9 %collective-permute-start.10 = (bf16[32,2176]{1,0:T(8,128)(2,1)S(1)}, bf16[32,2176]{1,0:T(8,128)(2,1)S(1)}, u32[]{:S(2)}, u32[]{:S(2)}) collective-permute-start(bf16[32,2176]{1,0:T(8,128)(2,1)S(1)} %get-tuple-element.19), channel_id=1, source_target_pairs={{0,96},{16,112},{32,0},{48,16},{64,32},{80,48},{96,64},{112,80},{1... | collective-permute-start | bytes 417800 | tf_op jit(solution)/shard_map/ppermute | solution.py:261
  66.4 15.5 %collective-permute-start.4 = (bf16[64,2176]{1,0:T(8,128)(2,1)S(1)}, bf16[64,2176]{1,0:T(8,128)(2,1)S(1)}, u32[]{:S(2)}, u32[]{:S(2)}) collective-permute-start(bf16[64,2176]{1,0:T(8,128)(2,1)S(1)} %fusion.2), channel_id=1, source_target_pairs={{0,1},{1,0},{2,3},{3,2},{4,5},{5,4},{6,7},{7,6},{8,9},{9,8},{10,11... | collective-permute-start | bytes 835592 | tf_op jit(solution)/shard_map/ppermute | solution.py:265
  71.1 5.5 %collective-permute-start.14 = (bf16[32,2176]{1,0:T(8,128)(2,1)S(1)}, bf16[32,2176]{1,0:T(8,128)(2,1)S(1)}, u32[]{:S(2)}, u32[]{:S(2)}) collective-permute-start(bf16[32,2176]{1,0:T(8,128)(2,1)S(1)} %fusion.8.refs_0_), channel_id=1, source_target_pairs={{0,64},{16,80},{32,96},{48,112},{64,0},{80,16},{96,32},{112,48},{1... | collective-permute-start | bytes 417800 | tf_op jit(solution)/shard_map/ppermute | solution.py:261
  73.2 6.1 %collective-permute-start.13 = (bf16[32,2176]{1,0:T(8,128)(2,1)S(1)}, bf16[32,2176]{1,0:T(8,128)(2,1)S(1)}, u32[]{:S(2)}, u32[]{:S(2)}) collective-permute-start(bf16[32,2176]{1,0:T(8,128)(2,1)S(1)} %fusion.8.refs_0_), channel_id=1, source_target_pairs={{0,96},{16,112},{32,0},{48,16},{64,32},{80,48},{96,64},{112,80},{1... | collective-permute-start | bytes 417800 | tf_op jit(solution)/shard_map/ppermute | solution.py:261
  74.8 6.0 %collective-permute-start.12 = (bf16[32,2176]{1,0:T(8,128)(2,1)S(1)}, bf16[32,2176]{1,0:T(8,128)(2,1)S(1)}, u32[]{:S(2)}, u32[]{:S(2)}) collective-permute-start(bf16[32,2176]{1,0:T(8,128)(2,1)S(1)} %fusion.8.refs_0_), channel_id=1, source_target_pairs={{0,32},{16,48},{32,64},{48,80},{64,96},{80,112},{96,0},{112,16},{1... | collective-permute-start | bytes 417800 | tf_op jit(solution)/shard_map/ppermute | solution.py:261
  81.4 18.2 %collective-permute-start.20 = (bf16[128,2176]{1,0:T(8,128)(2,1)S(1)}, bf16[128,2176]{1,0:T(8,128)(2,1)S(1)}, u32[]{:S(2)}, u32[]{:S(2)}) collective-permute-start(bf16[128,2176]{1,0:T(8,128)(2,1)S(1)} %shard_map.53.refs_2_), channel_id=1, source_target_pairs={{0,1},{1,0},{2,3},{3,2},{4,5},{5,4},{6,7},{7,6},{8,9},{9,8},{10,11... | collective-permute-start | bytes 1671176 | tf_op jit(solution)/shard_map/ppermute | solution.py:265
  81.9 7.0 %collective-permute-start.18 = (bf16[64,2176]{1,0:T(8,128)(2,1)S(1)}, bf16[64,2176]{1,0:T(8,128)(2,1)S(1)}, u32[]{:S(2)}, u32[]{:S(2)}) collective-permute-start(bf16[64,2176]{1,0:T(8,128)(2,1)S(1)} %add_convert_fusion.1.refs_0_), channel_id=1, source_target_pairs={{0,64},{16,80},{32,96},{48,112},{64,0},{80,16},{96,32},{112,48},{1... | collective-permute-start | bytes 835592 | tf_op jit(solution)/shard_map/ppermute | solution.py:261
  83.4 13.0 %collective-permute-start.17 = (bf16[64,2176]{1,0:T(8,128)(2,1)S(1)}, bf16[64,2176]{1,0:T(8,128)(2,1)S(1)}, u32[]{:S(2)}, u32[]{:S(2)}) collective-permute-start(bf16[64,2176]{1,0:T(8,128)(2,1)S(1)} %add_convert_fusion.1.refs_0_), channel_id=1, source_target_pairs={{0,96},{16,112},{32,0},{48,16},{64,32},{80,48},{96,64},{112,80},{1... | collective-permute-start | bytes 835592 | tf_op jit(solution)/shard_map/ppermute | solution.py:261
  85.8 11.5 %collective-permute-start.16 = (bf16[64,2176]{1,0:T(8,128)(2,1)S(1)}, bf16[64,2176]{1,0:T(8,128)(2,1)S(1)}, u32[]{:S(2)}, u32[]{:S(2)}) collective-permute-start(bf16[64,2176]{1,0:T(8,128)(2,1)S(1)} %add_convert_fusion.1.refs_0_), channel_id=1, source_target_pairs={{0,32},{16,48},{32,64},{48,80},{64,96},{80,112},{96,0},{112,16},{1... | collective-permute-start | bytes 835592 | tf_op jit(solution)/shard_map/ppermute | solution.py:261
  97.9 5.6 %collective-permute-start.19 = (bf16[192,2176]{1,0:T(8,128)(2,1)S(1)}, bf16[192,2176]{1,0:T(8,128)(2,1)}, u32[]{:S(2)}, u32[]{:S(2)}) collective-permute-start(bf16[192,2176]{1,0:T(8,128)(2,1)S(1)} %shard_map.54.refs_4_), channel_id=1, source_target_pairs={{0,16},{16,0},{32,48},{48,32},{64,80},{80,64},{96,112},{112,96},{1... | collective-permute-start | bytes 2506760 | tf_op jit(solution)/shard_map/ppermute | solution.py:256
  99.5 3.2 %collective-permute-start.15 = (bf16[128,2176]{1,0:T(8,128)(2,1)S(1)}, bf16[128,2176]{1,0:T(8,128)(2,1)S(1)}, u32[]{:S(2)}, u32[]{:S(2)}) collective-permute-start(bf16[128,2176]{1,0:T(8,128)(2,1)S(1)} %shard_map.53.refs_2_), channel_id=1, source_target_pairs={{0,16},{16,0},{32,48},{48,32},{64,80},{80,64},{96,112},{112,96},{1... | collective-permute-start | bytes 1671176 | tf_op jit(solution)/shard_map/ppermute | solution.py:256
  99.6 3.9 %collective-permute-start.21 = (bf16[128,2176]{1,0:T(8,128)(2,1)S(1)}, bf16[128,2176]{1,0:T(8,128)(2,1)S(1)}, u32[]{:S(2)}, u32[]{:S(2)}) collective-permute-start(bf16[128,2176]{1,0:T(8,128)(2,1)S(1)} %collective-permute-done.20.refs_6_), channel_id=1, source_target_pairs={{0,16},{16,0},{32,48},{48,32},{64,80},{80,64},{96,112},{112,96},{1... | collective-permute-start | bytes 1671176 | tf_op jit(solution)/shard_map/ppermute | solution.py:256
  100.0 2.6 %collective-permute-start.5 = (bf16[64,2176]{1,0:T(8,128)(2,1)S(1)}, bf16[64,2176]{1,0:T(8,128)(2,1)}, u32[]{:S(2)}, u32[]{:S(2)}) collective-permute-start(bf16[64,2176]{1,0:T(8,128)(2,1)S(1)} %add_convert_fusion.1.refs_0_), channel_id=1, source_target_pairs={{0,16},{16,0},{32,48},{48,32},{64,80},{80,64},{96,112},{112,96},{1... | collective-permute-start | bytes 835592 | tf_op jit(solution)/shard_map/ppermute | solution.py:256
  118.9 33.1 %all-to-all-start.1 = ((bf16[16,448,128]{2,1,0:T(8,128)(2,1)}), bf16[16,448,128]{2,1,0:T(8,128)(2,1)S(1)}, u32[]{:S(2)}, u32[]{:S(2)}) async-start(bf16[16,448,128]{2,1,0:T(8,128)(2,1)} %shard_map.55), calls=%async_computation.1 | async-start | bytes 3670016 | tf_op jit(solution)/shard_map/all_to_all | solution.py:313
